TPU v7x, 256 devices: a whole 4x4x8 slice. The times are simulated.
256 devices in a mesh: sweep: 16 (over y, x), cross: 2 (over core), band: 8 (over z).
Axes of the slice: x: 4, y: 4, z: 8, core: 2. Of those that a mesh axis runs over, the one named last changes fastest.
Arguments:
- operator: float32 [8, 16, 1024, 512], P('band', 'sweep', 'cross'), may hold values from -0.375 to 0.375
- source: float32 [8, 16, 1024, 512], P('band', 'sweep', 'cross'), may hold values from -6 to 6
- sky: float32 [8, 1024, 512], P('band', 'cross'), may hold values from -6 to 6
- response: float32 [8, 16, 1024, 512], P('band', 'sweep', 'cross'), may hold values from -6 to 6
- extinction: float32 [8], P('band'), may hold values from 0.2 to 1
- leaf_density: float32 [16], replicated, may hold values from 0.1 to 1.5
- leaf_class: int32 [16, 1024], P('sweep', 'cross'), may hold values from 0 to 15
- occupied: int32 [16, 1024], P('sweep', 'cross'), may hold values 0 or 1
Outputs:
- observed: float32 [8, 16, 1024, 512], P('band', 'sweep', 'cross')
- lai_grad: float32 [16, 1024], P('sweep', 'cross')
All inputs are finite; a program needn't handle non-finite values. No bound on the sum of `occupied` on one device may be relied on, other than what follows from the above.
Results may differ from a plain program's by a relative error of at most 0.00023.
Values sent between devices are 32-bit elements; how exact they have to be, the bound alone decides.
No kernel may reach another device: no remote copies, remote signals or barrier semaphores. Data moves between devices by JAX's collectives and lax.ppermute only.
A program may use at most 192 MiB of HBM per device.

v0:
```python
import math

import jax
import jax.numpy as jnp
from jax import lax
from jax.sharding import PartitionSpec as P

FC = 16
FV = 32


lateral_weight = 0.25


def padded_2(cells, sides, width):
    for axis, dim in sides:
        count = lax.axis_size(axis)
        ends = count - 1
        head = lax.slice_in_dim(cells, 0, width, axis=dim)
        tail = lax.slice_in_dim(cells, cells.shape[dim] - width, cells.shape[dim], axis=dim)
        cells = jnp.concatenate(
            [
                lax.ppermute(tail, axis, [(i, (i + 1) % count) for i in range(ends)]),
                cells,
                lax.ppermute(head, axis, [((i + 1) % count, i) for i in range(ends)]),
            ],
            axis=dim,
        )
    return cells


def from_behind(value, axis, by):
    count = lax.axis_size(axis)
    pairs = [(i, i + by) for i in range(count) if 0 <= i + by < count]
    return lax.ppermute(value, axis, pairs)


def product(left, right):
    return jnp.dot(left, right, precision=lax.Precision.HIGHEST, preferred_element_type=jnp.float32)


def product_flipped(left, right):
    return lax.dot_general(
        left,
        right,
        (((0,), (0,)), ((), ())),
        precision=lax.Precision.HIGHEST,
        preferred_element_type=jnp.float32,
    )


def smooth_rows(padded, grid):
    return grid + lateral_weight * (padded[:-2] + padded[2:] - 2.0 * grid)


def per_device(operator, source, sky, response, extinction, leaf_density, leaf_class, occupied):
    matrix = operator[0, 0]
    emitted = source[0, 0]
    sky_field = sky[0]
    weights = response[0, 0]
    width = matrix.shape[1]
    rays = emitted.shape[1]
    classes = leaf_class[0]
    blocked = occupied[0]
    coeff = extinction[0]
    table_size = leaf_density.shape[0]
    density = jnp.sum(
        jnp.where(classes[:, None] == jnp.arange(table_size)[None, :], leaf_density[None, :], 0.0),
        axis=1,
    )
    transmit = (1 - blocked).astype(jnp.float32) * jnp.exp(-coeff * density)
    local_op = transmit[:, None] * matrix
    position = lax.axis_index("sweep")
    count = lax.axis_size("sweep")
    first_tile = position == 0
    zeros_field = jnp.zeros((width, rays), jnp.float32)
    resp_grid = weights.reshape(FC, FV * rays)
    resp_padded = padded_2(resp_grid, (("cross", 0),), 1)
    cotangent = (smooth_rows(resp_padded, resp_grid) / math.sqrt(rays)).reshape(width, rays)

    def forward_step(step, carry):
        outgoing, incoming = carry
        shifted = from_behind(outgoing, "sweep", 1)
        incoming = jnp.where(first_tile, sky_field, shifted)
        outgoing = product(local_op, incoming) + emitted
        return (outgoing, incoming)

    outgoing, incoming = lax.fori_loop(0, count, forward_step, (zeros_field, zeros_field))

    def backward_step(step, carry):
        sent, adjoint = carry
        arriving = from_behind(sent, "sweep", -1)
        adjoint = cotangent + arriving
        sent = product_flipped(local_op, adjoint)
        return (sent, adjoint)

    sent, adjoint = lax.fori_loop(0, count, backward_step, (zeros_field, zeros_field))
    out_grid = outgoing.reshape(FC, FV * rays)
    out_padded = padded_2(out_grid, (("cross", 0),), 1)
    observed = smooth_rows(out_padded, out_grid).reshape(width, rays)
    pushed = product(matrix, incoming)
    along = jnp.sum(adjoint * pushed, axis=1)
    term = -coeff * transmit * along
    total = lax.psum(term, "band")
    return (observed[None, None], total[None])


def solution(mesh):
    in_specs = (
        P("band", "sweep", "cross", None),
        P("band", "sweep", "cross", None),
        P("band", "cross", None),
        P("band", "sweep", "cross", None),
        P("band"),
        P(),
        P("sweep", "cross"),
        P("sweep", "cross"),
    )
    out_specs = (P("band", "sweep", "cross", None), P("sweep", "cross"))
    return jax.shard_map(
        per_device, mesh=mesh, in_specs=in_specs, out_specs=out_specs, check_vma=False
    )
```

profile of v0, /device:TPU:24, one launch (start us, length us, event | category | flops | bytes accessed | tf_op | source)
XLA Modules:
  0.0 943.6 jit_solution(1792914252483059136)
XLA Ops:
  7.6 442.4 %while.26 = (s32[]{:T(128)}, f32[512,512]{0,1:T(8,128)S(1)}, f32[512,512]{0,1:T(8,128)}, pred[]{:T(512)}, f32[512,512]{0,1:T(8,128)S(1)}, /*index=5*/f32[512,512...) while((s32[]{:T(128)}, f32[512,512]{0,1:T(8,128)S(1)}, f32[512,512]{0,1:T(8,128)}, ...), condition=%wide.region_2.3_spmd.clone, body=%wide.region_1.2_spmd.clone.sunk | while | flops 1611399168 | bytes 22020296 | solution.py:88
  12.0 25.7 %collective-permute-done.1 = f32[512,512]{0,1:T(8,128)S(1)} collective-permute-done((f32[512,512]{0,1:T(8,128)}, f32[512,512]{0,1:T(8,128)S(1)}, u32[]{:S(2)}, u32[]{:S(2)}) %collective-permute-start.1) | collective-permute-done | bytes 1048608 | tf_op jit(solution)/shard_map/while/body/eval_jaxpr/ppermute | solution.py:35
  44.1 26.3 %collective-permute-done.1 = f32[512,512]{0,1:T(8,128)S(1)} collective-permute-done((f32[512,512]{0,1:T(8,128)}, f32[512,512]{0,1:T(8,128)S(1)}, u32[]{:S(2)}, u32[]{:S(2)}) %collective-permute-start.1) | collective-permute-done | bytes 1048608 | tf_op jit(solution)/shard_map/while/body/eval_jaxpr/ppermute | solution.py:35
  76.7 25.4 %collective-permute-done.1 = f32[512,512]{0,1:T(8,128)S(1)} collective-permute-done((f32[512,512]{0,1:T(8,128)}, f32[512,512]{0,1:T(8,128)S(1)}, u32[]{:S(2)}, u32[]{:S(2)}) %collective-permute-start.1) | collective-permute-done | bytes 1048608 | tf_op jit(solution)/shard_map/while/body/eval_jaxpr/ppermute | solution.py:35
  108.4 24.5 %collective-permute-done.1 = f32[512,512]{0,1:T(8,128)S(1)} collective-permute-done((f32[512,512]{0,1:T(8,128)}, f32[512,512]{0,1:T(8,128)S(1)}, u32[]{:S(2)}, u32[]{:S(2)}) %collective-permute-start.1) | collective-permute-done | bytes 1048608 | tf_op jit(solution)/shard_map/while/body/eval_jaxpr/ppermute | solution.py:35
  139.2 23.5 %collective-permute-done.1 = f32[512,512]{0,1:T(8,128)S(1)} collective-permute-done((f32[512,512]{0,1:T(8,128)}, f32[512,512]{0,1:T(8,128)S(1)}, u32[]{:S(2)}, u32[]{:S(2)}) %collective-permute-start.1) | collective-permute-done | bytes 1048608 | tf_op jit(solution)/shard_map/while/body/eval_jaxpr/ppermute | solution.py:35
  169.0 22.6 %collective-permute-done.1 = f32[512,512]{0,1:T(8,128)S(1)} collective-permute-done((f32[512,512]{0,1:T(8,128)}, f32[512,512]{0,1:T(8,128)S(1)}, u32[]{:S(2)}, u32[]{:S(2)}) %collective-permute-start.1) | collective-permute-done | bytes 1048608 | tf_op jit(solution)/shard_map/while/body/eval_jaxpr/ppermute | solution.py:35
  198.0 21.7 %collective-permute-done.1 = f32[512,512]{0,1:T(8,128)S(1)} collective-permute-done((f32[512,512]{0,1:T(8,128)}, f32[512,512]{0,1:T(8,128)S(1)}, u32[]{:S(2)}, u32[]{:S(2)}) %collective-permute-start.1) | collective-permute-done | bytes 1048608 | tf_op jit(solution)/shard_map/while/body/eval_jaxpr/ppermute | solution.py:35
  226.0 20.8 %collective-permute-done.1 = f32[512,512]{0,1:T(8,128)S(1)} collective-permute-done((f32[512,512]{0,1:T(8,128)}, f32[512,512]{0,1:T(8,128)S(1)}, u32[]{:S(2)}, u32[]{:S(2)}) %collective-permute-start.1) | collective-permute-done | bytes 1048608 | tf_op jit(solution)/shard_map/while/body/eval_jaxpr/ppermute | solution.py:35
  253.1 19.9 %collective-permute-done.1 = f32[512,512]{0,1:T(8,128)S(1)} collective-permute-done((f32[512,512]{0,1:T(8,128)}, f32[512,512]{0,1:T(8,128)S(1)}, u32[]{:S(2)}, u32[]{:S(2)}) %collective-permute-start.1) | collective-permute-done | bytes 1048608 | tf_op jit(solution)/shard_map/while/body/eval_jaxpr/ppermute | solution.py:35
  279.3 18.9 %collective-permute-done.1 = f32[512,512]{0,1:T(8,128)S(1)} collective-permute-done((f32[512,512]{0,1:T(8,128)}, f32[512,512]{0,1:T(8,128)S(1)}, u32[]{:S(2)}, u32[]{:S(2)}) %collective-permute-start.1) | collective-permute-done | bytes 1048608 | tf_op jit(solution)/shard_map/while/body/eval_jaxpr/ppermute | solution.py:35
  304.5 18.0 %collective-permute-done.1 = f32[512,512]{0,1:T(8,128)S(1)} collective-permute-done((f32[512,512]{0,1:T(8,128)}, f32[512,512]{0,1:T(8,128)S(1)}, u32[]{:S(2)}, u32[]{:S(2)}) %collective-permute-start.1) | collective-permute-done | bytes 1048608 | tf_op jit(solution)/shard_map/while/body/eval_jaxpr/ppermute | solution.py:35
  328.9 17.2 %collective-permute-done.1 = f32[512,512]{0,1:T(8,128)S(1)} collective-permute-done((f32[512,512]{0,1:T(8,128)}, f32[512,512]{0,1:T(8,128)S(1)}, u32[]{:S(2)}, u32[]{:S(2)}) %collective-permute-start.1) | collective-permute-done | bytes 1048608 | tf_op jit(solution)/shard_map/while/body/eval_jaxpr/ppermute | solution.py:35
  352.4 18.3 %collective-permute-done.1 = f32[512,512]{0,1:T(8,128)S(1)} collective-permute-done((f32[512,512]{0,1:T(8,128)}, f32[512,512]{0,1:T(8,128)S(1)}, u32[]{:S(2)}, u32[]{:S(2)}) %collective-permute-start.1) | collective-permute-done | bytes 1048608 | tf_op jit(solution)/shard_map/while/body/eval_jaxpr/ppermute | solution.py:35
  377.0 19.4 %collective-permute-done.1 = f32[512,512]{0,1:T(8,128)S(1)} collective-permute-done((f32[512,512]{0,1:T(8,128)}, f32[512,512]{0,1:T(8,128)S(1)}, u32[]{:S(2)}, u32[]{:S(2)}) %collective-permute-start.1) | collective-permute-done | bytes 1048608 | tf_op jit(solution)/shard_map/while/body/eval_jaxpr/ppermute | solution.py:35
  402.8 20.5 %collective-permute-done.1 = f32[512,512]{0,1:T(8,128)S(1)} collective-permute-done((f32[512,512]{0,1:T(8,128)}, f32[512,512]{0,1:T(8,128)S(1)}, u32[]{:S(2)}, u32[]{:S(2)}) %collective-permute-start.1) | collective-permute-done | bytes 1048608 | tf_op jit(solution)/shard_map/while/body/eval_jaxpr/ppermute | solution.py:35
  429.6 17.1 %collective-permute-done.1 = f32[512,512]{0,1:T(8,128)S(1)} collective-permute-done((f32[512,512]{0,1:T(8,128)}, f32[512,512]{0,1:T(8,128)S(1)}, u32[]{:S(2)}, u32[]{:S(2)}) %collective-permute-start.1) | collective-permute-done | bytes 1048608 | tf_op jit(solution)/shard_map/while/body/eval_jaxpr/ppermute | solution.py:35
  470.5 449.0 %while.25 = (s32[]{:T(128)}, f32[512,512]{0,1:T(8,128)}, f32[512,512]{0,1:T(8,128)}, f32[512,512]{0,1:T(8,128)S(1)}, f32[512,512]{1,0:T(8,128)S(1)}, /*index=5*/s32[]{:T(128)}) while((s32[]{:T(128)}, f32[512,512]{0,1:T(8,128)}, f32[512,512]{0,1:T(8,128)}, f32[512,512]{0,1:T(8,128)S(1)}, f32[512,512]{1,0:T(8,128)S(1)}, ...), condition=%wide.region_4.5_spmd, body=%wide.region_3.4_spmd.sunk | while | flops 1610874880 | bytes 14680201 | solution.py:97
  472.5 26.2 %collective-permute-done = f32[512,512]{0,1:T(8,128)} collective-permute-done((f32[512,512]{0,1:T(8,128)}, f32[512,512]{0,1:T(8,128)}, u32[]{:S(2)}, u32[]{:S(2)}) %collective-permute-start) | collective-permute-done | bytes 1048608 | tf_op jit(solution)/shard_map/while/body/eval_jaxpr/ppermute | solution.py:35
  506.8 23.6 %collective-permute-done = f32[512,512]{0,1:T(8,128)} collective-permute-done((f32[512,512]{0,1:T(8,128)}, f32[512,512]{0,1:T(8,128)}, u32[]{:S(2)}, u32[]{:S(2)}) %collective-permute-start) | collective-permute-done | bytes 1048608 | tf_op jit(solution)/shard_map/while/body/eval_jaxpr/ppermute | solution.py:35
  540.7 22.2 %collective-permute-done = f32[512,512]{0,1:T(8,128)} collective-permute-done((f32[512,512]{0,1:T(8,128)}, f32[512,512]{0,1:T(8,128)}, u32[]{:S(2)}, u32[]{:S(2)}) %collective-permute-start) | collective-permute-done | bytes 1048608 | tf_op jit(solution)/shard_map/while/body/eval_jaxpr/ppermute | solution.py:35
  567.2 6.5 collective-permute-start
  573.7 21.3 %collective-permute-done = f32[512,512]{0,1:T(8,128)} collective-permute-done((f32[512,512]{0,1:T(8,128)}, f32[512,512]{0,1:T(8,128)}, u32[]{:S(2)}, u32[]{:S(2)}) %collective-permute-start) | collective-permute-done | bytes 1048608 | tf_op jit(solution)/shard_map/while/body/eval_jaxpr/ppermute | solution.py:35
  599.4 6.5 collective-permute-start
  605.9 20.4 %collective-permute-done = f32[512,512]{0,1:T(8,128)} collective-permute-done((f32[512,512]{0,1:T(8,128)}, f32[512,512]{0,1:T(8,128)}, u32[]{:S(2)}, u32[]{:S(2)}) %collective-permute-start) | collective-permute-done | bytes 1048608 | tf_op jit(solution)/shard_map/while/body/eval_jaxpr/ppermute | solution.py:35
  630.6 6.5 collective-permute-start
  637.1 19.5 %collective-permute-done = f32[512,512]{0,1:T(8,128)} collective-permute-done((f32[512,512]{0,1:T(8,128)}, f32[512,512]{0,1:T(8,128)}, u32[]{:S(2)}, u32[]{:S(2)}) %collective-permute-start) | collective-permute-done | bytes 1048608 | tf_op jit(solution)/shard_map/while/body/eval_jaxpr/ppermute | solution.py:35
  660.8 6.5 collective-permute-start
  667.3 18.5 %collective-permute-done = f32[512,512]{0,1:T(8,128)} collective-permute-done((f32[512,512]{0,1:T(8,128)}, f32[512,512]{0,1:T(8,128)}, u32[]{:S(2)}, u32[]{:S(2)}) %collective-permute-start) | collective-permute-done | bytes 1048608 | tf_op jit(solution)/shard_map/while/body/eval_jaxpr/ppermute | solution.py:35
  690.2 6.5 collective-permute-start
  696.7 17.6 %collective-permute-done = f32[512,512]{0,1:T(8,128)} collective-permute-done((f32[512,512]{0,1:T(8,128)}, f32[512,512]{0,1:T(8,128)}, u32[]{:S(2)}, u32[]{:S(2)}) %collective-permute-start) | collective-permute-done | bytes 1048608 | tf_op jit(solution)/shard_map/while/body/eval_jaxpr/ppermute | solution.py:35
  718.6 6.5 collective-permute-start
  725.1 16.7 %collective-permute-done = f32[512,512]{0,1:T(8,128)} collective-permute-done((f32[512,512]{0,1:T(8,128)}, f32[512,512]{0,1:T(8,128)}, u32[]{:S(2)}, u32[]{:S(2)}) %collective-permute-start) | collective-permute-done | bytes 1048608 | tf_op jit(solution)/shard_map/while/body/eval_jaxpr/ppermute | solution.py:35
  746.1 6.5 collective-permute-start
  752.6 15.8 %collective-permute-done = f32[512,512]{0,1:T(8,128)} collective-permute-done((f32[512,512]{0,1:T(8,128)}, f32[512,512]{0,1:T(8,128)}, u32[]{:S(2)}, u32[]{:S(2)}) %collective-permute-start) | collective-permute-done | bytes 1048608 | tf_op jit(solution)/shard_map/while/body/eval_jaxpr/ppermute | solution.py:35
  772.7 6.5 collective-permute-start
  779.2 14.8 %collective-permute-done = f32[512,512]{0,1:T(8,128)} collective-permute-done((f32[512,512]{0,1:T(8,128)}, f32[512,512]{0,1:T(8,128)}, u32[]{:S(2)}, u32[]{:S(2)}) %collective-permute-start) | collective-permute-done | bytes 1048608 | tf_op jit(solution)/shard_map/while/body/eval_jaxpr/ppermute | solution.py:35
  798.3 6.5 collective-permute-start
  804.8 13.9 %collective-permute-done = f32[512,512]{0,1:T(8,128)} collective-permute-done((f32[512,512]{0,1:T(8,128)}, f32[512,512]{0,1:T(8,128)}, u32[]{:S(2)}, u32[]{:S(2)}) %collective-permute-start) | collective-permute-done | bytes 1048608 | tf_op jit(solution)/shard_map/while/body/eval_jaxpr/ppermute | solution.py:35
  823.0 6.5 collective-permute-start
  829.5 13.0 %collective-permute-done = f32[512,512]{0,1:T(8,128)} collective-permute-done((f32[512,512]{0,1:T(8,128)}, f32[512,512]{0,1:T(8,128)}, u32[]{:S(2)}, u32[]{:S(2)}) %collective-permute-start) | collective-permute-done | bytes 1048608 | tf_op jit(solution)/shard_map/while/body/eval_jaxpr/ppermute | solution.py:35
  846.8 6.5 collective-permute-start
  853.3 13.3 %collective-permute-done = f32[512,512]{0,1:T(8,128)} collective-permute-done((f32[512,512]{0,1:T(8,128)}, f32[512,512]{0,1:T(8,128)}, u32[]{:S(2)}, u32[]{:S(2)}) %collective-permute-start) | collective-permute-done | bytes 1048608 | tf_op jit(solution)/shard_map/while/body/eval_jaxpr/ppermute | solution.py:35
  870.9 6.5 collective-permute-start
  877.4 14.4 %collective-permute-done = f32[512,512]{0,1:T(8,128)} collective-permute-done((f32[512,512]{0,1:T(8,128)}, f32[512,512]{0,1:T(8,128)}, u32[]{:S(2)}, u32[]{:S(2)}) %collective-permute-start) | collective-permute-done | bytes 1048608 | tf_op jit(solution)/shard_map/while/body/eval_jaxpr/ppermute | solution.py:35
  896.1 6.5 collective-permute-start
  902.6 12.6 %collective-permute-done = f32[512,512]{0,1:T(8,128)} collective-permute-done((f32[512,512]{0,1:T(8,128)}, f32[512,512]{0,1:T(8,128)}, u32[]{:S(2)}, u32[]{:S(2)}) %collective-permute-start) | collective-permute-done | bytes 1048608 | tf_op jit(solution)/shard_map/while/body/eval_jaxpr/ppermute | solution.py:35
  923.0 20.6 %psum.7 = f32[1,512]{1,0:T(1,128)} all-reduce(f32[1,512]{1,0:T(1,128)S(1)} %bitcast.62), channel_id=1, replica_groups=mesh['sweep'=16,'cross'=2,'band'=8] {'band'}, use_global_device_ids=true, to_apply=%region_6.7 | all-reduce | flops 512 | bytes 4096 | tf_op jit(solution)/shard_map/psum | solution.py:104
  (243 shorter events, 212.4 us)
Async XLA Ops:
  8.6 29.1 %collective-permute-start.1 = (f32[512,512]{0,1:T(8,128)}, f32[512,512]{0,1:T(8,128)S(1)}, u32[]{:S(2)}, u32[]{:S(2)}) collective-permute-start(f32[512,512]{0,1:T(8,128)} %broadcast_select_fusion.4), channel_id=1, source_target_pairs={{0,16},{16,32},{32,48},{48,64},{64,80},{80,96},{96,112},{112,128},... | collective-permute-start | bytes 3145736 | tf_op jit(solution)/shard_map/while/body/eval_jaxpr/ppermute | solution.py:35
  42.1 28.2 %collective-permute-start.1 = (f32[512,512]{0,1:T(8,128)}, f32[512,512]{0,1:T(8,128)S(1)}, u32[]{:S(2)}, u32[]{:S(2)}) collective-permute-start(f32[512,512]{0,1:T(8,128)} %broadcast_select_fusion.4), channel_id=1, source_target_pairs={{0,16},{16,32},{32,48},{48,64},{64,80},{80,96},{96,112},{112,128},... | collective-permute-start | bytes 3145736 | tf_op jit(solution)/shard_map/while/body/eval_jaxpr/ppermute | solution.py:35
  70.6 3.1 copy-start.1
  74.8 27.3 %collective-permute-start.1 = (f32[512,512]{0,1:T(8,128)}, f32[512,512]{0,1:T(8,128)S(1)}, u32[]{:S(2)}, u32[]{:S(2)}) collective-permute-start(f32[512,512]{0,1:T(8,128)} %broadcast_select_fusion.4), channel_id=1, source_target_pairs={{0,16},{16,32},{32,48},{48,64},{64,80},{80,96},{96,112},{112,128},... | collective-permute-start | bytes 3145736 | tf_op jit(solution)/shard_map/while/body/eval_jaxpr/ppermute | solution.py:35
  106.5 26.4 %collective-permute-start.1 = (f32[512,512]{0,1:T(8,128)}, f32[512,512]{0,1:T(8,128)S(1)}, u32[]{:S(2)}, u32[]{:S(2)}) collective-permute-start(f32[512,512]{0,1:T(8,128)} %broadcast_select_fusion.4), channel_id=1, source_target_pairs={{0,16},{16,32},{32,48},{48,64},{64,80},{80,96},{96,112},{112,128},... | collective-permute-start | bytes 3145736 | tf_op jit(solution)/shard_map/while/body/eval_jaxpr/ppermute | solution.py:35
  137.3 25.5 %collective-permute-start.1 = (f32[512,512]{0,1:T(8,128)}, f32[512,512]{0,1:T(8,128)S(1)}, u32[]{:S(2)}, u32[]{:S(2)}) collective-permute-start(f32[512,512]{0,1:T(8,128)} %broadcast_select_fusion.4), channel_id=1, source_target_pairs={{0,16},{16,32},{32,48},{48,64},{64,80},{80,96},{96,112},{112,128},... | collective-permute-start | bytes 3145736 | tf_op jit(solution)/shard_map/while/body/eval_jaxpr/ppermute | solution.py:35
  162.9 3.1 copy-start.1
  167.1 24.5 %collective-permute-start.1 = (f32[512,512]{0,1:T(8,128)}, f32[512,512]{0,1:T(8,128)S(1)}, u32[]{:S(2)}, u32[]{:S(2)}) collective-permute-start(f32[512,512]{0,1:T(8,128)} %broadcast_select_fusion.4), channel_id=1, source_target_pairs={{0,16},{16,32},{32,48},{48,64},{64,80},{80,96},{96,112},{112,128},... | collective-permute-start | bytes 3145736 | tf_op jit(solution)/shard_map/while/body/eval_jaxpr/ppermute | solution.py:35
  191.9 3.1 copy-start.1
  196.1 23.6 %collective-permute-start.1 = (f32[512,512]{0,1:T(8,128)}, f32[512,512]{0,1:T(8,128)S(1)}, u32[]{:S(2)}, u32[]{:S(2)}) collective-permute-start(f32[512,512]{0,1:T(8,128)} %broadcast_select_fusion.4), channel_id=1, source_target_pairs={{0,16},{16,32},{32,48},{48,64},{64,80},{80,96},{96,112},{112,128},... | collective-permute-start | bytes 3145736 | tf_op jit(solution)/shard_map/while/body/eval_jaxpr/ppermute | solution.py:35
  219.9 3.1 copy-start.1
  224.1 22.7 %collective-permute-start.1 = (f32[512,512]{0,1:T(8,128)}, f32[512,512]{0,1:T(8,128)S(1)}, u32[]{:S(2)}, u32[]{:S(2)}) collective-permute-start(f32[512,512]{0,1:T(8,128)} %broadcast_select_fusion.4), channel_id=1, source_target_pairs={{0,16},{16,32},{32,48},{48,64},{64,80},{80,96},{96,112},{112,128},... | collective-permute-start | bytes 3145736 | tf_op jit(solution)/shard_map/while/body/eval_jaxpr/ppermute | solution.py:35
  251.2 21.8 %collective-permute-start.1 = (f32[512,512]{0,1:T(8,128)}, f32[512,512]{0,1:T(8,128)S(1)}, u32[]{:S(2)}, u32[]{:S(2)}) collective-permute-start(f32[512,512]{0,1:T(8,128)} %broadcast_select_fusion.4), channel_id=1, source_target_pairs={{0,16},{16,32},{32,48},{48,64},{64,80},{80,96},{96,112},{112,128},... | collective-permute-start | bytes 3145736 | tf_op jit(solution)/shard_map/while/body/eval_jaxpr/ppermute | solution.py:35
  273.2 3.1 copy-start.1
  277.4 20.8 %collective-permute-start.1 = (f32[512,512]{0,1:T(8,128)}, f32[512,512]{0,1:T(8,128)S(1)}, u32[]{:S(2)}, u32[]{:S(2)}) collective-permute-start(f32[512,512]{0,1:T(8,128)} %broadcast_select_fusion.4), channel_id=1, source_target_pairs={{0,16},{16,32},{32,48},{48,64},{64,80},{80,96},{96,112},{112,128},... | collective-permute-start | bytes 3145736 | tf_op jit(solution)/shard_map/while/body/eval_jaxpr/ppermute | solution.py:35
  298.4 3.1 copy-start.1
  302.6 19.9 %collective-permute-start.1 = (f32[512,512]{0,1:T(8,128)}, f32[512,512]{0,1:T(8,128)S(1)}, u32[]{:S(2)}, u32[]{:S(2)}) collective-permute-start(f32[512,512]{0,1:T(8,128)} %broadcast_select_fusion.4), channel_id=1, source_target_pairs={{0,16},{16,32},{32,48},{48,64},{64,80},{80,96},{96,112},{112,128},... | collective-permute-start | bytes 3145736 | tf_op jit(solution)/shard_map/while/body/eval_jaxpr/ppermute | solution.py:35
  322.8 3.1 copy-start.1
  326.9 19.2 %collective-permute-start.1 = (f32[512,512]{0,1:T(8,128)}, f32[512,512]{0,1:T(8,128)S(1)}, u32[]{:S(2)}, u32[]{:S(2)}) collective-permute-start(f32[512,512]{0,1:T(8,128)} %broadcast_select_fusion.4), channel_id=1, source_target_pairs={{0,16},{16,32},{32,48},{48,64},{64,80},{80,96},{96,112},{112,128},... | collective-permute-start | bytes 3145736 | tf_op jit(solution)/shard_map/while/body/eval_jaxpr/ppermute | solution.py:35
  350.5 20.2 %collective-permute-start.1 = (f32[512,512]{0,1:T(8,128)}, f32[512,512]{0,1:T(8,128)S(1)}, u32[]{:S(2)}, u32[]{:S(2)}) collective-permute-start(f32[512,512]{0,1:T(8,128)} %broadcast_select_fusion.4), channel_id=1, source_target_pairs={{0,16},{16,32},{32,48},{48,64},{64,80},{80,96},{96,112},{112,128},... | collective-permute-start | bytes 3145736 | tf_op jit(solution)/shard_map/while/body/eval_jaxpr/ppermute | solution.py:35
  375.1 21.3 %collective-permute-start.1 = (f32[512,512]{0,1:T(8,128)}, f32[512,512]{0,1:T(8,128)S(1)}, u32[]{:S(2)}, u32[]{:S(2)}) collective-permute-start(f32[512,512]{0,1:T(8,128)} %broadcast_select_fusion.4), channel_id=1, source_target_pairs={{0,16},{16,32},{32,48},{48,64},{64,80},{80,96},{96,112},{112,128},... | collective-permute-start | bytes 3145736 | tf_op jit(solution)/shard_map/while/body/eval_jaxpr/ppermute | solution.py:35
  396.7 3.1 copy-start.1
  400.8 22.4 %collective-permute-start.1 = (f32[512,512]{0,1:T(8,128)}, f32[512,512]{0,1:T(8,128)S(1)}, u32[]{:S(2)}, u32[]{:S(2)}) collective-permute-start(f32[512,512]{0,1:T(8,128)} %broadcast_select_fusion.4), channel_id=1, source_target_pairs={{0,16},{16,32},{32,48},{48,64},{64,80},{80,96},{96,112},{112,128},... | collective-permute-start | bytes 3145736 | tf_op jit(solution)/shard_map/while/body/eval_jaxpr/ppermute | solution.py:35
  423.4 3.1 copy-start.1
  427.6 19.0 %collective-permute-start.1 = (f32[512,512]{0,1:T(8,128)}, f32[512,512]{0,1:T(8,128)S(1)}, u32[]{:S(2)}, u32[]{:S(2)}) collective-permute-start(f32[512,512]{0,1:T(8,128)} %broadcast_select_fusion.4), channel_id=1, source_target_pairs={{0,16},{16,32},{32,48},{48,64},{64,80},{80,96},{96,112},{112,128},... | collective-permute-start | bytes 3145736 | tf_op jit(solution)/shard_map/while/body/eval_jaxpr/ppermute | solution.py:35
  446.8 3.1 copy-start.1
  450.0 6.0 copy-start.4
  452.6 10.8 %collective-permute-start.2 = (f32[1,16384]{1,0:T(1,128)}, f32[1,16384]{1,0:T(1,128)S(1)}, u32[]{:S(2)}, u32[]{:S(2)}) collective-permute-start(f32[1,16384]{1,0:T(1,128)} %bitcast.12), channel_id=1, source_target_pairs={{0,8},{1,9},{2,10},{3,11},{4,12},{5,13},{6,14},{7,15},{16,24},{17,... | collective-permute-start | bytes 196616 | tf_op jit(solution)/shard_map/ppermute | solution.py:23
  454.7 8.7 collective-permute-start.3
  456.0 11.2 %collective-permute-start.4 = (f32[1,16384]{1,0:T(1,128)S(1)}, f32[1,16384]{1,0:T(1,128)S(1)}, u32[]{:S(2)}, u32[]{:S(2)}) collective-permute-start(f32[1,16384]{1,0:T(1,128)S(1)} %bitcast.59), channel_id=1, source_target_pairs={{0,8},{1,9},{2,10},{3,11},{4,12},{5,13},{6,14},{7,15},{16,24},{17,... | collective-permute-start | bytes 196616 | tf_op jit(solution)/shard_map/ppermute | solution.py:23
  459.2 8.1 collective-permute-start.5
  470.5 449.1 %copy-start.2 = (f32[512,512]{0,1:T(8,128)S(1)}, f32[512,512]{0,1:T(8,128)}, u32[]{:S(2)}) copy-start(f32[512,512]{0,1:T(8,128)} %get-tuple-element.67) | copy-start | bytes 3145732
  470.5 28.2 %collective-permute-start = (f32[512,512]{0,1:T(8,128)}, f32[512,512]{0,1:T(8,128)}, u32[]{:S(2)}, u32[]{:S(2)}) collective-permute-start(f32[512,512]{0,1:T(8,128)} %get-tuple-element.233), channel_id=1, source_target_pairs={{16,0},{32,16},{48,32},{64,48},{80,64},{96,80},{112,96},{128,112},... | collective-permute-start | bytes 3145736 | tf_op jit(solution)/shard_map/while/body/eval_jaxpr/ppermute | solution.py:35
  503.0 27.4 %collective-permute-start = (f32[512,512]{0,1:T(8,128)}, f32[512,512]{0,1:T(8,128)}, u32[]{:S(2)}, u32[]{:S(2)}) collective-permute-start(f32[512,512]{0,1:T(8,128)} %get-tuple-element.233), channel_id=1, source_target_pairs={{16,0},{32,16},{48,32},{64,48},{80,64},{96,80},{112,96},{128,112},... | collective-permute-start | bytes 3145736 | tf_op jit(solution)/shard_map/while/body/eval_jaxpr/ppermute | solution.py:35
  534.7 28.2 %collective-permute-start = (f32[512,512]{0,1:T(8,128)}, f32[512,512]{0,1:T(8,128)}, u32[]{:S(2)}, u32[]{:S(2)}) collective-permute-start(f32[512,512]{0,1:T(8,128)} %get-tuple-element.233), channel_id=1, source_target_pairs={{16,0},{32,16},{48,32},{64,48},{80,64},{96,80},{112,96},{128,112},... | collective-permute-start | bytes 3145736 | tf_op jit(solution)/shard_map/while/body/eval_jaxpr/ppermute | solution.py:35
  567.2 27.8 %collective-permute-start = (f32[512,512]{0,1:T(8,128)}, f32[512,512]{0,1:T(8,128)}, u32[]{:S(2)}, u32[]{:S(2)}) collective-permute-start(f32[512,512]{0,1:T(8,128)} %get-tuple-element.233), channel_id=1, source_target_pairs={{16,0},{32,16},{48,32},{64,48},{80,64},{96,80},{112,96},{128,112},... | collective-permute-start | bytes 3145736 | tf_op jit(solution)/shard_map/while/body/eval_jaxpr/ppermute | solution.py:35
  599.4 26.9 %collective-permute-start = (f32[512,512]{0,1:T(8,128)}, f32[512,512]{0,1:T(8,128)}, u32[]{:S(2)}, u32[]{:S(2)}) collective-permute-start(f32[512,512]{0,1:T(8,128)} %get-tuple-element.233), channel_id=1, source_target_pairs={{16,0},{32,16},{48,32},{64,48},{80,64},{96,80},{112,96},{128,112},... | collective-permute-start | bytes 3145736 | tf_op jit(solution)/shard_map/while/body/eval_jaxpr/ppermute | solution.py:35
  630.6 26.0 %collective-permute-start = (f32[512,512]{0,1:T(8,128)}, f32[512,512]{0,1:T(8,128)}, u32[]{:S(2)}, u32[]{:S(2)}) collective-permute-start(f32[512,512]{0,1:T(8,128)} %get-tuple-element.233), channel_id=1, source_target_pairs={{16,0},{32,16},{48,32},{64,48},{80,64},{96,80},{112,96},{128,112},... | collective-permute-start | bytes 3145736 | tf_op jit(solution)/shard_map/while/body/eval_jaxpr/ppermute | solution.py:35
  660.8 25.0 %collective-permute-start = (f32[512,512]{0,1:T(8,128)}, f32[512,512]{0,1:T(8,128)}, u32[]{:S(2)}, u32[]{:S(2)}) collective-permute-start(f32[512,512]{0,1:T(8,128)} %get-tuple-element.233), channel_id=1, source_target_pairs={{16,0},{32,16},{48,32},{64,48},{80,64},{96,80},{112,96},{128,112},... | collective-permute-start | bytes 3145736 | tf_op jit(solution)/shard_map/while/body/eval_jaxpr/ppermute | solution.py:35
  690.2 24.1 %collective-permute-start = (f32[512,512]{0,1:T(8,128)}, f32[512,512]{0,1:T(8,128)}, u32[]{:S(2)}, u32[]{:S(2)}) collective-permute-start(f32[512,512]{0,1:T(8,128)} %get-tuple-element.233), channel_id=1, source_target_pairs={{16,0},{32,16},{48,32},{64,48},{80,64},{96,80},{112,96},{128,112},... | collective-permute-start | bytes 3145736 | tf_op jit(solution)/shard_map/while/body/eval_jaxpr/ppermute | solution.py:35
  718.6 23.2 %collective-permute-start = (f32[512,512]{0,1:T(8,128)}, f32[512,512]{0,1:T(8,128)}, u32[]{:S(2)}, u32[]{:S(2)}) collective-permute-start(f32[512,512]{0,1:T(8,128)} %get-tuple-element.233), channel_id=1, source_target_pairs={{16,0},{32,16},{48,32},{64,48},{80,64},{96,80},{112,96},{128,112},... | collective-permute-start | bytes 3145736 | tf_op jit(solution)/shard_map/while/body/eval_jaxpr/ppermute | solution.py:35
  746.1 22.3 %collective-permute-start = (f32[512,512]{0,1:T(8,128)}, f32[512,512]{0,1:T(8,128)}, u32[]{:S(2)}, u32[]{:S(2)}) collective-permute-start(f32[512,512]{0,1:T(8,128)} %get-tuple-element.233), channel_id=1, source_target_pairs={{16,0},{32,16},{48,32},{64,48},{80,64},{96,80},{112,96},{128,112},... | collective-permute-start | bytes 3145736 | tf_op jit(solution)/shard_map/while/body/eval_jaxpr/ppermute | solution.py:35
  772.7 21.3 %collective-permute-start = (f32[512,512]{0,1:T(8,128)}, f32[512,512]{0,1:T(8,128)}, u32[]{:S(2)}, u32[]{:S(2)}) collective-permute-start(f32[512,512]{0,1:T(8,128)} %get-tuple-element.233), channel_id=1, source_target_pairs={{16,0},{32,16},{48,32},{64,48},{80,64},{96,80},{112,96},{128,112},... | collective-permute-start | bytes 3145736 | tf_op jit(solution)/shard_map/while/body/eval_jaxpr/ppermute | solution.py:35
  798.3 20.4 %collective-permute-start = (f32[512,512]{0,1:T(8,128)}, f32[512,512]{0,1:T(8,128)}, u32[]{:S(2)}, u32[]{:S(2)}) collective-permute-start(f32[512,512]{0,1:T(8,128)} %get-tuple-element.233), channel_id=1, source_target_pairs={{16,0},{32,16},{48,32},{64,48},{80,64},{96,80},{112,96},{128,112},... | collective-permute-start | bytes 3145736 | tf_op jit(solution)/shard_map/while/body/eval_jaxpr/ppermute | solution.py:35
  823.0 19.5 %collective-permute-start = (f32[512,512]{0,1:T(8,128)}, f32[512,512]{0,1:T(8,128)}, u32[]{:S(2)}, u32[]{:S(2)}) collective-permute-start(f32[512,512]{0,1:T(8,128)} %get-tuple-element.233), channel_id=1, source_target_pairs={{16,0},{32,16},{48,32},{64,48},{80,64},{96,80},{112,96},{128,112},... | collective-permute-start | bytes 3145736 | tf_op jit(solution)/shard_map/while/body/eval_jaxpr/ppermute | solution.py:35
  846.8 19.8 %collective-permute-start = (f32[512,512]{0,1:T(8,128)}, f32[512,512]{0,1:T(8,128)}, u32[]{:S(2)}, u32[]{:S(2)}) collective-permute-start(f32[512,512]{0,1:T(8,128)} %get-tuple-element.233), channel_id=1, source_target_pairs={{16,0},{32,16},{48,32},{64,48},{80,64},{96,80},{112,96},{128,112},... | collective-permute-start | bytes 3145736 | tf_op jit(solution)/shard_map/while/body/eval_jaxpr/ppermute | solution.py:35
  870.9 20.9 %collective-permute-start = (f32[512,512]{0,1:T(8,128)}, f32[512,512]{0,1:T(8,128)}, u32[]{:S(2)}, u32[]{:S(2)}) collective-permute-start(f32[512,512]{0,1:T(8,128)} %get-tuple-element.233), channel_id=1, source_target_pairs={{16,0},{32,16},{48,32},{64,48},{80,64},{96,80},{112,96},{128,112},... | collective-permute-start | bytes 3145736 | tf_op jit(solution)/shard_map/while/body/eval_jaxpr/ppermute | solution.py:35
  896.1 19.1 %collective-permute-start = (f32[512,512]{0,1:T(8,128)}, f32[512,512]{0,1:T(8,128)}, u32[]{:S(2)}, u32[]{:S(2)}) collective-permute-start(f32[512,512]{0,1:T(8,128)} %get-tuple-element.233), channel_id=1, source_target_pairs={{16,0},{32,16},{48,32},{64,48},{80,64},{96,80},{112,96},{128,112},... | collective-permute-start | bytes 3145736 | tf_op jit(solution)/shard_map/while/body/eval_jaxpr/ppermute | solution.py:35
  (42 other events, 91.4 us)
where the time goes:
time: 948 us; the launch traced here: 944 us
  waiting for transfers between devices  624 us (66%)
  starting transfers between devices  135 us (14%)
  matrix products  79 us (8%)
  other arithmetic  46.6 us (5%)
  local copies, waits for them, and re-layouts  36 us (4%)
  blocking collectives  20.6 us (2%)
    ppermute x32, waiting for transfers between devices, from_behind(): return lax.ppermute(value, axis, pairs)  624 us
    ppermute x32, starting transfers between devices, from_behind(): return lax.ppermute(value, axis, pairs)  128 us
    dot_general x16, matrix products, product_flipped(): lax.dot_general(left, right, (((0,), (0,)), ((), ())), precision=lax.Prec...  45.9 us
    dot_general x17, matrix products, product(): jnp.dot(left, right, precision=lax.Precision.HIGHEST, preferred_element_t...  33.2 us
    add x16, other arithmetic, backward_step(): adjoint = cotangent + arriving  22.9 us
    psum x1, blocking collectives, per_device(): total = lax.psum(term, 'band')  20.6 us
    while x96, local copies, waits for them, and re-layouts  19.6 us
  transfers between devices with their start and end apart: 36, of which 32 were waited for; matrix products, arithmetic and copies ran while one was open for 1% of the time, Pallas kernels for 0%

commit v1 on v0

v1 whole, which is shorter than its diff:
```python
import functools
import math

import jax
import jax.numpy as jnp
from jax import lax
from jax.experimental import pallas as pl
from jax.experimental.pallas import tpu as pltpu
from jax.sharding import PartitionSpec as P

K = 512
R = 512
FV = 32
ROW = 4
ROWS = 4
CH = R // ROW
BANDS = 8
CROSS = 2
F32 = jnp.float32
BF16 = jnp.bfloat16
NT = (((1,), (1,)), ((), ()))
NN = (((1,), (0,)), ((), ()))
PARAMS = pltpu.CompilerParams(vmem_limit_bytes=56 * 1024 * 1024)

X_RING = {
    d: [(ROW * y + x, ROW * y + (x + d) % ROW) for y in range(ROWS) for x in range(ROW)] for d in range(1, ROW)
}
SWAP = [1, 0, 3, 2]
TURN = [3, 2, 1, 0]
Y_SWAP = [(ROW * y + x, ROW * SWAP[y] + x) for y in range(ROWS) for x in range(ROW)]
Y_TURN = [(ROW * y + x, ROW * TURN[y] + x) for y in range(ROWS) for x in range(ROW)]


def shift_x(value, by):
    return lax.ppermute(value, "sweep", X_RING[by % ROW])


def call(body, outs, *args, scratch=()):
    scalar = pl.BlockSpec(memory_space=pltpu.SMEM)
    vector = pl.BlockSpec(memory_space=pltpu.VMEM)
    return pl.pallas_call(
        body,
        out_shape=[jax.ShapeDtypeStruct(shape, dtype) for shape, dtype in outs],
        in_specs=[scalar if arg.ndim == 1 else vector for arg in args],
        out_specs=[vector] * len(outs),
        scratch_shapes=list(scratch),
        compiler_params=PARAMS,
    )(*args)


def place():
    at = lax.axis_index("sweep")
    return at % ROW, at // ROW


def split(value):
    high = value.astype(BF16)
    return high, (value - high.astype(F32)).astype(BF16)


def times(rows, high, low, dims):
    rows_high, rows_low = split(rows)
    count = rows.shape[0]
    both = lax.dot_general(
        jnp.concatenate([rows_high, rows_low], axis=0), high, dims, preferred_element_type=F32
    )
    cross = lax.dot_general(rows_high, low, dims, preferred_element_type=F32)
    return both[:count] + (both[count:] + cross)


def spread_body(source, response, before, after, sky, first, second, sky_rays):
    x, y = place()
    upsun = y < 2
    scale = 1.0 / math.sqrt(R)
    weights = response[...]
    up = jnp.concatenate([before[...], weights[:-FV]], axis=0)
    down = jnp.concatenate([weights[FV:], after[...]], axis=0)
    cot = (0.5 * weights + 0.25 * (up + down)) * scale
    for chunk in range(ROW):
        dist = (chunk - x + ROW) % ROW
        cols = slice(chunk * CH, (chunk + 1) * CH)
        emitted = source[:, cols].T
        cotangent = cot[:, cols].T
        first[dist] = jnp.where(upsun, emitted, cotangent)
        second[dist] = jnp.where(upsun, cotangent, emitted)
    sky_rays[...] = sky[:, pl.ds(pl.multiple_of(x * CH, CH), CH)].T


def forward_chain(high, low, emitted, incoming, keep):
    def step(j, state):
        gained = times(state, high[j], low[j], NT)
        state = gained + emitted[j]
        keep(j, gained, state)
        return state

    return lax.fori_loop(0, ROW, step, incoming)


def backward_chain(high, low, cotangent, incoming, keep, through):
    def step(i, state):
        j = ROW - 1 - i
        adjoint = cotangent[j] + state
        keep(j, adjoint)
        return times(adjoint, high[j], low[j], NN)

    state = lax.fori_loop(0, ROW - 1, step, incoming)
    adjoint = cotangent[0] + state
    keep(0, adjoint)
    if through:
        return times(adjoint, high[0], low[0], NN)
    return None


def start_body(own, left_top, left_bottom, right_top, right_bottom, far_top, far_bottom, e0, e1, e2, e3, sky_rays,
               high, low, given, saved, radiance, out):
    x, y = place()
    half = K // 2
    for dist, parts in enumerate(((own,), (left_top, left_bottom), (far_top, far_bottom), (right_top, right_bottom))):
        tile = (x - dist + ROW) % ROW
        size = K // len(parts)
        for at, part in enumerate(parts):
            part_high, part_low = split(part[...])
            high[tile, at * size:(at + 1) * size] = part_high
            low[tile, at * size:(at + 1) * size] = part_low
    for dist, part in enumerate((e0, e1, e2, e3)):
        given[(x - dist + ROW) % ROW] = part[...]

    @pl.when(y == 0)
    def _():
        def keep(j, gained, state):
            saved[j] = gained
            radiance[j] = state

        out[...] = forward_chain(high, low, given, sky_rays[...], keep)

    @pl.when(y == ROWS - 1)
    def _():
        def keep(j, adjoint):
            saved[j] = adjoint

        out[...] = backward_chain(high, low, given, jnp.zeros((CH, K), F32), keep, True)


def ends(high, low, given, y, forward_row, out):
    @pl.when(y == forward_row)
    def _():
        def step(j, state):
            return times(state, high[j], low[j], NT) + given[j]

        out[...] = lax.fori_loop(1, ROW, step, given[0])

    @pl.when(y == ROWS - 1 - forward_row)
    def _():
        out[...] = backward_chain(high, low, given, jnp.zeros((CH, K), F32), lambda j, a: None, True)


def compose_body(high, low, given, whole_high, whole_low, added):
    _, y = place()

    @pl.when((y == 1) | (y == 2))
    def _():
        def pair(at):
            return times(high[at + 1].astype(F32) + low[at + 1].astype(F32), high[at], low[at], NN)

        first_high, first_low = split(pair(0))
        whole = times(pair(2), first_high, first_low, NN)
        whole_high[...], whole_low[...] = split(whole)

    ends(high, low, given, y, 1, added)


def later_body(high, low, s0, s1, s2, s3, given, added):
    x, y = place()
    for dist, part in enumerate((s0, s1, s2, s3)):
        given[(x - dist + ROW) % ROW] = part[...]
    ends(high, low, given, y, 2, added)


def pass_body(forward_row, incoming, whole_high, whole_low, added, out):
    _, y = place()

    @pl.when(y == forward_row)
    def _():
        out[...] = times(incoming[...], whole_high[...], whole_low[...], NT) + added[...]

    @pl.when(y == ROWS - 1 - forward_row)
    def _():
        out[...] = times(incoming[...], whole_high[...], whole_low[...], NN) + added[...]


def middle_body(high, low, given, later, first_in, second_in, radiance, along, saved):
    _, y = place()
    for row, emitted, cotangent, state, adjoint_in in (
        (1, given, later, first_in, second_in),
        (2, later, given, second_in, first_in),
    ):
        @pl.when(y == row)
        def _():
            def keep_state(j, gained, new_state):
                saved[j] = gained
                radiance[j] = new_state

            def keep_adjoint(j, adjoint):
                along[j] = jnp.sum(adjoint * saved[j], axis=0, keepdims=True)

            forward_chain(high, low, emitted, state[...], keep_state)
            backward_chain(high, low, cotangent, adjoint_in[...], keep_adjoint, False)


def last_body(coeff, high, low, later, last_in, saved, early, middle, middle_along, out, along):
    x, y = place()
    factor = -coeff[0]

    @pl.when(y == 0)
    def _():
        def keep(j, adjoint):
            along[j] = factor * jnp.sum(adjoint * saved[j], axis=0, keepdims=True)

        backward_chain(high, low, later, last_in[...], keep, False)

    @pl.when(y == ROWS - 1)
    def _():
        def keep(j, gained, state):
            along[j] = factor * jnp.sum(gained * saved[j], axis=0, keepdims=True)
            out[(j - x + ROW) % ROW] = state

        forward_chain(high, low, later, last_in[...], keep)

    @pl.when(y == 0)
    def _():
        for j in range(ROW):
            out[(j - x + ROW) % ROW] = early[j]

    @pl.when((y == 1) | (y == 2))
    def _():
        for j in range(ROW):
            out[(j - x + ROW) % ROW] = middle[j]
            along[j] = factor * middle_along[j]


def sum_body(*refs):
    parts, out, held = refs[:BANDS], refs[BANDS], refs[BANDS + 1]
    x, _ = place()
    z = lax.axis_index("band")
    for dist, part in enumerate(parts):
        held[(z - dist + BANDS) % BANDS] = part[...]
    total = held[0]
    for band in range(1, BANDS):
        total = total + held[band]
    held[0] = total
    for dist in range(ROW):
        out[dist] = held[0, (x + dist) % ROW]


def turn_body(r0, r1, r2, r3, out, edge, grid):
    x, _ = place()
    for dist, part in enumerate((r0, r1, r2, r3)):
        chunk = (x - dist + ROW) % ROW
        grid[:, pl.ds(pl.multiple_of(chunk * CH, CH), CH)] = part[...].T
    whole = grid[...]
    zero = jnp.zeros((FV, R), F32)
    up = jnp.concatenate([zero, whole[:-FV]], axis=0)
    down = jnp.concatenate([whole[FV:], zero], axis=0)
    out[...] = 0.5 * whole + 0.25 * (up + down)
    edge[...] = jnp.where(lax.axis_index("cross") == 0, whole[-FV:], whole[:FV])


def per_device(operator, source, sky, response, extinction, leaf_density, leaf_class, occupied):
    matrix = operator[0, 0]
    weights = response[0, 0]
    coeff = extinction[0]
    table_size = leaf_density.shape[0]
    density = jnp.sum(
        jnp.where(leaf_class[0][:, None] == jnp.arange(table_size)[None, :], leaf_density[None, :], 0.0), axis=1
    )
    transmit = (1 - occupied[0]).astype(F32) * jnp.exp(-coeff * density)
    local = transmit[:, None] * matrix
    side = lax.axis_index("cross")
    other_side = [(0, 1), (1, 0)]

    half = K // 2
    top, bottom = local[:half], local[half:]
    left_top = shift_x(top, 1)
    right_bottom = shift_x(bottom, -1)
    left_bottom = shift_x(bottom, 1)
    right_top = shift_x(top, -1)

    edge = lax.ppermute(jnp.where(side == 0, weights[-FV:], weights[:FV]), "cross", other_side)
    before = jnp.where(side == 1, edge, 0.0)
    after = jnp.where(side == 0, edge, 0.0)
    chunk = ((ROW, CH, K), F32)
    part = ((CH, K), F32)
    first, second, sky_rays = call(spread_body, [chunk, chunk, part], source[0, 0], weights, before, after, sky[0])
    e0 = first[0]
    e1, e2, e3 = (shift_x(first[d], d) for d in (1, 2, 3))
    far_top = shift_x(left_top, 1)
    far_bottom = shift_x(right_bottom, -1)

    operators = ((ROW, K, K), BF16)
    high, low, given, saved, early, out = call(
        start_body, [operators, operators, chunk, chunk, chunk, part],
        local, left_top, left_bottom, right_top, right_bottom, far_top, far_bottom, e0, e1, e2, e3, sky_rays)
    first_in = lax.ppermute(out, "sweep", Y_SWAP)
    s0 = second[0]
    s1, s2, s3 = (shift_x(second[d], d) for d in (1, 2, 3))
    whole = ((K, K), BF16)
    whole_high, whole_low, added = call(compose_body, [whole, whole, part], high, low, given)
    (out,) = call(functools.partial(pass_body, 1), [part], first_in, whole_high, whole_low, added)
    second_in = lax.ppermute(out, "sweep", Y_TURN)
    later, added = call(later_body, [chunk, part], high, low, s0, s1, s2, s3)
    (out,) = call(functools.partial(pass_body, 2), [part], second_in, whole_high, whole_low, added)
    last_in = lax.ppermute(out, "sweep", Y_SWAP)
    line = ((ROW, 1, K), F32)
    middle, middle_along = call(
        middle_body, [chunk, line], high, low, given, later, first_in, second_in,
        scratch=[pltpu.VMEM((ROW, CH, K), F32)])
    rays, along = call(last_body, [chunk, line], extinction, high, low, later, last_in, saved, early, middle, middle_along)

    r0 = rays[0]
    r1, r2, r3 = (shift_x(rays[d], d) for d in (1, 2, 3))
    bands = [along] + [
        lax.ppermute(along, "band", [(i, (i + d) % BANDS) for i in range(BANDS)]) for d in range(1, BANDS)
    ]
    (lines,) = call(sum_body, [line], *bands, scratch=[pltpu.VMEM((BANDS, ROW, 1, K), F32)])
    total = lines[0] + shift_x(lines[1], 1) + shift_x(lines[2], 2) + shift_x(lines[3], 3)

    grid = ((K, R), F32)
    smooth, edge = call(turn_body, [grid, ((FV, R), F32)], r0, r1, r2, r3, scratch=[pltpu.VMEM((K, R), F32)])
    edge = lax.ppermute(edge, "cross", other_side)
    row = jnp.where(side == 0, K - FV, 0)
    rim = lax.dynamic_slice(smooth, (row, 0), (FV, R)) + 0.25 * edge
    observed = lax.dynamic_update_slice(smooth, rim, (row, 0))
    return (observed[None, None], total)


def solution(mesh):
    in_specs = (
        P("band", "sweep", "cross", None),
        P("band", "sweep", "cross", None),
        P("band", "cross", None),
        P("band", "sweep", "cross", None),
        P("band"),
        P(),
        P("sweep", "cross"),
        P("sweep", "cross"),
    )
    out_specs = (P("band", "sweep", "cross", None), P("sweep", "cross"))
    return jax.shard_map(
        per_device, mesh=mesh, in_specs=in_specs, out_specs=out_specs, check_vma=False
    )
```

time: 948 us -> 156 us (0.16)
  waiting for transfers between devices: 624 us -> 46.3 us
  starting transfers between devices: 135 us -> 49.5 us
  matrix products: 79 us -> 0 us
  other arithmetic: 46.6 us -> 6.51 us
  Pallas kernels: 0 us -> 37.6 us
  local copies, waits for them, and re-layouts: 36 us -> 13.2 us
  blocking collectives: 20.6 us -> 0 us
    ppermute x36 -> x30, waiting for transfers between devices: 624 us -> 46.3 us  [the longest x18 38.2 us: shift_x(): return lax.ppermute(value, 'sweep', X_RING[by % ROW])]
    ppermute x36 -> x30, starting transfers between devices: 135 us -> 49.5 us  [the longest x18 25.7 us: shift_x(): return lax.ppermute(value, 'sweep', X_RING[by % ROW])]
    dot_general x33 -> x0, matrix products: 79 us -> none  [the longest x16 45.9 us: product_flipped(): lax.dot_general(left, right, (((0,), (0,)), ((), ())), precision=lax.Prec...]
    pallas_call x0 -> x10, Pallas kernels: none -> 37.6 us  [call(): pl.pallas_call(body, out_shape=[jax.ShapeDtypeStruct(shape, dtype) for sh...]
    add x17 -> x1, other arithmetic: 24.3 us -> 1.27 us  [per_device(): lines[0] + shift_x(lines[1], 1) + shift_x(lines[2], 2)]
    while x98 -> x0, local copies, waits for them, and re-layouts: 21.2 us -> none
    psum x1 -> x0, blocking collectives: 20.6 us -> none  [per_device(): total = lax.psum(term, 'band')]
    while x16 -> x0, other arithmetic: 17.1 us -> none
  transfers between devices with their start and end apart: 36 -> 30, of which waited for: 32 -> 11; matrix products, arithmetic and copies ran while one was open for 1% -> 6% of each run, Pallas kernels for 0% -> 14%
where the time goes in v1:
time: 156 us; the launch traced here: 155 us
  starting transfers between devices  49.5 us (32%)
  waiting for transfers between devices  46.3 us (30%)
  Pallas kernels  37.6 us (24%)
  local copies, waits for them, and re-layouts  13.2 us (8%)
  other arithmetic  6.51 us (4%)
    ppermute x18, waiting for transfers between devices, shift_x(): return lax.ppermute(value, 'sweep', X_RING[by % ROW])  38.2 us
    pallas_call x10, Pallas kernels, call(): pl.pallas_call(body, out_shape=[jax.ShapeDtypeStruct(shape, dtype) for sh...  37.6 us
    ppermute x18, starting transfers between devices, shift_x(): return lax.ppermute(value, 'sweep', X_RING[by % ROW])  25.7 us
    ppermute x7, starting transfers between devices, per_device(): lax.ppermute(along, 'band', [(i, (i + d) % BANDS) for i in range(BANDS)])  19.8 us
    unnamed x59, local copies, waits for them, and re-layouts  7.68 us
    ppermute x7, waiting for transfers between devices, per_device(): lax.ppermute(along, 'band', [(i, (i + d) % BANDS) for i in range(BANDS)])  5.7 us
    ppermute x1, starting transfers between devices, per_device(): last_in = lax.ppermute(out, 'sweep', Y_SWAP)  3.57 us
  transfers between devices with their start and end apart: 30, of which 11 were waited for; matrix products, arithmetic and copies ran while one was open for 6% of the time, Pallas kernels for 14%

profile of v1, /device:TPU:24, one launch (start us, length us, event | category | flops | bytes accessed | tf_op | source)
XLA Modules:
  0.0 154.6 jit_solution(10710476976612891969)
XLA Ops:
  0.6 0.9 select_bitcast_fusion
  3.0 0.8 select_reduce_fusion
  3.8 1.4 bitcast_multiply_fusion.own
  5.2 2.8 %collective-permute-start.3 = (f32[256,512]{1,0:T(8,128)S(1)}, f32[256,512]{1,0:T(8,128)S(1)}, u32[]{:S(2)}, u32[]{:S(2)}) collective-permute-start(f32[256,512]{1,0:T(8,128)S(1)} %get-tuple-element.54), channel_id=1, source_target_pairs={{0,48},{16,0},{32,16},{48,32},{64,112},{80,64},{96,80},{112,96},{1... | collective-permute-start | bytes 1572872 | tf_op jit(solution)/shard_map/ppermute | solution.py:35
  8.7 4.0 %shard_map.95 = (f32[4,128,512]{2,1,0:T(8,128)}, f32[4,128,512]{2,1,0:T(8,128)}, f32[128,512]{1,0:T(8,128)}) custom-call(f32[512,512]{1,0:T(8,128)} %bitcast.53, f32[512,512]{1,0:T(8,128)} %bitcast.51, f32[32,512]{1,0:T(8,128)} %get-tuple-element.57.before, f32[32,512]{1,0:T(8,128)} %get-tuple-element.56.after, f32[512,512]{1,0:T(8,128)} %bitcast.54), custom_call_target="tpu_custom_call" | custom-call | tf_op jit(solution)/shard_map/pallas_call | solution.py:41
  12.7 2.0 %slice_bitcast_fusion.8 = (f32[128,512]{1,0:T(8,128)S(1)}, f32[128,512]{1,0:T(8,128)S(1)}, f32[128,512]{1,0:T(8,128)S(1)}, f32[128,512]{1,0:T(8,128)}) fusion(f32[4,128,512]{2,1,0:T(8,128)} %get-tuple-element.22), kind=kLoop, calls=%fused_computation.9 | loop fusion | bytes 2097152 | tf_op jit(solution)/shard_map/squeeze | solution.py:295
  14.7 3.2 %collective-permute-start.9 = (f32[128,512]{1,0:T(8,128)S(1)}, f32[128,512]{1,0:T(8,128)S(1)}, u32[]{:S(2)}, u32[]{:S(2)}) collective-permute-start(f32[128,512]{1,0:T(8,128)S(1)} %get-tuple-element.50), channel_id=1, source_target_pairs={{0,48},{16,0},{32,16},{48,32},{64,112},{80,64},{96,80},{112,96},{1... | collective-permute-start | bytes 786440 | tf_op jit(solution)/shard_map/ppermute | solution.py:35
  17.9 1.5 collective-permute-start.8
  19.4 11.8 %collective-permute-done.9.e3 = f32[128,512]{1,0:T(8,128)S(1)} collective-permute-done((f32[128,512]{1,0:T(8,128)S(1)}, f32[128,512]{1,0:T(8,128)S(1)}, u32[]{:S(2)}, u32[]{:S(2)}) %collective-permute-start.9) | collective-permute-done | bytes 262176 | tf_op jit(solution)/shard_map/ppermute | solution.py:35
  31.2 3.7 %collective-permute-start.2 = (f32[256,512]{1,0:T(8,128)S(1)}, f32[256,512]{1,0:T(8,128)S(1)}, u32[]{:S(2)}, u32[]{:S(2)}) collective-permute-start(f32[256,512]{1,0:T(8,128)S(1)} %get-tuple-element.55), channel_id=1, source_target_pairs={{0,48},{16,0},{32,16},{48,32},{64,112},{80,64},{96,80},{112,96},{1... | collective-permute-start | bytes 1572872 | tf_op jit(solution)/shard_map/ppermute | solution.py:35
  34.9 1.9 %collective-permute-start.4 = (f32[256,512]{1,0:T(8,128)S(1)}, f32[256,512]{1,0:T(8,128)S(1)}, u32[]{:S(2)}, u32[]{:S(2)}) collective-permute-start(f32[256,512]{1,0:T(8,128)S(1)} %collective-permute-done.left_top), channel_id=1, source_target_pairs={{0,16},{16,32},{32,48},{48,0},{64,80},{80,96},{96,112},{112,64},{1... | collective-permute-start | bytes 1572872 | tf_op jit(solution)/shard_map/ppermute | solution.py:35
  36.9 3.1 %collective-permute-done.8.e2 = f32[128,512]{1,0:T(8,128)S(1)} collective-permute-done((f32[128,512]{1,0:T(8,128)S(1)}, f32[128,512]{1,0:T(8,128)S(1)}, u32[]{:S(2)}, u32[]{:S(2)}) %collective-permute-start.8) | collective-permute-done | bytes 262176 | tf_op jit(solution)/shard_map/ppermute | solution.py:35
  40.0 17.0 %collective-permute-done.7.e1 = f32[128,512]{1,0:T(8,128)S(1)} collective-permute-done((f32[128,512]{1,0:T(8,128)S(1)}, f32[128,512]{1,0:T(8,128)S(1)}, u32[]{:S(2)}, u32[]{:S(2)}) %collective-permute-start.7) | collective-permute-done | bytes 262176 | tf_op jit(solution)/shard_map/ppermute | solution.py:35
  58.5 7.9 %shard_map.96 = (bf16[4,512,512]{2,1,0:T(8,128)(2,1)}, bf16[4,512,512]{2,1,0:T(8,128)(2,1)}, f32[4,128,512]{2,1,0:T(8,128)}, f32[4,128,512]{2,1,0:T(8,128)}, f32[4,128,512]{2,1,0:T(8,128)}, /*index=5*/f32[128,512]{1,0:T(8,128)}) custom-call(f32[512,512]{1,0:T(8,128)} %copy-done, f32[256,512]{1,0:T(8,128)} %copy-done.6, f32[256,512]{1,0:T(8,128)} %copy-done.7, ...), custom_call_target="tpu_custom_call" | custom-call | tf_op jit(solution)/shard_map/pallas_call | solution.py:41
  66.4 0.8 slice_bitcast_fusion.4
  67.2 3.4 %collective-permute-start.12 = (f32[128,512]{1,0:T(8,128)S(1)}, f32[128,512]{1,0:T(8,128)S(1)}, u32[]{:S(2)}, u32[]{:S(2)}) collective-permute-start(f32[128,512]{1,0:T(8,128)S(1)} %get-tuple-element.46), channel_id=1, source_target_pairs={{0,48},{16,0},{32,16},{48,32},{64,112},{80,64},{96,80},{112,96},{1... | collective-permute-start | bytes 786440 | tf_op jit(solution)/shard_map/ppermute | solution.py:35
  70.5 0.9 collective-permute-start.10
  71.4 3.5 %shard_map.98 = (bf16[512,512]{1,0:T(8,128)(2,1)}, bf16[512,512]{1,0:T(8,128)(2,1)}, f32[128,512]{1,0:T(8,128)}) custom-call(bf16[4,512,512]{2,1,0:T(8,128)(2,1)} %get-tuple-element.24.high, bf16[4,512,512]{2,1,0:T(8,128)(2,1)} %get-tuple-element.25.low, f32[4,128,512]{2,1,0:T(8,128)} %get-tuple-element.29.given), custom_call_target="tpu_custom_call" | custom-call | tf_op jit(solution)/shard_map/pallas_call | solution.py:41
  75.6 2.0 %shard_map.99 = f32[128,512]{1,0:T(8,128)} custom-call(f32[128,512]{1,0:T(8,128)} %copy-done.3, bf16[512,512]{1,0:T(8,128)(2,1)} %get-tuple-element.30.whole_high, bf16[512,512]{1,0:T(8,128)(2,1)} %get-tuple-element.31.whole_low, f32[128,512]{1,0:T(8,128)} %get-tuple-element.32.added), custom_call_target="tpu_custom_call" | custom-call | tf_op jit(solution)/shard_map/pallas_call | solution.py:41
  77.9 2.8 %collective-permute-done.12.s3 = f32[128,512]{1,0:T(8,128)S(1)} collective-permute-done((f32[128,512]{1,0:T(8,128)S(1)}, f32[128,512]{1,0:T(8,128)S(1)}, u32[]{:S(2)}, u32[]{:S(2)}) %collective-permute-start.12) | collective-permute-done | bytes 262176 | tf_op jit(solution)/shard_map/ppermute | solution.py:35
  81.3 2.8 %collective-permute-done.10.s1 = f32[128,512]{1,0:T(8,128)S(1)} collective-permute-done((f32[128,512]{1,0:T(8,128)S(1)}, f32[128,512]{1,0:T(8,128)S(1)}, u32[]{:S(2)}, u32[]{:S(2)}) %collective-permute-start.10) | collective-permute-done | bytes 262176 | tf_op jit(solution)/shard_map/ppermute | solution.py:35
  84.8 3.6 %shard_map.97 = (f32[4,128,512]{2,1,0:T(8,128)}, f32[128,512]{1,0:T(8,128)}) custom-call(bf16[4,512,512]{2,1,0:T(8,128)(2,1)} %get-tuple-element.24.high, bf16[4,512,512]{2,1,0:T(8,128)(2,1)} %get-tuple-element.25.low, f32[128,512]{1,0:T(8,128)} %get-tuple-element.49.s0, f32[128,512]{1,0:T(8,128)} %copy-done.13, f32[128,512]{1,0:T(8,128)} %copy-done.12, ...), custom_call_target="tpu_custom_call" | custom-call | tf_op jit(solution)/shard_map/pallas_call | solution.py:41
  89.1 2.0 %shard_map.100 = f32[128,512]{1,0:T(8,128)} custom-call(f32[128,512]{1,0:T(8,128)} %copy-done.4, bf16[512,512]{1,0:T(8,128)(2,1)} %get-tuple-element.30.whole_high, bf16[512,512]{1,0:T(8,128)(2,1)} %get-tuple-element.31.whole_low, f32[128,512]{1,0:T(8,128)} %get-tuple-element.33.added), custom_call_target="tpu_custom_call" | custom-call | tf_op jit(solution)/shard_map/pallas_call | solution.py:41
  91.1 3.6 %collective-permute-start.15 = (f32[128,512]{1,0:T(8,128)}, f32[128,512]{1,0:T(8,128)S(1)}, u32[]{:S(2)}, u32[]{:S(2)}) collective-permute-start(f32[128,512]{1,0:T(8,128)} %shard_map.100), channel_id=1, source_target_pairs={{0,64},{16,80},{32,96},{48,112},{64,0},{80,16},{96,32},{112,48},{1... | collective-permute-start | bytes 786440 | tf_op jit(solution)/shard_map/ppermute | solution.py:312
  94.7 3.9 %shard_map.101 = (f32[4,128,512]{2,1,0:T(8,128)}, f32[4,1,512]{2,1,0:T(1,128)}) custom-call(bf16[4,512,512]{2,1,0:T(8,128)(2,1)} %get-tuple-element.24.high, bf16[4,512,512]{2,1,0:T(8,128)(2,1)} %get-tuple-element.25.low, f32[4,128,512]{2,1,0:T(8,128)} %get-tuple-element.29.given, f32[4,128,512]{2,1,0:T(8,128)} %get-tuple-element.27.later, ...), custom_call_target="tpu_custom_call" | custom-call | tf_op jit(solution)/shard_map/pallas_call | solution.py:41
  98.6 2.4 %collective-permute-done.15.last_in = f32[128,512]{1,0:T(8,128)S(1)} collective-permute-done((f32[128,512]{1,0:T(8,128)}, f32[128,512]{1,0:T(8,128)S(1)}, u32[]{:S(2)}, u32[]{:S(2)}) %collective-permute-start.15) | collective-permute-done | bytes 262176 | tf_op jit(solution)/shard_map/ppermute | solution.py:312
  101.7 6.4 %shard_map.102 = (f32[4,128,512]{2,1,0:T(8,128)}, f32[4,1,512]{2,1,0:T(1,128)}) custom-call(f32[1]{0:T(128)S(6)} %copy.11.coeff, bf16[4,512,512]{2,1,0:T(8,128)(2,1)} %get-tuple-element.24.high, bf16[4,512,512]{2,1,0:T(8,128)(2,1)} %get-tuple-element.25.low, f32[4,128,512]{2,1,0:T(8,128)} %get-tuple-element.27.later, f32[128,512]{1,0:T(8,128)} %copy-done.14, ...), custom_call_target="tpu_custom_call" | custom-call | tf_op jit(solution)/shard_map/pallas_call | solution.py:41
  108.1 2.0 %slice_bitcast_fusion = (f32[128,512]{1,0:T(8,128)S(1)}, f32[128,512]{1,0:T(8,128)S(1)}, f32[128,512]{1,0:T(8,128)S(1)}, f32[128,512]{1,0:T(8,128)}) fusion(f32[4,128,512]{2,1,0:T(8,128)} %get-tuple-element.38), kind=kLoop, calls=%fused_computation.1 | loop fusion | bytes 2097152 | tf_op jit(solution)/shard_map/squeeze | solution.py:320
  110.1 2.2 %collective-permute-start.17 = (f32[128,512]{1,0:T(8,128)S(1)}, f32[128,512]{1,0:T(8,128)S(1)}, u32[]{:S(2)}, u32[]{:S(2)}) collective-permute-start(f32[128,512]{1,0:T(8,128)S(1)} %get-tuple-element.43), channel_id=1, source_target_pairs={{0,32},{16,48},{32,0},{48,16},{64,96},{80,112},{96,64},{112,80},{1... | collective-permute-start | bytes 786440 | tf_op jit(solution)/shard_map/ppermute | solution.py:35
  112.3 5.9 %collective-permute-start.26 = (f32[4,1,512]{2,1,0:T(1,128)S(1)}, f32[4,1,512]{2,1,0:T(1,128)S(1)}, u32[]{:S(2)}, u32[]{:S(2)}) collective-permute-start(f32[4,1,512]{2,1,0:T(1,128)S(1)} %copy-done.21), channel_id=1, source_target_pairs={{0,7},{1,0},{2,1},{3,2},{4,3},{5,4},{6,5},{7,6},{8,15},{9,8},{10,9... | collective-permute-start | bytes 24584 | tf_op jit(solution)/shard_map/ppermute | solution.py:322
  118.1 1.4 collective-permute-start.25
  119.6 3.1 %collective-permute-start.24 = (f32[4,1,512]{2,1,0:T(1,128)S(1)}, f32[4,1,512]{2,1,0:T(1,128)S(1)}, u32[]{:S(2)}, u32[]{:S(2)}) collective-permute-start(f32[4,1,512]{2,1,0:T(1,128)S(1)} %copy-done.21), channel_id=1, source_target_pairs={{0,5},{1,6},{2,7},{3,0},{4,1},{5,2},{6,3},{7,4},{8,13},{9,14},{10,... | collective-permute-start | bytes 24584 | tf_op jit(solution)/shard_map/ppermute | solution.py:322
  122.7 2.4 %collective-permute-start.23 = (f32[4,1,512]{2,1,0:T(1,128)S(1)}, f32[4,1,512]{2,1,0:T(1,128)S(1)}, u32[]{:S(2)}, u32[]{:S(2)}) collective-permute-start(f32[4,1,512]{2,1,0:T(1,128)S(1)} %copy-done.21), channel_id=1, source_target_pairs={{0,4},{1,5},{2,6},{3,7},{4,0},{5,1},{6,2},{7,3},{8,12},{9,13},{10,... | collective-permute-start | bytes 24584 | tf_op jit(solution)/shard_map/ppermute | solution.py:322
  125.1 3.3 %collective-permute-start.22 = (f32[4,1,512]{2,1,0:T(1,128)S(1)}, f32[4,1,512]{2,1,0:T(1,128)S(1)}, u32[]{:S(2)}, u32[]{:S(2)}) collective-permute-start(f32[4,1,512]{2,1,0:T(1,128)S(1)} %copy-done.21), channel_id=1, source_target_pairs={{0,3},{1,4},{2,5},{3,6},{4,7},{5,0},{6,1},{7,2},{8,11},{9,12},{10,... | collective-permute-start | bytes 24584 | tf_op jit(solution)/shard_map/ppermute | solution.py:322
  128.4 1.8 %collective-permute-done.23.refs_4_ = f32[4,1,512]{2,1,0:T(1,128)S(1)} collective-permute-done((f32[4,1,512]{2,1,0:T(1,128)S(1)}, f32[4,1,512]{2,1,0:T(1,128)S(1)}, u32[]{:S(2)}, u32[]{:S(2)}) %collective-permute-start.23) | collective-permute-done | bytes 8224 | tf_op jit(solution)/shard_map/ppermute | solution.py:322
  130.2 2.7 %collective-permute-start.21 = (f32[4,1,512]{2,1,0:T(1,128)S(1)}, f32[4,1,512]{2,1,0:T(1,128)S(1)}, u32[]{:S(2)}, u32[]{:S(2)}) collective-permute-start(f32[4,1,512]{2,1,0:T(1,128)S(1)} %copy-done.21), channel_id=1, source_target_pairs={{0,2},{1,3},{2,4},{3,5},{4,6},{5,7},{6,0},{7,1},{8,10},{9,11},{10,... | collective-permute-start | bytes 24584 | tf_op jit(solution)/shard_map/ppermute | solution.py:322
  133.0 1.0 collective-permute-start.20
  134.0 2.0 %collective-permute-done.21.refs_2_ = f32[4,1,512]{2,1,0:T(1,128)S(1)} collective-permute-done((f32[4,1,512]{2,1,0:T(1,128)S(1)}, f32[4,1,512]{2,1,0:T(1,128)S(1)}, u32[]{:S(2)}, u32[]{:S(2)}) %collective-permute-start.21) | collective-permute-done | bytes 8224 | tf_op jit(solution)/shard_map/ppermute | solution.py:322
  136.0 1.8 %collective-permute-done.20.refs_1_ = f32[4,1,512]{2,1,0:T(1,128)S(1)} collective-permute-done((f32[4,1,512]{2,1,0:T(1,128)S(1)}, f32[4,1,512]{2,1,0:T(1,128)S(1)}, u32[]{:S(2)}, u32[]{:S(2)}) %collective-permute-start.20) | collective-permute-done | bytes 8224 | tf_op jit(solution)/shard_map/ppermute | solution.py:322
  138.5 1.4 shard_map.104
  140.6 1.3 collective-permute-start.27
  141.9 2.0 %collective-permute-start.29 = (f32[1,512]{1,0:T(1,128)S(1)}, f32[1,512]{1,0:T(1,128)S(1)}, u32[]{:S(2)}, u32[]{:S(2)}) collective-permute-start(f32[1,512]{1,0:T(1,128)S(1)} %get-tuple-element.59), channel_id=1, source_target_pairs={{0,48},{16,0},{32,16},{48,32},{64,112},{80,64},{96,80},{112,96},{1... | collective-permute-start | bytes 6152 | tf_op jit(solution)/shard_map/ppermute | solution.py:35
  143.9 2.8 %collective-permute-start.28 = (f32[1,512]{1,0:T(1,128)S(1)}, f32[1,512]{1,0:T(1,128)S(1)}, u32[]{:S(2)}, u32[]{:S(2)}) collective-permute-start(f32[1,512]{1,0:T(1,128)S(1)} %get-tuple-element.60), channel_id=1, source_target_pairs={{0,32},{16,48},{32,0},{48,16},{64,96},{80,112},{96,64},{112,80},{1... | collective-permute-start | bytes 6152 | tf_op jit(solution)/shard_map/ppermute | solution.py:35
  147.5 2.8 %shard_map.103 = (f32[512,512]{1,0:T(8,128)}, f32[32,512]{1,0:T(8,128)}) custom-call(f32[128,512]{1,0:T(8,128)} %get-tuple-element.45.r0, f32[128,512]{1,0:T(8,128)} %copy-done.17, f32[128,512]{1,0:T(8,128)} %copy-done.16, f32[128,512]{1,0:T(8,128)} %copy-done.15), custom_call_target="tpu_custom_call" | custom-call | tf_op jit(solution)/shard_map/pallas_call | solution.py:41
  150.3 1.3 fusion.2
  151.5 1.2 copy.10
  152.8 0.9 bitcast_dynamic-update-slice_fusion
  153.6 1.0 copy-done.2
  (94 shorter events, 8.8 us)
Async XLA Ops:
  1.5 6.5 %collective-permute-start.6 = (f32[32,512]{1,0:T(8,128)S(1)}, f32[32,512]{1,0:T(8,128)S(1)}, u32[]{:S(2)}, u32[]{:S(2)}) collective-permute-start(f32[32,512]{1,0:T(8,128)S(1)} %select_bitcast_fusion), channel_id=1, source_target_pairs={{0,8},{8,0},{1,9},{9,1},{2,10},{10,2},{3,11},{11,3},{4,12},{12,4},... | collective-permute-start | bytes 196616 | tf_op jit(solution)/shard_map/ppermute | solution.py:288
  5.1 7.6 %copy-start = (f32[512,512]{1,0:T(8,128)}, f32[512,512]{1,0:T(8,128)S(1)}, u32[]{:S(2)}) copy-start(f32[512,512]{1,0:T(8,128)S(1)} %bitcast_multiply_fusion.own) | copy-start | bytes 3145732
  5.2 29.6 %collective-permute-start.3 = (f32[256,512]{1,0:T(8,128)S(1)}, f32[256,512]{1,0:T(8,128)S(1)}, u32[]{:S(2)}, u32[]{:S(2)}) collective-permute-start(f32[256,512]{1,0:T(8,128)S(1)} %get-tuple-element.54), channel_id=1, source_target_pairs={{0,48},{16,0},{32,16},{48,32},{64,112},{80,64},{96,80},{112,96},{1... | collective-permute-start | bytes 1572872 | tf_op jit(solution)/shard_map/ppermute | solution.py:35
  8.0 26.9 %collective-permute-start = (f32[256,512]{1,0:T(8,128)S(1)}, f32[256,512]{1,0:T(8,128)S(1)}, u32[]{:S(2)}, u32[]{:S(2)}) collective-permute-start(f32[256,512]{1,0:T(8,128)S(1)} %get-tuple-element.55), channel_id=1, source_target_pairs={{0,16},{16,32},{32,48},{48,0},{64,80},{80,96},{96,112},{112,64},{1... | collective-permute-start | bytes 1572872 | tf_op jit(solution)/shard_map/ppermute | solution.py:35
  14.7 16.5 %collective-permute-start.9 = (f32[128,512]{1,0:T(8,128)S(1)}, f32[128,512]{1,0:T(8,128)S(1)}, u32[]{:S(2)}, u32[]{:S(2)}) collective-permute-start(f32[128,512]{1,0:T(8,128)S(1)} %get-tuple-element.50), channel_id=1, source_target_pairs={{0,48},{16,0},{32,16},{48,32},{64,112},{80,64},{96,80},{112,96},{1... | collective-permute-start | bytes 786440 | tf_op jit(solution)/shard_map/ppermute | solution.py:35
  17.9 39.1 %collective-permute-start.1 = (f32[256,512]{1,0:T(8,128)S(1)}, f32[256,512]{1,0:T(8,128)S(1)}, u32[]{:S(2)}, u32[]{:S(2)}) collective-permute-start(f32[256,512]{1,0:T(8,128)S(1)} %get-tuple-element.54), channel_id=1, source_target_pairs={{0,16},{16,32},{32,48},{48,0},{64,80},{80,96},{96,112},{112,64},{1... | collective-permute-start | bytes 1572872 | tf_op jit(solution)/shard_map/ppermute | solution.py:35
  17.9 22.0 %collective-permute-start.8 = (f32[128,512]{1,0:T(8,128)S(1)}, f32[128,512]{1,0:T(8,128)S(1)}, u32[]{:S(2)}, u32[]{:S(2)}) collective-permute-start(f32[128,512]{1,0:T(8,128)S(1)} %get-tuple-element.51), channel_id=1, source_target_pairs={{0,32},{16,48},{32,0},{48,16},{64,96},{80,112},{96,64},{112,80},{1... | collective-permute-start | bytes 786440 | tf_op jit(solution)/shard_map/ppermute | solution.py:35
  31.2 26.0 %copy-start.18 = (f32[128,512]{1,0:T(8,128)}, f32[128,512]{1,0:T(8,128)S(1)}, u32[]{:S(2)}) copy-start(f32[128,512]{1,0:T(8,128)S(1)} %collective-permute-done.9.e3) | copy-start | bytes 786436
  31.2 25.9 %collective-permute-start.2 = (f32[256,512]{1,0:T(8,128)S(1)}, f32[256,512]{1,0:T(8,128)S(1)}, u32[]{:S(2)}, u32[]{:S(2)}) collective-permute-start(f32[256,512]{1,0:T(8,128)S(1)} %get-tuple-element.55), channel_id=1, source_target_pairs={{0,48},{16,0},{32,16},{48,32},{64,112},{80,64},{96,80},{112,96},{1... | collective-permute-start | bytes 1572872 | tf_op jit(solution)/shard_map/ppermute | solution.py:35
  34.8 22.3 %copy-start.5 = (f32[256,512]{1,0:T(8,128)}, f32[256,512]{1,0:T(8,128)S(1)}, u32[]{:S(2)}) copy-start(f32[256,512]{1,0:T(8,128)S(1)} %collective-permute-done.3.right_bottom) | copy-start | bytes 1572868
  34.8 22.3 %collective-permute-start.5 = (f32[256,512]{1,0:T(8,128)S(1)}, f32[256,512]{1,0:T(8,128)S(1)}, u32[]{:S(2)}, u32[]{:S(2)}) collective-permute-start(f32[256,512]{1,0:T(8,128)S(1)} %collective-permute-done.3.right_bottom), channel_id=1, source_target_pairs={{0,48},{16,0},{32,16},{48,32},{64,112},{80,64},{96,80},{112,96},{1... | collective-permute-start | bytes 1572872 | tf_op jit(solution)/shard_map/ppermute | solution.py:35
  34.9 22.2 %copy-start.6 = (f32[256,512]{1,0:T(8,128)}, f32[256,512]{1,0:T(8,128)S(1)}, u32[]{:S(2)}) copy-start(f32[256,512]{1,0:T(8,128)S(1)} %collective-permute-done.left_top) | copy-start | bytes 1572868
  34.9 22.2 %collective-permute-start.4 = (f32[256,512]{1,0:T(8,128)S(1)}, f32[256,512]{1,0:T(8,128)S(1)}, u32[]{:S(2)}, u32[]{:S(2)}) collective-permute-start(f32[256,512]{1,0:T(8,128)S(1)} %collective-permute-done.left_top), channel_id=1, source_target_pairs={{0,16},{16,32},{32,48},{48,0},{64,80},{80,96},{96,112},{112,64},{1... | collective-permute-start | bytes 1572872 | tf_op jit(solution)/shard_map/ppermute | solution.py:35
  40.0 17.2 %copy-start.19 = (f32[128,512]{1,0:T(8,128)}, f32[128,512]{1,0:T(8,128)S(1)}, u32[]{:S(2)}) copy-start(f32[128,512]{1,0:T(8,128)S(1)} %collective-permute-done.8.e2) | copy-start | bytes 786436
  40.0 17.0 %collective-permute-start.7 = (f32[128,512]{1,0:T(8,128)S(1)}, f32[128,512]{1,0:T(8,128)S(1)}, u32[]{:S(2)}, u32[]{:S(2)}) collective-permute-start(f32[128,512]{1,0:T(8,128)S(1)} %get-tuple-element.52), channel_id=1, source_target_pairs={{0,16},{16,32},{32,48},{48,0},{64,80},{80,96},{96,112},{112,64},{1... | collective-permute-start | bytes 786440 | tf_op jit(solution)/shard_map/ppermute | solution.py:35
  57.1 1.2 copy-start.9
  57.1 1.3 copy-start.10
  58.4 7.9 %copy-start.1 = (f32[4,128,512]{2,1,0:T(8,128)S(1)}, f32[4,128,512]{2,1,0:T(8,128)}, u32[]{:S(2)}) copy-start(f32[4,128,512]{2,1,0:T(8,128)} %get-tuple-element.26) | copy-start | bytes 3145732
  66.4 8.5 %collective-permute-start.13 = (f32[128,512]{1,0:T(8,128)}, f32[128,512]{1,0:T(8,128)S(1)}, u32[]{:S(2)}, u32[]{:S(2)}) collective-permute-start(f32[128,512]{1,0:T(8,128)} %get-tuple-element.28), channel_id=1, source_target_pairs={{0,64},{16,80},{32,96},{48,112},{64,0},{80,16},{96,32},{112,48},{1... | collective-permute-start | bytes 786440 | tf_op jit(solution)/shard_map/ppermute | solution.py:303
  67.2 13.6 %collective-permute-start.12 = (f32[128,512]{1,0:T(8,128)S(1)}, f32[128,512]{1,0:T(8,128)S(1)}, u32[]{:S(2)}, u32[]{:S(2)}) collective-permute-start(f32[128,512]{1,0:T(8,128)S(1)} %get-tuple-element.46), channel_id=1, source_target_pairs={{0,48},{16,0},{32,16},{48,32},{64,112},{80,64},{96,80},{112,96},{1... | collective-permute-start | bytes 786440 | tf_op jit(solution)/shard_map/ppermute | solution.py:35
  70.5 10.8 %collective-permute-start.11 = (f32[128,512]{1,0:T(8,128)S(1)}, f32[128,512]{1,0:T(8,128)S(1)}, u32[]{:S(2)}, u32[]{:S(2)}) collective-permute-start(f32[128,512]{1,0:T(8,128)S(1)} %get-tuple-element.47), channel_id=1, source_target_pairs={{0,32},{16,48},{32,0},{48,16},{64,96},{80,112},{96,64},{112,80},{1... | collective-permute-start | bytes 786440 | tf_op jit(solution)/shard_map/ppermute | solution.py:35
  70.5 13.6 %collective-permute-start.10 = (f32[128,512]{1,0:T(8,128)S(1)}, f32[128,512]{1,0:T(8,128)S(1)}, u32[]{:S(2)}, u32[]{:S(2)}) collective-permute-start(f32[128,512]{1,0:T(8,128)S(1)} %get-tuple-element.48), channel_id=1, source_target_pairs={{0,16},{16,32},{32,48},{48,0},{64,80},{80,96},{96,112},{112,64},{1... | collective-permute-start | bytes 786440 | tf_op jit(solution)/shard_map/ppermute | solution.py:35
  77.6 10.7 %collective-permute-start.14 = (f32[128,512]{1,0:T(8,128)}, f32[128,512]{1,0:T(8,128)S(1)}, u32[]{:S(2)}, u32[]{:S(2)}) collective-permute-start(f32[128,512]{1,0:T(8,128)} %shard_map.99), channel_id=1, source_target_pairs={{0,192},{16,208},{32,224},{48,240},{64,128},{80,144},{96,160},{112... | collective-permute-start | bytes 786440 | tf_op jit(solution)/shard_map/ppermute | solution.py:309
  80.7 3.4 %copy-start.11 = (f32[128,512]{1,0:T(8,128)}, f32[128,512]{1,0:T(8,128)S(1)}, u32[]{:S(2)}) copy-start(f32[128,512]{1,0:T(8,128)S(1)} %collective-permute-done.12.s3) | copy-start | bytes 786436
  81.3 2.8 %copy-start.12 = (f32[128,512]{1,0:T(8,128)}, f32[128,512]{1,0:T(8,128)S(1)}, u32[]{:S(2)}) copy-start(f32[128,512]{1,0:T(8,128)S(1)} %collective-permute-done.11.s2) | copy-start | bytes 786436
  91.1 9.9 %collective-permute-start.15 = (f32[128,512]{1,0:T(8,128)}, f32[128,512]{1,0:T(8,128)S(1)}, u32[]{:S(2)}, u32[]{:S(2)}) collective-permute-start(f32[128,512]{1,0:T(8,128)} %shard_map.100), channel_id=1, source_target_pairs={{0,64},{16,80},{32,96},{48,112},{64,0},{80,16},{96,32},{112,48},{1... | collective-permute-start | bytes 786440 | tf_op jit(solution)/shard_map/ppermute | solution.py:312
  108.1 4.2 %copy-start.21 = (f32[4,1,512]{2,1,0:T(1,128)S(1)}, f32[4,1,512]{2,1,0:T(1,128)}, u32[]{:S(2)}) copy-start(f32[4,1,512]{2,1,0:T(1,128)} %get-tuple-element.41.refs_0_) | copy-start | bytes 24580
  110.1 33.8 %collective-permute-start.18 = (f32[128,512]{1,0:T(8,128)S(1)}, f32[128,512]{1,0:T(8,128)S(1)}, u32[]{:S(2)}, u32[]{:S(2)}) collective-permute-start(f32[128,512]{1,0:T(8,128)S(1)} %get-tuple-element.42), channel_id=1, source_target_pairs={{0,48},{16,0},{32,16},{48,32},{64,112},{80,64},{96,80},{112,96},{1... | collective-permute-start | bytes 786440 | tf_op jit(solution)/shard_map/ppermute | solution.py:35
  110.1 36.6 %collective-permute-start.17 = (f32[128,512]{1,0:T(8,128)S(1)}, f32[128,512]{1,0:T(8,128)S(1)}, u32[]{:S(2)}, u32[]{:S(2)}) collective-permute-start(f32[128,512]{1,0:T(8,128)S(1)} %get-tuple-element.43), channel_id=1, source_target_pairs={{0,32},{16,48},{32,0},{48,16},{64,96},{80,112},{96,64},{112,80},{1... | collective-permute-start | bytes 786440 | tf_op jit(solution)/shard_map/ppermute | solution.py:35
  112.3 34.4 %collective-permute-start.16 = (f32[128,512]{1,0:T(8,128)S(1)}, f32[128,512]{1,0:T(8,128)S(1)}, u32[]{:S(2)}, u32[]{:S(2)}) collective-permute-start(f32[128,512]{1,0:T(8,128)S(1)} %get-tuple-element.44), channel_id=1, source_target_pairs={{0,16},{16,32},{32,48},{48,0},{64,80},{80,96},{96,112},{112,64},{1... | collective-permute-start | bytes 786440 | tf_op jit(solution)/shard_map/ppermute | solution.py:35
  112.3 7.3 %collective-permute-start.26 = (f32[4,1,512]{2,1,0:T(1,128)S(1)}, f32[4,1,512]{2,1,0:T(1,128)S(1)}, u32[]{:S(2)}, u32[]{:S(2)}) collective-permute-start(f32[4,1,512]{2,1,0:T(1,128)S(1)} %copy-done.21), channel_id=1, source_target_pairs={{0,7},{1,0},{2,1},{3,2},{4,3},{5,4},{6,5},{7,6},{8,15},{9,8},{10,9... | collective-permute-start | bytes 24584 | tf_op jit(solution)/shard_map/ppermute | solution.py:322
  118.1 4.5 %collective-permute-start.25 = (f32[4,1,512]{2,1,0:T(1,128)S(1)}, f32[4,1,512]{2,1,0:T(1,128)S(1)}, u32[]{:S(2)}, u32[]{:S(2)}) collective-permute-start(f32[4,1,512]{2,1,0:T(1,128)S(1)} %copy-done.21), channel_id=1, source_target_pairs={{0,6},{1,7},{2,0},{3,1},{4,2},{5,3},{6,4},{7,5},{8,14},{9,15},{10,... | collective-permute-start | bytes 24584 | tf_op jit(solution)/shard_map/ppermute | solution.py:322
  119.6 18.2 %copy-start.22 = (f32[4,1,512]{2,1,0:T(1,128)}, f32[4,1,512]{2,1,0:T(1,128)S(1)}, u32[]{:S(2)}) copy-start(f32[4,1,512]{2,1,0:T(1,128)S(1)} %collective-permute-done.26.refs_7_) | copy-start | bytes 24580
  119.6 5.5 %collective-permute-start.24 = (f32[4,1,512]{2,1,0:T(1,128)S(1)}, f32[4,1,512]{2,1,0:T(1,128)S(1)}, u32[]{:S(2)}, u32[]{:S(2)}) collective-permute-start(f32[4,1,512]{2,1,0:T(1,128)S(1)} %copy-done.21), channel_id=1, source_target_pairs={{0,5},{1,6},{2,7},{3,0},{4,1},{5,2},{6,3},{7,4},{8,13},{9,14},{10,... | collective-permute-start | bytes 24584 | tf_op jit(solution)/shard_map/ppermute | solution.py:322
  122.7 15.1 %copy-start.23 = (f32[4,1,512]{2,1,0:T(1,128)}, f32[4,1,512]{2,1,0:T(1,128)S(1)}, u32[]{:S(2)}) copy-start(f32[4,1,512]{2,1,0:T(1,128)S(1)} %collective-permute-done.25.refs_6_) | copy-start | bytes 24580
  122.7 7.6 %collective-permute-start.23 = (f32[4,1,512]{2,1,0:T(1,128)S(1)}, f32[4,1,512]{2,1,0:T(1,128)S(1)}, u32[]{:S(2)}, u32[]{:S(2)}) collective-permute-start(f32[4,1,512]{2,1,0:T(1,128)S(1)} %copy-done.21), channel_id=1, source_target_pairs={{0,4},{1,5},{2,6},{3,7},{4,0},{5,1},{6,2},{7,3},{8,12},{9,13},{10,... | collective-permute-start | bytes 24584 | tf_op jit(solution)/shard_map/ppermute | solution.py:322
  125.1 12.7 %copy-start.24 = (f32[4,1,512]{2,1,0:T(1,128)}, f32[4,1,512]{2,1,0:T(1,128)S(1)}, u32[]{:S(2)}) copy-start(f32[4,1,512]{2,1,0:T(1,128)S(1)} %collective-permute-done.24.refs_5_) | copy-start | bytes 24580
  125.1 7.9 %collective-permute-start.22 = (f32[4,1,512]{2,1,0:T(1,128)S(1)}, f32[4,1,512]{2,1,0:T(1,128)S(1)}, u32[]{:S(2)}, u32[]{:S(2)}) collective-permute-start(f32[4,1,512]{2,1,0:T(1,128)S(1)} %copy-done.21), channel_id=1, source_target_pairs={{0,3},{1,4},{2,5},{3,6},{4,7},{5,0},{6,1},{7,2},{8,11},{9,12},{10,... | collective-permute-start | bytes 24584 | tf_op jit(solution)/shard_map/ppermute | solution.py:322
  130.2 7.6 %copy-start.25 = (f32[4,1,512]{2,1,0:T(1,128)}, f32[4,1,512]{2,1,0:T(1,128)S(1)}, u32[]{:S(2)}) copy-start(f32[4,1,512]{2,1,0:T(1,128)S(1)} %collective-permute-done.23.refs_4_) | copy-start | bytes 24580
  130.2 5.8 %collective-permute-start.21 = (f32[4,1,512]{2,1,0:T(1,128)S(1)}, f32[4,1,512]{2,1,0:T(1,128)S(1)}, u32[]{:S(2)}, u32[]{:S(2)}) collective-permute-start(f32[4,1,512]{2,1,0:T(1,128)S(1)} %copy-done.21), channel_id=1, source_target_pairs={{0,2},{1,3},{2,4},{3,5},{4,6},{5,7},{6,0},{7,1},{8,10},{9,11},{10,... | collective-permute-start | bytes 24584 | tf_op jit(solution)/shard_map/ppermute | solution.py:322
  133.0 4.9 %copy-start.26 = (f32[4,1,512]{2,1,0:T(1,128)}, f32[4,1,512]{2,1,0:T(1,128)S(1)}, u32[]{:S(2)}) copy-start(f32[4,1,512]{2,1,0:T(1,128)S(1)} %collective-permute-done.22.refs_3_) | copy-start | bytes 24580
  133.0 4.9 %collective-permute-start.20 = (f32[4,1,512]{2,1,0:T(1,128)S(1)}, f32[4,1,512]{2,1,0:T(1,128)S(1)}, u32[]{:S(2)}, u32[]{:S(2)}) collective-permute-start(f32[4,1,512]{2,1,0:T(1,128)S(1)} %copy-done.21), channel_id=1, source_target_pairs={{0,1},{1,2},{2,3},{3,4},{4,5},{5,6},{6,7},{7,0},{8,9},{9,10},{10,1... | collective-permute-start | bytes 24584 | tf_op jit(solution)/shard_map/ppermute | solution.py:322
  136.0 1.8 %copy-start.27 = (f32[4,1,512]{2,1,0:T(1,128)}, f32[4,1,512]{2,1,0:T(1,128)S(1)}, u32[]{:S(2)}) copy-start(f32[4,1,512]{2,1,0:T(1,128)S(1)} %collective-permute-done.21.refs_2_) | copy-start | bytes 24580
  140.6 9.7 %collective-permute-start.27 = (f32[1,512]{1,0:T(1,128)S(1)}, f32[1,512]{1,0:T(1,128)S(1)}, u32[]{:S(2)}, u32[]{:S(2)}) collective-permute-start(f32[1,512]{1,0:T(1,128)S(1)} %get-tuple-element.58), channel_id=1, source_target_pairs={{0,16},{16,32},{32,48},{48,0},{64,80},{80,96},{96,112},{112,64},{1... | collective-permute-start | bytes 6152 | tf_op jit(solution)/shard_map/ppermute | solution.py:35
  141.9 8.4 %collective-permute-start.29 = (f32[1,512]{1,0:T(1,128)S(1)}, f32[1,512]{1,0:T(1,128)S(1)}, u32[]{:S(2)}, u32[]{:S(2)}) collective-permute-start(f32[1,512]{1,0:T(1,128)S(1)} %get-tuple-element.59), channel_id=1, source_target_pairs={{0,48},{16,0},{32,16},{48,32},{64,112},{80,64},{96,80},{112,96},{1... | collective-permute-start | bytes 6152 | tf_op jit(solution)/shard_map/ppermute | solution.py:35
  143.9 2.8 %copy-start.15 = (f32[128,512]{1,0:T(8,128)}, f32[128,512]{1,0:T(8,128)S(1)}, u32[]{:S(2)}) copy-start(f32[128,512]{1,0:T(8,128)S(1)} %collective-permute-done.18.r3) | copy-start | bytes 786436
  143.9 6.4 %collective-permute-start.28 = (f32[1,512]{1,0:T(1,128)S(1)}, f32[1,512]{1,0:T(1,128)S(1)}, u32[]{:S(2)}, u32[]{:S(2)}) collective-permute-start(f32[1,512]{1,0:T(1,128)S(1)} %get-tuple-element.60), channel_id=1, source_target_pairs={{0,32},{16,48},{32,0},{48,16},{64,96},{80,112},{96,64},{112,80},{1... | collective-permute-start | bytes 6152 | tf_op jit(solution)/shard_map/ppermute | solution.py:35
  150.2 2.5 %collective-permute-start.19 = (f32[32,512]{1,0:T(8,128)}, f32[32,512]{1,0:T(8,128)S(1)}, u32[]{:S(2)}, u32[]{:S(2)}) collective-permute-start(f32[32,512]{1,0:T(8,128)} %get-tuple-element.40), channel_id=1, source_target_pairs={{0,8},{8,0},{1,9},{9,1},{2,10},{10,2},{3,11},{11,3},{4,12},{12,4},... | collective-permute-start | bytes 196616 | tf_op jit(solution)/shard_map/ppermute | solution.py:329
  (11 other events, 8.5 us)

commit v2 on v1

v2 whole, which is shorter than its diff:
```python
import functools
import math

import jax
import jax.numpy as jnp
from jax import lax
from jax.experimental import pallas as pl
from jax.experimental.pallas import tpu as pltpu
from jax.sharding import PartitionSpec as P

K = 512
R = 512
FV = 32
ROW = 4
ROWS = 4
CH = R // ROW
BANDS = 8
SPARE = 8
F32 = jnp.float32
BF16 = jnp.bfloat16
NT = (((1,), (1,)), ((), ()))
NN = (((1,), (0,)), ((), ()))
PARAMS = pltpu.CompilerParams(vmem_limit_bytes=24 * 1024 * 1024)

X_RING = {
    d: [(ROW * y + x, ROW * y + (x + d) % ROW) for y in range(ROWS) for x in range(ROW)] for d in range(1, ROW)
}
SWAP = [1, 0, 3, 2]
TURN = [3, 2, 1, 0]
Y_SWAP = [(ROW * y + x, ROW * SWAP[y] + x) for y in range(ROWS) for x in range(ROW)]
Y_TURN = [(ROW * y + x, ROW * TURN[y] + x) for y in range(ROWS) for x in range(ROW)]
ROW_BANDS = [[(ROW * y + x) * BANDS + z for x in range(ROW) for z in range(BANDS)] for y in range(ROWS)]


def shift_x(value, by):
    return lax.ppermute(value, "sweep", X_RING[by % ROW])


def call(body, outs, *args, scratch=()):
    scalar = pl.BlockSpec(memory_space=pltpu.SMEM)
    vector = pl.BlockSpec(memory_space=pltpu.VMEM)
    return pl.pallas_call(
        body,
        out_shape=[jax.ShapeDtypeStruct(shape, dtype) for shape, dtype in outs],
        in_specs=[scalar if arg.ndim == 1 else vector for arg in args],
        out_specs=[vector] * len(outs),
        scratch_shapes=list(scratch),
        compiler_params=PARAMS,
    )(*args)


def place():
    at = lax.axis_index("sweep")
    return at % ROW, at // ROW


def split(value):
    high = value.astype(BF16)
    return high, (value - high.astype(F32)).astype(BF16)


def times(rows, high, low, dims):
    rows_high, rows_low = split(rows)
    count = rows.shape[0]
    both = lax.dot_general(
        jnp.concatenate([rows_high, rows_low], axis=0), high, dims, preferred_element_type=F32
    )
    cross = lax.dot_general(rows_high, low, dims, preferred_element_type=F32)
    return both[:count] + (both[count:] + cross)


def spread_body(coeff, table, source, response, before, after, sky, classes, blocked, f0, f1, f2, f3, s0, s1, s2, s3, sky_rays):
    x, y = place()
    upsun = y < 2
    density = jnp.zeros((1, K), F32)
    for at in range(table.shape[0]):
        density = jnp.where(classes[...] == at, table[at], density)
    transmit = (1 - blocked[...]).astype(F32) * jnp.exp(-coeff[0] * density)
    scale = 1.0 / math.sqrt(R)
    for dist, (first, second) in enumerate(((f0, s0), (f1, s1), (f2, s2), (f3, s3))):
        cols = pl.ds(pl.multiple_of((x + dist) % ROW * CH, CH), CH)
        weights = response[:, cols]
        up = jnp.concatenate([before[:, cols], weights[:-FV]], axis=0)
        down = jnp.concatenate([weights[FV:], after[:, cols]], axis=0)
        cotangent = ((0.5 * weights + 0.25 * (up + down)) * scale).T
        emitted = source[:, cols].T
        first[:CH] = jnp.where(upsun, emitted, cotangent)
        first[CH:] = jnp.broadcast_to(transmit, (SPARE, K))
        second[...] = jnp.where(upsun, cotangent, emitted)
    sky_rays[...] = sky[:, pl.ds(pl.multiple_of(x * CH, CH), CH)].T


def forward_chain(apply, thin, emitted, incoming, keep, first=0):
    def step(j, state):
        gained = apply(state, j, NT) * thin[j]
        state = gained + emitted[j]
        keep(j, gained, state)
        return state

    return lax.fori_loop(first, ROW, step, incoming)


def backward_chain(apply, thin, cotangent, incoming, keep, through):
    def step(i, state):
        j = ROW - 1 - i
        adjoint = cotangent[j] + state
        keep(j, adjoint)
        return apply(adjoint * thin[j], j, NN)

    state = lax.fori_loop(0, ROW - 1, step, incoming)
    adjoint = cotangent[0] + state
    keep(0, adjoint)
    if through:
        return apply(adjoint * thin[0], 0, NN)
    return None


def cut_body(left, right, e1, e2, e3, far_top, far_bottom):
    far_top[...] = left[:K // 2]
    far_bottom[...] = right[K // 2:]


def near_body(own, left, right, e0, e1, e2, e3, high, low, thin, given, pair_high, pair_low):
    x, y = place()
    for dist, part in enumerate((e0, e1, e2, e3)):
        tile = (x - dist + ROW) % ROW
        given[tile] = part[:CH]
        thin[tile] = part[CH:CH + 1]
    for dist, part in ((0, own), (1, left), (3, right)):
        tile = (x - dist + ROW) % ROW
        high[tile], low[tile] = split(part[...])

    @pl.when((y == 1) | (y == 2))
    def _():
        base = jnp.where(x < 2, 0, 2)
        rows = (high[base + 1].astype(F32) + low[base + 1].astype(F32)) * thin[base]
        pair_high[...], pair_low[...] = split(times(rows, high[base], low[base], NN))


def start_body(high, low, far_top, far_bottom, thin, given, pair_high, pair_low, sky_rays,
               far_high, far_low, saved, radiance, whole_high, whole_low, out, far_pair):
    x, y = place()
    far = (x + 2) % ROW
    far_high[:K // 2], far_low[:K // 2] = split(far_top[...])
    far_high[K // 2:], far_low[K // 2:] = split(far_bottom[...])

    def apply(rows, j, dims):
        return lax.cond(
            j == far,
            lambda: times(rows, far_high[...], far_low[...], dims),
            lambda: times(rows, high[j], low[j], dims),
        )

    @pl.when(y == 0)
    def _():
        def keep(j, gained, state):
            saved[j] = gained
            radiance[j] = state

        out[...] = forward_chain(apply, thin, given, sky_rays[...], keep)

    @pl.when(y == ROWS - 1)
    def _():
        def keep(j, adjoint):
            saved[j] = adjoint

        out[...] = backward_chain(apply, thin, given, jnp.zeros((CH, K), F32), keep, True)

    inner = (y == 1) | (y == 2)

    @pl.when(inner & (x % 2 == 0))
    def _():
        rows = (high[far + 1].astype(F32) + low[far + 1].astype(F32)) * thin[far]
        far_pair[...] = times(rows, far_high[...], far_low[...], NN)

    @pl.when(inner & (x % 2 == 1))
    def _():
        rows = (far_high[...].astype(F32) + far_low[...].astype(F32)) * thin[far - 1]
        far_pair[...] = times(rows, high[far - 1], low[far - 1], NN)

    @pl.when(inner & (x < 2))
    def _():
        whole = times(far_pair[...] * thin[1], pair_high[...], pair_low[...], NN)
        whole_high[...], whole_low[...] = split(whole)

    @pl.when(inner & (x >= 2))
    def _():
        rows = (pair_high[...].astype(F32) + pair_low[...].astype(F32)) * thin[1]
        first_high, first_low = split(far_pair[...])
        whole_high[...], whole_low[...] = split(times(rows, first_high, first_low, NN))


def held_at(high, low):
    return lambda rows, j, dims: times(rows, high[j], low[j], dims)


def ends(high, low, thin, given, y, forward_row, out):
    @pl.when(y == forward_row)
    def _():
        out[...] = forward_chain(held_at(high, low), thin, given, given[0], lambda j, g, s: None, 1)

    @pl.when(y == ROWS - 1 - forward_row)
    def _():
        out[...] = backward_chain(held_at(high, low), thin, given, jnp.zeros((CH, K), F32), lambda j, a: None, True)


def ends_body(near_high, near_low, far_high, far_low, thin, given, high, low, added):
    far = (place()[0] + 2) % ROW
    for j in range(ROW):
        @pl.when(j == far)
        def _():
            high[j] = far_high[...]
            low[j] = far_low[...]

        @pl.when(j != far)
        def _():
            high[j] = near_high[j]
            low[j] = near_low[j]

    ends(high, low, thin, given, place()[1], 1, added)


def later_body(high, low, thin, s0, s1, s2, s3, given, added):
    x, y = place()
    for dist, part in enumerate((s0, s1, s2, s3)):
        given[(x - dist + ROW) % ROW] = part[...]
    ends(high, low, thin, given, y, 2, added)


def pass_body(forward_row, incoming, whole_high, whole_low, thin, added, out):
    _, y = place()

    @pl.when(y == forward_row)
    def _():
        out[...] = times(incoming[...], whole_high[...], whole_low[...], NT) * thin[ROW - 1] + added[...]

    @pl.when(y == ROWS - 1 - forward_row)
    def _():
        out[...] = times(incoming[...] * thin[ROW - 1], whole_high[...], whole_low[...], NN) + added[...]


def middle_body(high, low, thin, given, later, first_in, second_in, radiance, along, saved):
    _, y = place()
    for row, emitted, cotangent, state, adjoint_in in (
        (1, given, later, first_in, second_in),
        (2, later, given, second_in, first_in),
    ):
        @pl.when(y == row)
        def _():
            def keep_state(j, gained, new_state):
                saved[j] = gained
                radiance[j] = new_state

            def keep_adjoint(j, adjoint):
                along[j] = jnp.sum(adjoint * saved[j], axis=0, keepdims=True)

            forward_chain(held_at(high, low), thin, emitted, state[...], keep_state)
            backward_chain(held_at(high, low), thin, cotangent, adjoint_in[...], keep_adjoint, False)


def last_body(high, low, thin, later, last_in, early, middle, gain, x0, x1, x2, x3, held):
    x, y = place()
    outs = (x0, x1, x2, x3)

    @pl.when(y == ROWS - 1)
    def _():
        def keep(j, gained, state):
            gain[j] = gained
            held[j] = state

        forward_chain(held_at(high, low), thin, later, last_in[...], keep)
        for dist, out in enumerate(outs):
            out[...] = held[(x + dist) % ROW]

    @pl.when(y == 0)
    def _():
        for dist, out in enumerate(outs):
            out[...] = early[(x + dist) % ROW]

    @pl.when((y == 1) | (y == 2))
    def _():
        for dist, out in enumerate(outs):
            out[...] = middle[(x + dist) % ROW]


def along_body(coeff, high, low, thin, later, last_in, saved, gain, middle_along, out, along):
    x, y = place()
    factor = -coeff[0]

    @pl.when(y == 0)
    def _():
        def keep(j, adjoint):
            along[j] = jnp.sum(adjoint * saved[j], axis=0, keepdims=True)

        backward_chain(held_at(high, low), thin, later, last_in[...], keep, False)

    @pl.when(y == ROWS - 1)
    def _():
        for j in range(ROW):
            along[j] = jnp.sum(gain[j] * saved[j], axis=0, keepdims=True)

    @pl.when((y == 1) | (y == 2))
    def _():
        for j in range(ROW):
            along[j] = middle_along[j]

    for j in range(ROW):
        out[j * BANDS:(j + 1) * BANDS] = jnp.broadcast_to((factor * along[j])[None], (BANDS, 1, K))


def rim_body(r0, r1, r2, r3, edge):
    x, _ = place()
    low_side = lax.axis_index("cross") == 0
    for dist, part in enumerate((r0, r1, r2, r3)):
        cols = pl.ds(pl.multiple_of((x - dist + ROW) % ROW * CH, CH), CH)
        edge[:, cols] = jnp.where(low_side, part[:, K - FV:], part[:, :FV]).T


def turn_body(r0, r1, r2, r3, out):
    x, _ = place()
    for dist, part in enumerate((r0, r1, r2, r3)):
        cols = pl.ds(pl.multiple_of((x - dist + ROW) % ROW * CH, CH), CH)
        out[:, cols] = part[...].T


def smooth_body(grid, edge, out, done):
    low_side = lax.axis_index("cross") == 0
    whole = grid[...]
    halo = edge[...]
    up = jnp.concatenate([jnp.where(low_side, 0.0, halo), whole[:-FV]], axis=0)
    down = jnp.concatenate([whole[FV:], jnp.where(low_side, halo, 0.0)], axis=0)
    out[...] = 0.5 * whole + 0.25 * (up + down)
    done[...] = halo[:8, :128]


def total_body(lines, done, out):
    out[...] = jnp.sum(lines[...], axis=0)


def per_device(operator, source, sky, response, extinction, leaf_density, leaf_class, occupied):
    local = operator[0, 0]
    weights = response[0, 0]
    side = lax.axis_index("cross")
    other_side = [(0, 1), (1, 0)]

    left = shift_x(local, 1)
    right = shift_x(local, -1)

    edge = lax.ppermute(jnp.where(side == 0, weights[-FV:], weights[:FV]), "cross", other_side)
    before = jnp.where(side == 1, edge, 0.0)
    after = jnp.where(side == 0, edge, 0.0)
    part = ((CH, K), F32)
    chunk = ((ROW, CH, K), F32)
    line = ((ROW, 1, K), F32)
    first = ((CH + SPARE, K), F32)
    f0, f1, f2, f3, s0, s1, s2, s3, sky_rays = call(
        spread_body, [first] * ROW + [part] * (ROW + 1),
        extinction, leaf_density, source[0, 0], weights, before, after, sky[0], leaf_class, occupied)
    e0, e1, e2, e3 = f0, shift_x(f1, 1), shift_x(f2, 2), shift_x(f3, 3)
    half = ((K // 2, K), F32)
    operators = ((ROW, K, K), BF16)
    whole = ((K, K), BF16)
    far_top, far_bottom = call(cut_body, [half, half], left, right, e1, e2, e3)
    far_top = shift_x(far_top, 1)
    far_bottom = shift_x(far_bottom, -1)
    near_high, near_low, thin, given, pair_high, pair_low = call(
        near_body, [operators, operators, line, chunk, whole, whole], local, left, right, e0, e1, e2, e3)
    far_high, far_low, saved, early, whole_high, whole_low, out = call(
        start_body, [whole, whole, chunk, chunk, whole, whole, part],
        near_high, near_low, far_top, far_bottom, thin, given, pair_high, pair_low, sky_rays,
        scratch=[pltpu.VMEM((K, K), F32)])
    first_in = lax.ppermute(out, "sweep", Y_SWAP)
    s1, s2, s3 = shift_x(s1, 1), shift_x(s2, 2), shift_x(s3, 3)
    high, low, added = call(
        ends_body, [operators, operators, part], near_high, near_low, far_high, far_low, thin, given)
    (out,) = call(functools.partial(pass_body, 1), [part], first_in, whole_high, whole_low, thin, added)
    second_in = lax.ppermute(out, "sweep", Y_TURN)
    later, added = call(later_body, [chunk, part], high, low, thin, s0, s1, s2, s3)
    (out,) = call(functools.partial(pass_body, 2), [part], second_in, whole_high, whole_low, thin, added)
    last_in = lax.ppermute(out, "sweep", Y_SWAP)
    held = pltpu.VMEM((ROW, CH, K), F32)
    middle, middle_along = call(
        middle_body, [chunk, line], high, low, thin, given, later, first_in, second_in, scratch=[held])
    gain, x0, x1, x2, x3 = call(
        last_body, [chunk] + [part] * ROW, high, low, thin, later, last_in, early, middle, scratch=[held])
    r0, r1, r2, r3 = x0, shift_x(x1, 1), shift_x(x2, 2), shift_x(x3, 3)
    (lines,) = call(
        along_body, [((ROW * BANDS, 1, K), F32)], extinction, high, low, thin, later, last_in, saved, gain, middle_along,
        scratch=[pltpu.VMEM((ROW, 1, K), F32)])
    lines = lax.all_to_all(lines, ("sweep", "band"), 0, 0, axis_index_groups=ROW_BANDS)

    (edge,) = call(rim_body, [((FV, R), F32)], r0, r1, r2, r3)
    edge = lax.ppermute(edge, "cross", other_side)
    (grid,) = call(turn_body, [((K, R), F32)], r0, r1, r2, r3)
    observed, done = call(smooth_body, [((K, R), F32), ((8, 128), F32)], grid, edge)
    (total,) = call(total_body, [((1, K), F32)], lines, done)
    return (observed[None, None], total)


def solution(mesh):
    in_specs = (
        P("band", "sweep", "cross", None),
        P("band", "sweep", "cross", None),
        P("band", "cross", None),
        P("band", "sweep", "cross", None),
        P("band"),
        P(),
        P("sweep", "cross"),
        P("sweep", "cross"),
    )
    out_specs = (P("band", "sweep", "cross", None), P("sweep", "cross"))
    return jax.shard_map(
        per_device, mesh=mesh, in_specs=in_specs, out_specs=out_specs, check_vma=False
    )
```

time: 156 us -> 106 us (0.68)
  Pallas kernels: 37.6 us -> 9.47 us
  starting transfers between devices: 49.5 us -> 34.7 us
  local copies, waits for them, and re-layouts: 13.2 us -> 5.69 us
  waiting for transfers between devices: 46.3 us -> 53.3 us
  other arithmetic: 6.51 us -> 0.89 us
    pallas_call x10 -> x15, Pallas kernels: 37.6 us -> 9.47 us  [call(): pl.pallas_call(body, out_shape=[jax.ShapeDtypeStruct(shape, dtype) for sh...]
    ppermute x7 -> x0, starting transfers between devices: 19.8 us -> none  [per_device(): lax.ppermute(along, 'band', [(i, (i + d) % BANDS) for i in range(BANDS)])]
    all_to_all x0 -> x1, starting transfers between devices: none -> 10.2 us  [per_device(): lax.all_to_all(lines, ('sweep', 'band'), 0, 0, axis_index_groups=ROW_BANDS)]
    all_to_all x0 -> x1, waiting for transfers between devices: none -> 7.14 us  [per_device(): lax.all_to_all(lines, ('sweep', 'band'), 0, 0, axis_index_groups=ROW_BANDS)]
    ppermute x18 -> x13, starting transfers between devices: 25.7 us -> 19.9 us  [shift_x(): return lax.ppermute(value, 'sweep', X_RING[by % ROW])]
    ppermute x7 -> x0, waiting for transfers between devices: 5.7 us -> none  [per_device(): lax.ppermute(along, 'band', [(i, (i + d) % BANDS) for i in range(BANDS)])]
    squeeze x4 -> x0, local copies, waits for them, and re-layouts: 5.42 us -> none  [the longest x1 2 us: per_device(): r1, r2, r3 = (shift_x(rays[d], d) for d in (1, 2, 3))]
    unnamed x59 -> x14, local copies, waits for them, and re-layouts: 7.68 us -> 5.69 us
  transfers between devices with their start and end apart: 30 -> 19, of which waited for: 11 -> 10; matrix products, arithmetic and copies ran while one was open for 6% -> 1% of each run, Pallas kernels for 14% -> 4%
where the time goes in v2:
time: 106 us; the launch traced here: 105 us
  waiting for transfers between devices  53.3 us (50%)
  starting transfers between devices  34.7 us (33%)
  Pallas kernels  9.47 us (9%)
  local copies, waits for them, and re-layouts  5.69 us (5%)
  between operations  1.45 us (1%)
    ppermute x13, waiting for transfers between devices, shift_x(): return lax.ppermute(value, 'sweep', X_RING[by % ROW])  39.2 us
    ppermute x13, starting transfers between devices, shift_x(): return lax.ppermute(value, 'sweep', X_RING[by % ROW])  19.9 us
    all_to_all x1, starting transfers between devices, per_device(): lax.all_to_all(lines, ('sweep', 'band'), 0, 0, axis_index_groups=ROW_BANDS)  10.2 us
    pallas_call x15, Pallas kernels, call(): pl.pallas_call(body, out_shape=[jax.ShapeDtypeStruct(shape, dtype) for sh...  9.47 us
    all_to_all x1, waiting for transfers between devices, per_device(): lax.all_to_all(lines, ('sweep', 'band'), 0, 0, axis_index_groups=ROW_BANDS)  7.14 us
    unnamed x14, local copies, waits for them, and re-layouts  5.69 us
    ppermute x1, waiting for transfers between devices, per_device(): last_in = lax.ppermute(out, 'sweep', Y_SWAP)  4.35 us
    ppermute x1, starting transfers between devices, per_device(): last_in = lax.ppermute(out, 'sweep', Y_SWAP)  2.63 us
  transfers between devices with their start and end apart: 19, of which 10 were waited for; matrix products, arithmetic and copies ran while one was open for 1% of the time, Pallas kernels for 4%

profile of v2, /device:TPU:24, one launch (start us, length us, event | category | flops | bytes accessed | tf_op | source)
XLA Modules:
  0.0 105.4 jit_solution(16888240920325791349)
XLA Ops:
  0.6 2.8 %collective-permute-start.1 = (f32[512,512]{1,0:T(8,128)}, f32[512,512]{1,0:T(8,128)S(1)}, u32[]{:S(2)}, u32[]{:S(2)}) collective-permute-start(f32[512,512]{1,0:T(8,128)} %bitcast.10), channel_id=1, source_target_pairs={{0,48},{16,0},{32,16},{48,32},{64,112},{80,64},{96,80},{112,96},{1... | collective-permute-start | bytes 3145736 | tf_op jit(solution)/shard_map/ppermute | solution.py:36
  3.5 0.9 select_bitcast_fusion
  4.4 0.1 collective-permute-start.2
  5.1 0.6 collective-permute-done.2
  5.7 0.0 copy-start
  5.7 1.2 %copy-done = f32[1,1,512,512]{3,2,1,0:T(8,128)S(1)} copy-done((f32[1,1,512,512]{3,2,1,0:T(8,128)S(1)}, f32[1,1,512,512]{3,2,1,0:T(8,128)}, u32[]{:S(2)}) %copy-start) | copy-done | bytes 1048600
  6.9 1.2 %copy-done.1 = f32[1,1,512,512]{3,2,1,0:T(8,128)S(1)} copy-done((f32[1,1,512,512]{3,2,1,0:T(8,128)S(1)}, f32[1,1,512,512]{3,2,1,0:T(8,128)}, u32[]{:S(2)}) %copy-start.1) | copy-done | bytes 1048600
  8.2 1.2 %copy-done.2 = f32[1,512,512]{2,1,0:T(8,128)S(1)} copy-done((f32[1,512,512]{2,1,0:T(8,128)S(1)}, f32[1,512,512]{2,1,0:T(8,128)}, u32[]{:S(2)}) %copy-start.2) | copy-done | bytes 1048600
  9.4 0.7 copy-done.4
  10.1 0.7 copy-done.5
  10.8 0.7 copy-done.6
  11.4 1.2 %shard_map.95 = (f32[136,512]{1,0:T(8,128)S(1)}, f32[136,512]{1,0:T(8,128)S(1)}, f32[136,512]{1,0:T(8,128)S(1)}, f32[136,512]{1,0:T(8,128)S(1)}, f32[128,512]{1,...) custom-call(f32[1]{0:T(128)S(6)} %copy.10.coeff, ...), custom_call_target="tpu_custom_call" | custom-call | tf_op jit(solution)/shard_map/pallas_call | solution.py:42
  12.7 0.0 copy-start.3
  12.7 0.8 collective-permute-start.3
  13.5 3.9 %collective-permute-start.4 = (f32[136,512]{1,0:T(8,128)S(1)}, f32[136,512]{1,0:T(8,128)S(1)}, u32[]{:S(2)}, u32[]{:S(2)}) collective-permute-start(f32[136,512]{1,0:T(8,128)S(1)} %get-tuple-element.42), channel_id=1, source_target_pairs={{0,32},{16,48},{32,0},{48,16},{64,96},{80,112},{96,64},{112,80},{1... | collective-permute-start | bytes 835592 | tf_op jit(solution)/shard_map/ppermute | solution.py:36
  17.4 0.2 collective-permute-start.5
  17.7 23.8 %collective-permute-done.3.e1 = f32[136,512]{1,0:T(8,128)S(1)} collective-permute-done((f32[136,512]{1,0:T(8,128)S(1)}, f32[136,512]{1,0:T(8,128)S(1)}, u32[]{:S(2)}, u32[]{:S(2)}) %collective-permute-start.3) | collective-permute-done | bytes 278560 | tf_op jit(solution)/shard_map/ppermute | solution.py:36
  41.5 0.1 shard_map.97
  41.5 0.1 collective-permute-start.6
  41.6 3.2 %collective-permute-start.7 = (f32[256,512]{1,0:T(8,128)S(1)}, f32[256,512]{1,0:T(8,128)S(1)}, u32[]{:S(2)}, u32[]{:S(2)}) collective-permute-start(f32[256,512]{1,0:T(8,128)S(1)} %get-tuple-element.47), channel_id=1, source_target_pairs={{0,48},{16,0},{32,16},{48,32},{64,112},{80,64},{96,80},{112,96},{1... | collective-permute-start | bytes 1572872 | tf_op jit(solution)/shard_map/ppermute | solution.py:36
  44.9 0.5 shard_map.96
  45.4 9.0 %collective-permute-done.6.far_top = f32[256,512]{1,0:T(8,128)S(1)} collective-permute-done((f32[256,512]{1,0:T(8,128)S(1)}, f32[256,512]{1,0:T(8,128)S(1)}, u32[]{:S(2)}, u32[]{:S(2)}) %collective-permute-start.6) | collective-permute-done | bytes 524320 | tf_op jit(solution)/shard_map/ppermute | solution.py:36
  54.4 2.1 %shard_map.98 = (bf16[512,512]{1,0:T(8,128)(2,1)S(1)}, bf16[512,512]{1,0:T(8,128)(2,1)S(1)}, f32[4,128,512]{2,1,0:T(8,128)S(1)}, f32[4,128,512]{2,1,0:T(8,128)S(...) custom-call(bf16[4,512,512]{2,1,0:T(8,128)(2,1)S(1)} %get-tuple-element.44.high.near_high, ...), custom_call_target="tpu_custom_call" | custom-call | tf_op jit(solution)/shard_map/pallas_call | solution.py:42
  56.5 1.0 collective-permute-start.11
  57.6 0.3 collective-permute-start.8
  57.9 4.1 %collective-permute-start.9 = (f32[128,512]{1,0:T(8,128)S(1)}, f32[128,512]{1,0:T(8,128)S(1)}, u32[]{:S(2)}, u32[]{:S(2)}) collective-permute-start(f32[128,512]{1,0:T(8,128)S(1)} %get-tuple-element.59), channel_id=1, source_target_pairs={{0,32},{16,48},{32,0},{48,16},{64,96},{80,112},{96,64},{112,80},{1... | collective-permute-start | bytes 786440 | tf_op jit(solution)/shard_map/ppermute | solution.py:36
  62.0 0.3 shard_map.99
  62.3 0.7 collective-permute-done.11.incoming.first_in
  63.0 0.7 collective-permute-start.12
  63.7 3.5 %collective-permute-done.8.s1 = f32[128,512]{1,0:T(8,128)S(1)} collective-permute-done((f32[128,512]{1,0:T(8,128)S(1)}, f32[128,512]{1,0:T(8,128)S(1)}, u32[]{:S(2)}, u32[]{:S(2)}) %collective-permute-start.8) | collective-permute-done | bytes 262176 | tf_op jit(solution)/shard_map/ppermute | solution.py:36
  67.3 2.8 %collective-permute-done.9.s2 = f32[128,512]{1,0:T(8,128)S(1)} collective-permute-done((f32[128,512]{1,0:T(8,128)S(1)}, f32[128,512]{1,0:T(8,128)S(1)}, u32[]{:S(2)}, u32[]{:S(2)}) %collective-permute-start.9) | collective-permute-done | bytes 262176 | tf_op jit(solution)/shard_map/ppermute | solution.py:36
  70.1 0.1 shard_map.100
  70.2 0.4 collective-permute-done.12.incoming.second_in
  70.6 2.6 %collective-permute-start.13 = (f32[128,512]{1,0:T(8,128)S(1)}, f32[128,512]{1,0:T(8,128)S(1)}, u32[]{:S(2)}, u32[]{:S(2)}) collective-permute-start(f32[128,512]{1,0:T(8,128)S(1)} %shard_map.102), channel_id=1, source_target_pairs={{0,64},{16,80},{32,96},{48,112},{64,0},{80,16},{96,32},{112,48},{1... | collective-permute-start | bytes 786440 | tf_op jit(solution)/shard_map/ppermute | solution.py:380
  73.2 4.4 %collective-permute-done.13.last_in = f32[128,512]{1,0:T(8,128)S(1)} collective-permute-done((f32[128,512]{1,0:T(8,128)S(1)}, f32[128,512]{1,0:T(8,128)S(1)}, u32[]{:S(2)}, u32[]{:S(2)}) %collective-permute-start.13) | collective-permute-done | bytes 262176 | tf_op jit(solution)/shard_map/ppermute | solution.py:380
  77.6 1.9 %shard_map.104 = (f32[4,128,512]{2,1,0:T(8,128)S(1)}, f32[128,512]{1,0:T(8,128)S(1)}, f32[128,512]{1,0:T(8,128)S(1)}, f32[128,512]{1,0:T(8,128)S(1)}, f32[128,512]{1,0:T(8,128)S(1)}) custom-call(bf16[4,512,512]{2,1,0:T(8,128)(2,1)S(1)} %get-tuple-element.55.high, bf16[4,512,512]{2,1,0:T(8,128)(2,1)S(1)} %get-tuple-element.56.low, ...), custom_call_target="tpu_custom_call" | custom-call | tf_op jit(solution)/shard_map/pallas_call | solution.py:42
  79.5 1.2 %collective-permute-start.14 = (f32[128,512]{1,0:T(8,128)S(1)}, f32[128,512]{1,0:T(8,128)S(1)}, u32[]{:S(2)}, u32[]{:S(2)}) collective-permute-start(f32[128,512]{1,0:T(8,128)S(1)} %get-tuple-element.70), channel_id=1, source_target_pairs={{0,16},{16,32},{32,48},{48,0},{64,80},{80,96},{96,112},{112,64},{1... | collective-permute-start | bytes 786440 | tf_op jit(solution)/shard_map/ppermute | solution.py:36
  80.7 2.7 %collective-permute-start.15 = (f32[128,512]{1,0:T(8,128)S(1)}, f32[128,512]{1,0:T(8,128)S(1)}, u32[]{:S(2)}, u32[]{:S(2)}) collective-permute-start(f32[128,512]{1,0:T(8,128)S(1)} %get-tuple-element.71), channel_id=1, source_target_pairs={{0,32},{16,48},{32,0},{48,16},{64,96},{80,112},{96,64},{112,80},{1... | collective-permute-start | bytes 786440 | tf_op jit(solution)/shard_map/ppermute | solution.py:36
  83.4 0.4 collective-permute-start.16
  83.8 0.8 shard_map.108
  84.6 10.2 %all-to-all-start = ((f32[32,1,512]{2,1,0:T(1,128)}), f32[32,1,512]{2,1,0:T(1,128)S(1)}, u32[]{:S(2)}, u32[]{:S(2)}) async-start(f32[32,1,512]{2,1,0:T(1,128)} %shard_map.108), calls=%async_computation | async-start | bytes 131072 | tf_op jit(solution)/shard_map/all_to_all | solution.py:390
  94.8 0.4 shard_map.106
  95.2 0.1 collective-permute-start.17
  95.3 0.3 shard_map.105.grid
  95.6 0.9 collective-permute-done.17.edge
  96.5 1.1 %shard_map.107 = (f32[512,512]{1,0:T(8,128)}, f32[8,128]{1,0:T(8,128)S(1)}) custom-call(f32[512,512]{1,0:T(8,128)S(1)} %shard_map.105.grid, f32[32,512]{1,0:T(8,128)S(1)} %collective-permute-done.17.edge), custom_call_target="tpu_custom_call" | custom-call | tf_op jit(solution)/shard_map/pallas_call | solution.py:42
  97.7 7.1 %all-to-all-done.lines = f32[32,1,512]{2,1,0:T(1,128)S(1)} async-done(((f32[32,1,512]{2,1,0:T(1,128)}), f32[32,1,512]{2,1,0:T(1,128)S(1)}, u32[]{:S(2)}, u32[]{:S(2)}) %all-to-all-start) | async-done | bytes 65568 | tf_op jit(solution)/shard_map/all_to_all | solution.py:390
  104.8 0.6 shard_map.109
  (21 shorter events, 0.1 us)
Async XLA Ops:
  0.6 40.8 %collective-permute-start.1 = (f32[512,512]{1,0:T(8,128)}, f32[512,512]{1,0:T(8,128)S(1)}, u32[]{:S(2)}, u32[]{:S(2)}) collective-permute-start(f32[512,512]{1,0:T(8,128)} %bitcast.10), channel_id=1, source_target_pairs={{0,48},{16,0},{32,16},{48,32},{64,112},{80,64},{96,80},{112,96},{1... | collective-permute-start | bytes 3145736 | tf_op jit(solution)/shard_map/ppermute | solution.py:36
  3.5 38.0 %collective-permute-start = (f32[512,512]{1,0:T(8,128)}, f32[512,512]{1,0:T(8,128)S(1)}, u32[]{:S(2)}, u32[]{:S(2)}) collective-permute-start(f32[512,512]{1,0:T(8,128)} %bitcast.11), channel_id=1, source_target_pairs={{0,16},{16,32},{32,48},{48,0},{64,80},{80,96},{96,112},{112,64},{1... | collective-permute-start | bytes 3145736 | tf_op jit(solution)/shard_map/ppermute | solution.py:36
  4.4 1.3 %collective-permute-start.2 = (f32[32,512]{1,0:T(8,128)S(1)}, f32[32,512]{1,0:T(8,128)S(1)}, u32[]{:S(2)}, u32[]{:S(2)}) collective-permute-start(f32[32,512]{1,0:T(8,128)S(1)} %select_bitcast_fusion), channel_id=1, source_target_pairs={{0,8},{8,0},{1,9},{9,1},{2,10},{10,2},{3,11},{11,3},{4,12},{12,4},... | collective-permute-start | bytes 196616 | tf_op jit(solution)/shard_map/ppermute | solution.py:349
  5.7 1.2 %copy-start = (f32[1,1,512,512]{3,2,1,0:T(8,128)S(1)}, f32[1,1,512,512]{3,2,1,0:T(8,128)}, u32[]{:S(2)}) copy-start(f32[1,1,512,512]{3,2,1,0:T(8,128)} %param.11) | copy-start | bytes 3145732
  6.9 1.2 %copy-start.1 = (f32[1,1,512,512]{3,2,1,0:T(8,128)S(1)}, f32[1,1,512,512]{3,2,1,0:T(8,128)}, u32[]{:S(2)}) copy-start(f32[1,1,512,512]{3,2,1,0:T(8,128)} %param.9) | copy-start | bytes 3145732
  8.2 1.2 %copy-start.2 = (f32[1,512,512]{2,1,0:T(8,128)S(1)}, f32[1,512,512]{2,1,0:T(8,128)}, u32[]{:S(2)}) copy-start(f32[1,512,512]{2,1,0:T(8,128)} %param.10) | copy-start | bytes 3145732
  9.4 0.7 copy-start.4
  10.1 0.7 copy-start.5
  10.8 0.7 copy-start.6
  12.7 32.2 %copy-start.3 = (f32[1,1,512,512]{3,2,1,0:T(8,128)S(1)}, f32[1,1,512,512]{3,2,1,0:T(8,128)}, u32[]{:S(2)}) copy-start(f32[1,1,512,512]{3,2,1,0:T(8,128)} %param.8) | copy-start | bytes 3145732
  12.7 28.8 %collective-permute-start.3 = (f32[136,512]{1,0:T(8,128)S(1)}, f32[136,512]{1,0:T(8,128)S(1)}, u32[]{:S(2)}, u32[]{:S(2)}) collective-permute-start(f32[136,512]{1,0:T(8,128)S(1)} %get-tuple-element.41), channel_id=1, source_target_pairs={{0,16},{16,32},{32,48},{48,0},{64,80},{80,96},{96,112},{112,64},{1... | collective-permute-start | bytes 835592 | tf_op jit(solution)/shard_map/ppermute | solution.py:36
  13.5 27.9 %collective-permute-start.4 = (f32[136,512]{1,0:T(8,128)S(1)}, f32[136,512]{1,0:T(8,128)S(1)}, u32[]{:S(2)}, u32[]{:S(2)}) collective-permute-start(f32[136,512]{1,0:T(8,128)S(1)} %get-tuple-element.42), channel_id=1, source_target_pairs={{0,32},{16,48},{32,0},{48,16},{64,96},{80,112},{96,64},{112,80},{1... | collective-permute-start | bytes 835592 | tf_op jit(solution)/shard_map/ppermute | solution.py:36
  17.4 24.0 %collective-permute-start.5 = (f32[136,512]{1,0:T(8,128)S(1)}, f32[136,512]{1,0:T(8,128)S(1)}, u32[]{:S(2)}, u32[]{:S(2)}) collective-permute-start(f32[136,512]{1,0:T(8,128)S(1)} %get-tuple-element.43), channel_id=1, source_target_pairs={{0,48},{16,0},{32,16},{48,32},{64,112},{80,64},{96,80},{112,96},{1... | collective-permute-start | bytes 835592 | tf_op jit(solution)/shard_map/ppermute | solution.py:36
  41.5 12.9 %collective-permute-start.6 = (f32[256,512]{1,0:T(8,128)S(1)}, f32[256,512]{1,0:T(8,128)S(1)}, u32[]{:S(2)}, u32[]{:S(2)}) collective-permute-start(f32[256,512]{1,0:T(8,128)S(1)} %get-tuple-element.46), channel_id=1, source_target_pairs={{0,16},{16,32},{32,48},{48,0},{64,80},{80,96},{96,112},{112,64},{1... | collective-permute-start | bytes 1572872 | tf_op jit(solution)/shard_map/ppermute | solution.py:36
  41.6 12.8 %collective-permute-start.7 = (f32[256,512]{1,0:T(8,128)S(1)}, f32[256,512]{1,0:T(8,128)S(1)}, u32[]{:S(2)}, u32[]{:S(2)}) collective-permute-start(f32[256,512]{1,0:T(8,128)S(1)} %get-tuple-element.47), channel_id=1, source_target_pairs={{0,48},{16,0},{32,16},{48,32},{64,112},{80,64},{96,80},{112,96},{1... | collective-permute-start | bytes 1572872 | tf_op jit(solution)/shard_map/ppermute | solution.py:36
  56.5 6.5 %collective-permute-start.11 = (f32[128,512]{1,0:T(8,128)S(1)}, f32[128,512]{1,0:T(8,128)S(1)}, u32[]{:S(2)}, u32[]{:S(2)}) collective-permute-start(f32[128,512]{1,0:T(8,128)S(1)} %get-tuple-element.62), channel_id=1, source_target_pairs={{0,64},{16,80},{32,96},{48,112},{64,0},{80,16},{96,32},{112,48},{1... | collective-permute-start | bytes 786440 | tf_op jit(solution)/shard_map/ppermute | solution.py:372
  57.6 9.7 %collective-permute-start.8 = (f32[128,512]{1,0:T(8,128)S(1)}, f32[128,512]{1,0:T(8,128)S(1)}, u32[]{:S(2)}, u32[]{:S(2)}) collective-permute-start(f32[128,512]{1,0:T(8,128)S(1)} %get-tuple-element.58), channel_id=1, source_target_pairs={{0,16},{16,32},{32,48},{48,0},{64,80},{80,96},{96,112},{112,64},{1... | collective-permute-start | bytes 786440 | tf_op jit(solution)/shard_map/ppermute | solution.py:36
  57.9 12.2 %collective-permute-start.9 = (f32[128,512]{1,0:T(8,128)S(1)}, f32[128,512]{1,0:T(8,128)S(1)}, u32[]{:S(2)}, u32[]{:S(2)}) collective-permute-start(f32[128,512]{1,0:T(8,128)S(1)} %get-tuple-element.59), channel_id=1, source_target_pairs={{0,32},{16,48},{32,0},{48,16},{64,96},{80,112},{96,64},{112,80},{1... | collective-permute-start | bytes 786440 | tf_op jit(solution)/shard_map/ppermute | solution.py:36
  62.0 8.1 %collective-permute-start.10 = (f32[128,512]{1,0:T(8,128)S(1)}, f32[128,512]{1,0:T(8,128)S(1)}, u32[]{:S(2)}, u32[]{:S(2)}) collective-permute-start(f32[128,512]{1,0:T(8,128)S(1)} %get-tuple-element.60), channel_id=1, source_target_pairs={{0,48},{16,0},{32,16},{48,32},{64,112},{80,64},{96,80},{112,96},{1... | collective-permute-start | bytes 786440 | tf_op jit(solution)/shard_map/ppermute | solution.py:36
  63.0 7.6 %collective-permute-start.12 = (f32[128,512]{1,0:T(8,128)S(1)}, f32[128,512]{1,0:T(8,128)S(1)}, u32[]{:S(2)}, u32[]{:S(2)}) collective-permute-start(f32[128,512]{1,0:T(8,128)S(1)} %shard_map.101), channel_id=1, source_target_pairs={{0,192},{16,208},{32,224},{48,240},{64,128},{80,144},{96,160},{112... | collective-permute-start | bytes 786440 | tf_op jit(solution)/shard_map/ppermute | solution.py:377
  70.6 7.0 %collective-permute-start.13 = (f32[128,512]{1,0:T(8,128)S(1)}, f32[128,512]{1,0:T(8,128)S(1)}, u32[]{:S(2)}, u32[]{:S(2)}) collective-permute-start(f32[128,512]{1,0:T(8,128)S(1)} %shard_map.102), channel_id=1, source_target_pairs={{0,64},{16,80},{32,96},{48,112},{64,0},{80,16},{96,32},{112,48},{1... | collective-permute-start | bytes 786440 | tf_op jit(solution)/shard_map/ppermute | solution.py:380
  79.5 15.3 %collective-permute-start.14 = (f32[128,512]{1,0:T(8,128)S(1)}, f32[128,512]{1,0:T(8,128)S(1)}, u32[]{:S(2)}, u32[]{:S(2)}) collective-permute-start(f32[128,512]{1,0:T(8,128)S(1)} %get-tuple-element.70), channel_id=1, source_target_pairs={{0,16},{16,32},{32,48},{48,0},{64,80},{80,96},{96,112},{112,64},{1... | collective-permute-start | bytes 786440 | tf_op jit(solution)/shard_map/ppermute | solution.py:36
  80.7 14.1 %collective-permute-start.15 = (f32[128,512]{1,0:T(8,128)S(1)}, f32[128,512]{1,0:T(8,128)S(1)}, u32[]{:S(2)}, u32[]{:S(2)}) collective-permute-start(f32[128,512]{1,0:T(8,128)S(1)} %get-tuple-element.71), channel_id=1, source_target_pairs={{0,32},{16,48},{32,0},{48,16},{64,96},{80,112},{96,64},{112,80},{1... | collective-permute-start | bytes 786440 | tf_op jit(solution)/shard_map/ppermute | solution.py:36
  83.4 11.4 %collective-permute-start.16 = (f32[128,512]{1,0:T(8,128)S(1)}, f32[128,512]{1,0:T(8,128)S(1)}, u32[]{:S(2)}, u32[]{:S(2)}) collective-permute-start(f32[128,512]{1,0:T(8,128)S(1)} %get-tuple-element.72), channel_id=1, source_target_pairs={{0,48},{16,0},{32,16},{48,32},{64,112},{80,64},{96,80},{112,96},{1... | collective-permute-start | bytes 786440 | tf_op jit(solution)/shard_map/ppermute | solution.py:36
  84.6 20.2 %all-to-all-start = ((f32[32,1,512]{2,1,0:T(1,128)}), f32[32,1,512]{2,1,0:T(1,128)S(1)}, u32[]{:S(2)}, u32[]{:S(2)}) async-start(f32[32,1,512]{2,1,0:T(1,128)} %shard_map.108), calls=%async_computation | async-start | bytes 131072 | tf_op jit(solution)/shard_map/all_to_all | solution.py:390
  95.2 1.3 %collective-permute-start.17 = (f32[32,512]{1,0:T(8,128)S(1)}, f32[32,512]{1,0:T(8,128)S(1)}, u32[]{:S(2)}, u32[]{:S(2)}) collective-permute-start(f32[32,512]{1,0:T(8,128)S(1)} %shard_map.106), channel_id=1, source_target_pairs={{0,8},{8,0},{1,9},{9,1},{2,10},{10,2},{3,11},{11,3},{4,12},{12,4},... | collective-permute-start | bytes 196616 | tf_op jit(solution)/shard_map/ppermute | solution.py:393

commit v3 on v2

--- a/solution.py
+++ b/solution.py
@@ -97,7 +97,7 @@
         keep(j, gained, state)
         return state
 
-    return lax.fori_loop(first, ROW, step, incoming)
+    return lax.fori_loop(first, ROW, step, incoming, unroll=True)
 
 
 def backward_chain(apply, thin, cotangent, incoming, keep, through):
@@ -107,7 +107,7 @@
         keep(j, adjoint)
         return apply(adjoint * thin[j], j, NN)
 
-    state = lax.fori_loop(0, ROW - 1, step, incoming)
+    state = lax.fori_loop(0, ROW - 1, step, incoming, unroll=True)
     adjoint = cotangent[0] + state
     keep(0, adjoint)
     if through:

time: 106 us -> 105 us (level)
  transfers between devices with their start and end apart: 19 -> 19, of which waited for: 10 -> 10; matrix products, arithmetic and copies ran while one was open for 1% -> 1% of each run, Pallas kernels for 4% -> 5%
where the time goes in v3:
time: 105 us
  waiting for transfers between devices  53.2 us (51%)
  starting transfers between devices  34.4 us (33%)
  Pallas kernels  9.09 us (9%)
  local copies, waits for them, and re-layouts  5.69 us (5%)
  between operations  1.45 us (1%)
    ppermute x13, waiting for transfers between devices, shift_x(): return lax.ppermute(value, 'sweep', X_RING[by % ROW])  39.3 us
    ppermute x13, starting transfers between devices, shift_x(): return lax.ppermute(value, 'sweep', X_RING[by % ROW])  19.9 us
    all_to_all x1, starting transfers between devices, per_device(): lax.all_to_all(lines, ('sweep', 'band'), 0, 0, axis_index_groups=ROW_BANDS)  10.2 us
    pallas_call x15, Pallas kernels, call(): pl.pallas_call(body, out_shape=[jax.ShapeDtypeStruct(shape, dtype) for sh...  9.09 us
    all_to_all x1, waiting for transfers between devices, per_device(): lax.all_to_all(lines, ('sweep', 'band'), 0, 0, axis_index_groups=ROW_BANDS)  7.14 us
    unnamed x14, local copies, waits for them, and re-layouts  5.69 us
    ppermute x1, waiting for transfers between devices, per_device(): last_in = lax.ppermute(out, 'sweep', Y_SWAP)  4.35 us
    ppermute x1, starting transfers between devices, per_device(): last_in = lax.ppermute(out, 'sweep', Y_SWAP)  2.38 us
  transfers between devices with their start and end apart: 19, of which 10 were waited for; matrix products, arithmetic and copies ran while one was open for 1% of the time, Pallas kernels for 5%

profile of v3, /device:TPU:24, one launch (start us, length us, event | category | flops | bytes accessed | tf_op | source)
XLA Modules:
  0.0 104.8 jit_solution(16925999141462048564)
XLA Ops:
  0.6 2.8 %collective-permute-start.1 = (f32[512,512]{1,0:T(8,128)}, f32[512,512]{1,0:T(8,128)S(1)}, u32[]{:S(2)}, u32[]{:S(2)}) collective-permute-start(f32[512,512]{1,0:T(8,128)} %bitcast.10), channel_id=1, source_target_pairs={{0,48},{16,0},{32,16},{48,32},{64,112},{80,64},{96,80},{112,96},{1... | collective-permute-start | bytes 3145736 | tf_op jit(solution)/shard_map/ppermute | solution.py:36
  3.5 0.9 select_bitcast_fusion
  4.4 0.1 collective-permute-start.2
  5.1 0.6 collective-permute-done.2
  5.7 0.0 copy-start
  5.7 1.2 %copy-done = f32[1,1,512,512]{3,2,1,0:T(8,128)S(1)} copy-done((f32[1,1,512,512]{3,2,1,0:T(8,128)S(1)}, f32[1,1,512,512]{3,2,1,0:T(8,128)}, u32[]{:S(2)}) %copy-start) | copy-done | bytes 1048600
  6.9 1.2 %copy-done.1 = f32[1,1,512,512]{3,2,1,0:T(8,128)S(1)} copy-done((f32[1,1,512,512]{3,2,1,0:T(8,128)S(1)}, f32[1,1,512,512]{3,2,1,0:T(8,128)}, u32[]{:S(2)}) %copy-start.1) | copy-done | bytes 1048600
  8.2 1.2 %copy-done.2 = f32[1,512,512]{2,1,0:T(8,128)S(1)} copy-done((f32[1,512,512]{2,1,0:T(8,128)S(1)}, f32[1,512,512]{2,1,0:T(8,128)}, u32[]{:S(2)}) %copy-start.2) | copy-done | bytes 1048600
  9.4 0.7 copy-done.4
  10.1 0.7 copy-done.5
  10.8 0.7 copy-done.6
  11.4 1.2 %shard_map.95 = (f32[136,512]{1,0:T(8,128)S(1)}, f32[136,512]{1,0:T(8,128)S(1)}, f32[136,512]{1,0:T(8,128)S(1)}, f32[136,512]{1,0:T(8,128)S(1)}, f32[128,512]{1,...) custom-call(f32[1]{0:T(128)S(6)} %copy.10.coeff, ...), custom_call_target="tpu_custom_call" | custom-call | tf_op jit(solution)/shard_map/pallas_call | solution.py:42
  12.7 0.0 copy-start.3
  12.7 0.8 collective-permute-start.3
  13.5 3.9 %collective-permute-start.4 = (f32[136,512]{1,0:T(8,128)S(1)}, f32[136,512]{1,0:T(8,128)S(1)}, u32[]{:S(2)}, u32[]{:S(2)}) collective-permute-start(f32[136,512]{1,0:T(8,128)S(1)} %get-tuple-element.42), channel_id=1, source_target_pairs={{0,32},{16,48},{32,0},{48,16},{64,96},{80,112},{96,64},{112,80},{1... | collective-permute-start | bytes 835592 | tf_op jit(solution)/shard_map/ppermute | solution.py:36
  17.4 0.2 collective-permute-start.5
  17.7 23.8 %collective-permute-done.3.e1 = f32[136,512]{1,0:T(8,128)S(1)} collective-permute-done((f32[136,512]{1,0:T(8,128)S(1)}, f32[136,512]{1,0:T(8,128)S(1)}, u32[]{:S(2)}, u32[]{:S(2)}) %collective-permute-start.3) | collective-permute-done | bytes 278560 | tf_op jit(solution)/shard_map/ppermute | solution.py:36
  41.5 0.1 shard_map.97
  41.5 0.1 collective-permute-start.6
  41.6 3.2 %collective-permute-start.7 = (f32[256,512]{1,0:T(8,128)S(1)}, f32[256,512]{1,0:T(8,128)S(1)}, u32[]{:S(2)}, u32[]{:S(2)}) collective-permute-start(f32[256,512]{1,0:T(8,128)S(1)} %get-tuple-element.47), channel_id=1, source_target_pairs={{0,48},{16,0},{32,16},{48,32},{64,112},{80,64},{96,80},{112,96},{1... | collective-permute-start | bytes 1572872 | tf_op jit(solution)/shard_map/ppermute | solution.py:36
  44.9 0.5 shard_map.96
  45.4 9.0 %collective-permute-done.6.far_top = f32[256,512]{1,0:T(8,128)S(1)} collective-permute-done((f32[256,512]{1,0:T(8,128)S(1)}, f32[256,512]{1,0:T(8,128)S(1)}, u32[]{:S(2)}, u32[]{:S(2)}) %collective-permute-start.6) | collective-permute-done | bytes 524320 | tf_op jit(solution)/shard_map/ppermute | solution.py:36
  54.4 2.1 %shard_map.98 = (bf16[512,512]{1,0:T(8,128)(2,1)S(1)}, bf16[512,512]{1,0:T(8,128)(2,1)S(1)}, f32[4,128,512]{2,1,0:T(8,128)S(1)}, f32[4,128,512]{2,1,0:T(8,128)S(...) custom-call(bf16[4,512,512]{2,1,0:T(8,128)(2,1)S(1)} %get-tuple-element.44.high.near_high, ...), custom_call_target="tpu_custom_call" | custom-call | tf_op jit(solution)/shard_map/pallas_call | solution.py:42
  56.5 1.1 %collective-permute-start.11 = (f32[128,512]{1,0:T(8,128)S(1)}, f32[128,512]{1,0:T(8,128)S(1)}, u32[]{:S(2)}, u32[]{:S(2)}) collective-permute-start(f32[128,512]{1,0:T(8,128)S(1)} %get-tuple-element.62), channel_id=1, source_target_pairs={{0,64},{16,80},{32,96},{48,112},{64,0},{80,16},{96,32},{112,48},{1... | collective-permute-start | bytes 786440 | tf_op jit(solution)/shard_map/ppermute | solution.py:372
  57.6 0.3 collective-permute-start.8
  57.9 4.1 %collective-permute-start.9 = (f32[128,512]{1,0:T(8,128)S(1)}, f32[128,512]{1,0:T(8,128)S(1)}, u32[]{:S(2)}, u32[]{:S(2)}) collective-permute-start(f32[128,512]{1,0:T(8,128)S(1)} %get-tuple-element.59), channel_id=1, source_target_pairs={{0,32},{16,48},{32,0},{48,16},{64,96},{80,112},{96,64},{112,80},{1... | collective-permute-start | bytes 786440 | tf_op jit(solution)/shard_map/ppermute | solution.py:36
  62.0 0.3 shard_map.99
  62.3 0.6 collective-permute-done.11.incoming.first_in
  62.9 0.6 collective-permute-start.12
  63.6 3.7 %collective-permute-done.8.s1 = f32[128,512]{1,0:T(8,128)S(1)} collective-permute-done((f32[128,512]{1,0:T(8,128)S(1)}, f32[128,512]{1,0:T(8,128)S(1)}, u32[]{:S(2)}, u32[]{:S(2)}) %collective-permute-start.8) | collective-permute-done | bytes 262176 | tf_op jit(solution)/shard_map/ppermute | solution.py:36
  67.3 2.8 %collective-permute-done.9.s2 = f32[128,512]{1,0:T(8,128)S(1)} collective-permute-done((f32[128,512]{1,0:T(8,128)S(1)}, f32[128,512]{1,0:T(8,128)S(1)}, u32[]{:S(2)}, u32[]{:S(2)}) %collective-permute-start.9) | collective-permute-done | bytes 262176 | tf_op jit(solution)/shard_map/ppermute | solution.py:36
  70.1 0.1 shard_map.100
  70.2 0.3 collective-permute-done.12.incoming.second_in
  70.5 2.4 %collective-permute-start.13 = (f32[128,512]{1,0:T(8,128)S(1)}, f32[128,512]{1,0:T(8,128)S(1)}, u32[]{:S(2)}, u32[]{:S(2)}) collective-permute-start(f32[128,512]{1,0:T(8,128)S(1)} %shard_map.102), channel_id=1, source_target_pairs={{0,64},{16,80},{32,96},{48,112},{64,0},{80,16},{96,32},{112,48},{1... | collective-permute-start | bytes 786440 | tf_op jit(solution)/shard_map/ppermute | solution.py:380
  72.9 4.3 %collective-permute-done.13.last_in = f32[128,512]{1,0:T(8,128)S(1)} collective-permute-done((f32[128,512]{1,0:T(8,128)S(1)}, f32[128,512]{1,0:T(8,128)S(1)}, u32[]{:S(2)}, u32[]{:S(2)}) %collective-permute-start.13) | collective-permute-done | bytes 262176 | tf_op jit(solution)/shard_map/ppermute | solution.py:380
  77.2 1.6 %shard_map.104 = (f32[4,128,512]{2,1,0:T(8,128)S(1)}, f32[128,512]{1,0:T(8,128)S(1)}, f32[128,512]{1,0:T(8,128)S(1)}, f32[128,512]{1,0:T(8,128)S(1)}, f32[128,512]{1,0:T(8,128)S(1)}) custom-call(bf16[4,512,512]{2,1,0:T(8,128)(2,1)S(1)} %get-tuple-element.55.high, bf16[4,512,512]{2,1,0:T(8,128)(2,1)S(1)} %get-tuple-element.56.low, ...), custom_call_target="tpu_custom_call" | custom-call | tf_op jit(solution)/shard_map/pallas_call | solution.py:42
  78.9 1.3 %collective-permute-start.14 = (f32[128,512]{1,0:T(8,128)S(1)}, f32[128,512]{1,0:T(8,128)S(1)}, u32[]{:S(2)}, u32[]{:S(2)}) collective-permute-start(f32[128,512]{1,0:T(8,128)S(1)} %get-tuple-element.70), channel_id=1, source_target_pairs={{0,16},{16,32},{32,48},{48,0},{64,80},{80,96},{96,112},{112,64},{1... | collective-permute-start | bytes 786440 | tf_op jit(solution)/shard_map/ppermute | solution.py:36
  80.1 2.8 %collective-permute-start.15 = (f32[128,512]{1,0:T(8,128)S(1)}, f32[128,512]{1,0:T(8,128)S(1)}, u32[]{:S(2)}, u32[]{:S(2)}) collective-permute-start(f32[128,512]{1,0:T(8,128)S(1)} %get-tuple-element.71), channel_id=1, source_target_pairs={{0,32},{16,48},{32,0},{48,16},{64,96},{80,112},{96,64},{112,80},{1... | collective-permute-start | bytes 786440 | tf_op jit(solution)/shard_map/ppermute | solution.py:36
  83.0 0.2 collective-permute-start.16
  83.2 0.8 shard_map.108
  83.9 10.2 %all-to-all-start = ((f32[32,1,512]{2,1,0:T(1,128)}), f32[32,1,512]{2,1,0:T(1,128)S(1)}, u32[]{:S(2)}, u32[]{:S(2)}) async-start(f32[32,1,512]{2,1,0:T(1,128)} %shard_map.108), calls=%async_computation | async-start | bytes 131072 | tf_op jit(solution)/shard_map/all_to_all | solution.py:390
  94.2 0.4 shard_map.106
  94.6 0.1 collective-permute-start.17
  94.7 0.3 shard_map.105.grid
  95.0 0.9 collective-permute-done.17.edge
  95.9 1.1 %shard_map.107 = (f32[512,512]{1,0:T(8,128)}, f32[8,128]{1,0:T(8,128)S(1)}) custom-call(f32[512,512]{1,0:T(8,128)S(1)} %shard_map.105.grid, f32[32,512]{1,0:T(8,128)S(1)} %collective-permute-done.17.edge), custom_call_target="tpu_custom_call" | custom-call | tf_op jit(solution)/shard_map/pallas_call | solution.py:42
  97.0 7.1 %all-to-all-done.lines = f32[32,1,512]{2,1,0:T(1,128)S(1)} async-done(((f32[32,1,512]{2,1,0:T(1,128)}), f32[32,1,512]{2,1,0:T(1,128)S(1)}, u32[]{:S(2)}, u32[]{:S(2)}) %all-to-all-start) | async-done | bytes 65568 | tf_op jit(solution)/shard_map/all_to_all | solution.py:390
  104.2 0.6 shard_map.109
  (21 shorter events, 0.1 us)
Async XLA Ops:
  0.6 40.8 %collective-permute-start.1 = (f32[512,512]{1,0:T(8,128)}, f32[512,512]{1,0:T(8,128)S(1)}, u32[]{:S(2)}, u32[]{:S(2)}) collective-permute-start(f32[512,512]{1,0:T(8,128)} %bitcast.10), channel_id=1, source_target_pairs={{0,48},{16,0},{32,16},{48,32},{64,112},{80,64},{96,80},{112,96},{1... | collective-permute-start | bytes 3145736 | tf_op jit(solution)/shard_map/ppermute | solution.py:36
  3.5 38.0 %collective-permute-start = (f32[512,512]{1,0:T(8,128)}, f32[512,512]{1,0:T(8,128)S(1)}, u32[]{:S(2)}, u32[]{:S(2)}) collective-permute-start(f32[512,512]{1,0:T(8,128)} %bitcast.11), channel_id=1, source_target_pairs={{0,16},{16,32},{32,48},{48,0},{64,80},{80,96},{96,112},{112,64},{1... | collective-permute-start | bytes 3145736 | tf_op jit(solution)/shard_map/ppermute | solution.py:36
  4.4 1.3 %collective-permute-start.2 = (f32[32,512]{1,0:T(8,128)S(1)}, f32[32,512]{1,0:T(8,128)S(1)}, u32[]{:S(2)}, u32[]{:S(2)}) collective-permute-start(f32[32,512]{1,0:T(8,128)S(1)} %select_bitcast_fusion), channel_id=1, source_target_pairs={{0,8},{8,0},{1,9},{9,1},{2,10},{10,2},{3,11},{11,3},{4,12},{12,4},... | collective-permute-start | bytes 196616 | tf_op jit(solution)/shard_map/ppermute | solution.py:349
  5.7 1.2 %copy-start = (f32[1,1,512,512]{3,2,1,0:T(8,128)S(1)}, f32[1,1,512,512]{3,2,1,0:T(8,128)}, u32[]{:S(2)}) copy-start(f32[1,1,512,512]{3,2,1,0:T(8,128)} %param.11) | copy-start | bytes 3145732
  6.9 1.2 %copy-start.1 = (f32[1,1,512,512]{3,2,1,0:T(8,128)S(1)}, f32[1,1,512,512]{3,2,1,0:T(8,128)}, u32[]{:S(2)}) copy-start(f32[1,1,512,512]{3,2,1,0:T(8,128)} %param.9) | copy-start | bytes 3145732
  8.2 1.2 %copy-start.2 = (f32[1,512,512]{2,1,0:T(8,128)S(1)}, f32[1,512,512]{2,1,0:T(8,128)}, u32[]{:S(2)}) copy-start(f32[1,512,512]{2,1,0:T(8,128)} %param.10) | copy-start | bytes 3145732
  9.4 0.7 copy-start.4
  10.1 0.7 copy-start.5
  10.8 0.7 copy-start.6
  12.7 32.2 %copy-start.3 = (f32[1,1,512,512]{3,2,1,0:T(8,128)S(1)}, f32[1,1,512,512]{3,2,1,0:T(8,128)}, u32[]{:S(2)}) copy-start(f32[1,1,512,512]{3,2,1,0:T(8,128)} %param.8) | copy-start | bytes 3145732
  12.7 28.8 %collective-permute-start.3 = (f32[136,512]{1,0:T(8,128)S(1)}, f32[136,512]{1,0:T(8,128)S(1)}, u32[]{:S(2)}, u32[]{:S(2)}) collective-permute-start(f32[136,512]{1,0:T(8,128)S(1)} %get-tuple-element.41), channel_id=1, source_target_pairs={{0,16},{16,32},{32,48},{48,0},{64,80},{80,96},{96,112},{112,64},{1... | collective-permute-start | bytes 835592 | tf_op jit(solution)/shard_map/ppermute | solution.py:36
  13.5 27.9 %collective-permute-start.4 = (f32[136,512]{1,0:T(8,128)S(1)}, f32[136,512]{1,0:T(8,128)S(1)}, u32[]{:S(2)}, u32[]{:S(2)}) collective-permute-start(f32[136,512]{1,0:T(8,128)S(1)} %get-tuple-element.42), channel_id=1, source_target_pairs={{0,32},{16,48},{32,0},{48,16},{64,96},{80,112},{96,64},{112,80},{1... | collective-permute-start | bytes 835592 | tf_op jit(solution)/shard_map/ppermute | solution.py:36
  17.4 24.0 %collective-permute-start.5 = (f32[136,512]{1,0:T(8,128)S(1)}, f32[136,512]{1,0:T(8,128)S(1)}, u32[]{:S(2)}, u32[]{:S(2)}) collective-permute-start(f32[136,512]{1,0:T(8,128)S(1)} %get-tuple-element.43), channel_id=1, source_target_pairs={{0,48},{16,0},{32,16},{48,32},{64,112},{80,64},{96,80},{112,96},{1... | collective-permute-start | bytes 835592 | tf_op jit(solution)/shard_map/ppermute | solution.py:36
  41.5 12.9 %collective-permute-start.6 = (f32[256,512]{1,0:T(8,128)S(1)}, f32[256,512]{1,0:T(8,128)S(1)}, u32[]{:S(2)}, u32[]{:S(2)}) collective-permute-start(f32[256,512]{1,0:T(8,128)S(1)} %get-tuple-element.46), channel_id=1, source_target_pairs={{0,16},{16,32},{32,48},{48,0},{64,80},{80,96},{96,112},{112,64},{1... | collective-permute-start | bytes 1572872 | tf_op jit(solution)/shard_map/ppermute | solution.py:36
  41.6 12.8 %collective-permute-start.7 = (f32[256,512]{1,0:T(8,128)S(1)}, f32[256,512]{1,0:T(8,128)S(1)}, u32[]{:S(2)}, u32[]{:S(2)}) collective-permute-start(f32[256,512]{1,0:T(8,128)S(1)} %get-tuple-element.47), channel_id=1, source_target_pairs={{0,48},{16,0},{32,16},{48,32},{64,112},{80,64},{96,80},{112,96},{1... | collective-permute-start | bytes 1572872 | tf_op jit(solution)/shard_map/ppermute | solution.py:36
  56.5 6.5 %collective-permute-start.11 = (f32[128,512]{1,0:T(8,128)S(1)}, f32[128,512]{1,0:T(8,128)S(1)}, u32[]{:S(2)}, u32[]{:S(2)}) collective-permute-start(f32[128,512]{1,0:T(8,128)S(1)} %get-tuple-element.62), channel_id=1, source_target_pairs={{0,64},{16,80},{32,96},{48,112},{64,0},{80,16},{96,32},{112,48},{1... | collective-permute-start | bytes 786440 | tf_op jit(solution)/shard_map/ppermute | solution.py:372
  57.6 9.7 %collective-permute-start.8 = (f32[128,512]{1,0:T(8,128)S(1)}, f32[128,512]{1,0:T(8,128)S(1)}, u32[]{:S(2)}, u32[]{:S(2)}) collective-permute-start(f32[128,512]{1,0:T(8,128)S(1)} %get-tuple-element.58), channel_id=1, source_target_pairs={{0,16},{16,32},{32,48},{48,0},{64,80},{80,96},{96,112},{112,64},{1... | collective-permute-start | bytes 786440 | tf_op jit(solution)/shard_map/ppermute | solution.py:36
  57.9 12.2 %collective-permute-start.9 = (f32[128,512]{1,0:T(8,128)S(1)}, f32[128,512]{1,0:T(8,128)S(1)}, u32[]{:S(2)}, u32[]{:S(2)}) collective-permute-start(f32[128,512]{1,0:T(8,128)S(1)} %get-tuple-element.59), channel_id=1, source_target_pairs={{0,32},{16,48},{32,0},{48,16},{64,96},{80,112},{96,64},{112,80},{1... | collective-permute-start | bytes 786440 | tf_op jit(solution)/shard_map/ppermute | solution.py:36
  62.0 8.1 %collective-permute-start.10 = (f32[128,512]{1,0:T(8,128)S(1)}, f32[128,512]{1,0:T(8,128)S(1)}, u32[]{:S(2)}, u32[]{:S(2)}) collective-permute-start(f32[128,512]{1,0:T(8,128)S(1)} %get-tuple-element.60), channel_id=1, source_target_pairs={{0,48},{16,0},{32,16},{48,32},{64,112},{80,64},{96,80},{112,96},{1... | collective-permute-start | bytes 786440 | tf_op jit(solution)/shard_map/ppermute | solution.py:36
  62.9 7.6 %collective-permute-start.12 = (f32[128,512]{1,0:T(8,128)S(1)}, f32[128,512]{1,0:T(8,128)S(1)}, u32[]{:S(2)}, u32[]{:S(2)}) collective-permute-start(f32[128,512]{1,0:T(8,128)S(1)} %shard_map.101), channel_id=1, source_target_pairs={{0,192},{16,208},{32,224},{48,240},{64,128},{80,144},{96,160},{112... | collective-permute-start | bytes 786440 | tf_op jit(solution)/shard_map/ppermute | solution.py:377
  70.5 6.7 %collective-permute-start.13 = (f32[128,512]{1,0:T(8,128)S(1)}, f32[128,512]{1,0:T(8,128)S(1)}, u32[]{:S(2)}, u32[]{:S(2)}) collective-permute-start(f32[128,512]{1,0:T(8,128)S(1)} %shard_map.102), channel_id=1, source_target_pairs={{0,64},{16,80},{32,96},{48,112},{64,0},{80,16},{96,32},{112,48},{1... | collective-permute-start | bytes 786440 | tf_op jit(solution)/shard_map/ppermute | solution.py:380
  78.9 15.3 %collective-permute-start.14 = (f32[128,512]{1,0:T(8,128)S(1)}, f32[128,512]{1,0:T(8,128)S(1)}, u32[]{:S(2)}, u32[]{:S(2)}) collective-permute-start(f32[128,512]{1,0:T(8,128)S(1)} %get-tuple-element.70), channel_id=1, source_target_pairs={{0,16},{16,32},{32,48},{48,0},{64,80},{80,96},{96,112},{112,64},{1... | collective-permute-start | bytes 786440 | tf_op jit(solution)/shard_map/ppermute | solution.py:36
  80.1 14.0 %collective-permute-start.15 = (f32[128,512]{1,0:T(8,128)S(1)}, f32[128,512]{1,0:T(8,128)S(1)}, u32[]{:S(2)}, u32[]{:S(2)}) collective-permute-start(f32[128,512]{1,0:T(8,128)S(1)} %get-tuple-element.71), channel_id=1, source_target_pairs={{0,32},{16,48},{32,0},{48,16},{64,96},{80,112},{96,64},{112,80},{1... | collective-permute-start | bytes 786440 | tf_op jit(solution)/shard_map/ppermute | solution.py:36
  83.0 11.2 %collective-permute-start.16 = (f32[128,512]{1,0:T(8,128)S(1)}, f32[128,512]{1,0:T(8,128)S(1)}, u32[]{:S(2)}, u32[]{:S(2)}) collective-permute-start(f32[128,512]{1,0:T(8,128)S(1)} %get-tuple-element.72), channel_id=1, source_target_pairs={{0,48},{16,0},{32,16},{48,32},{64,112},{80,64},{96,80},{112,96},{1... | collective-permute-start | bytes 786440 | tf_op jit(solution)/shard_map/ppermute | solution.py:36
  83.9 20.2 %all-to-all-start = ((f32[32,1,512]{2,1,0:T(1,128)}), f32[32,1,512]{2,1,0:T(1,128)S(1)}, u32[]{:S(2)}, u32[]{:S(2)}) async-start(f32[32,1,512]{2,1,0:T(1,128)} %shard_map.108), calls=%async_computation | async-start | bytes 131072 | tf_op jit(solution)/shard_map/all_to_all | solution.py:390
  94.6 1.3 %collective-permute-start.17 = (f32[32,512]{1,0:T(8,128)S(1)}, f32[32,512]{1,0:T(8,128)S(1)}, u32[]{:S(2)}, u32[]{:S(2)}) collective-permute-start(f32[32,512]{1,0:T(8,128)S(1)} %shard_map.106), channel_id=1, source_target_pairs={{0,8},{8,0},{1,9},{9,1},{2,10},{10,2},{3,11},{11,3},{4,12},{12,4},... | collective-permute-start | bytes 196616 | tf_op jit(solution)/shard_map/ppermute | solution.py:393

commit v4 on v3

--- a/solution.py
+++ b/solution.py
@@ -20,7 +20,7 @@
 BF16 = jnp.bfloat16
 NT = (((1,), (1,)), ((), ()))
 NN = (((1,), (0,)), ((), ()))
-PARAMS = pltpu.CompilerParams(vmem_limit_bytes=24 * 1024 * 1024)
+PARAMS = pltpu.CompilerParams(vmem_limit_bytes=18 * 1024 * 1024)
 
 X_RING = {
     d: [(ROW * y + x, ROW * y + (x + d) % ROW) for y in range(ROWS) for x in range(ROW)] for d in range(1, ROW)
@@ -356,13 +356,16 @@
     f0, f1, f2, f3, s0, s1, s2, s3, sky_rays = call(
         spread_body, [first] * ROW + [part] * (ROW + 1),
         extinction, leaf_density, source[0, 0], weights, before, after, sky[0], leaf_class, occupied)
-    e0, e1, e2, e3 = f0, shift_x(f1, 1), shift_x(f2, 2), shift_x(f3, 3)
+    e0 = f0
+    e2 = shift_x(f2, 2)
+    e3 = shift_x(f3, 3)
+    e1 = shift_x(f1, 1)
     half = ((K // 2, K), F32)
     operators = ((ROW, K, K), BF16)
     whole = ((K, K), BF16)
     far_top, far_bottom = call(cut_body, [half, half], left, right, e1, e2, e3)
+    far_bottom = shift_x(far_bottom, -1)
     far_top = shift_x(far_top, 1)
-    far_bottom = shift_x(far_bottom, -1)
     near_high, near_low, thin, given, pair_high, pair_low = call(
         near_body, [operators, operators, line, chunk, whole, whole], local, left, right, e0, e1, e2, e3)
     far_high, far_low, saved, early, whole_high, whole_low, out = call(

time: 105 us -> 105 us (level)
  no operation moved by 1% of the time
where the time goes in v4:
time: 105 us
  waiting for transfers between devices  53.2 us (51%)
  starting transfers between devices  34.4 us (33%)
  Pallas kernels  9.09 us (9%)
  local copies, waits for them, and re-layouts  5.69 us (5%)
  between operations  1.45 us (1%)
    ppermute x13, waiting for transfers between devices, shift_x(): return lax.ppermute(value, 'sweep', X_RING[by % ROW])  39.3 us
    ppermute x13, starting transfers between devices, shift_x(): return lax.ppermute(value, 'sweep', X_RING[by % ROW])  19.9 us
    all_to_all x1, starting transfers between devices, per_device(): lax.all_to_all(lines, ('sweep', 'band'), 0, 0, axis_index_groups=ROW_BANDS)  10.2 us
    pallas_call x15, Pallas kernels, call(): pl.pallas_call(body, out_shape=[jax.ShapeDtypeStruct(shape, dtype) for sh...  9.09 us
    all_to_all x1, waiting for transfers between devices, per_device(): lax.all_to_all(lines, ('sweep', 'band'), 0, 0, axis_index_groups=ROW_BANDS)  7.14 us
    unnamed x14, local copies, waits for them, and re-layouts  5.69 us
    ppermute x1, waiting for transfers between devices, per_device(): last_in = lax.ppermute(out, 'sweep', Y_SWAP)  4.35 us
    ppermute x1, starting transfers between devices, per_device(): last_in = lax.ppermute(out, 'sweep', Y_SWAP)  2.38 us
  transfers between devices with their start and end apart: 19, of which 10 were waited for; matrix products, arithmetic and copies ran while one was open for 1% of the time, Pallas kernels for 5%

profile of v4, /device:TPU:24, one launch (start us, length us, event | category | flops | bytes accessed | tf_op | source)
XLA Modules:
  0.0 104.8 jit_solution(17682802633402132920)
XLA Ops:
  0.6 2.8 %collective-permute-start.1 = (f32[512,512]{1,0:T(8,128)}, f32[512,512]{1,0:T(8,128)S(1)}, u32[]{:S(2)}, u32[]{:S(2)}) collective-permute-start(f32[512,512]{1,0:T(8,128)} %bitcast.10), channel_id=1, source_target_pairs={{0,48},{16,0},{32,16},{48,32},{64,112},{80,64},{96,80},{112,96},{1... | collective-permute-start | bytes 3145736 | tf_op jit(solution)/shard_map/ppermute | solution.py:36
  3.5 0.9 select_bitcast_fusion
  4.4 0.1 collective-permute-start.2
  5.1 0.6 collective-permute-done.2
  5.7 0.0 copy-start
  5.7 1.2 %copy-done = f32[1,1,512,512]{3,2,1,0:T(8,128)S(1)} copy-done((f32[1,1,512,512]{3,2,1,0:T(8,128)S(1)}, f32[1,1,512,512]{3,2,1,0:T(8,128)}, u32[]{:S(2)}) %copy-start) | copy-done | bytes 1048600
  6.9 1.2 %copy-done.1 = f32[1,1,512,512]{3,2,1,0:T(8,128)S(1)} copy-done((f32[1,1,512,512]{3,2,1,0:T(8,128)S(1)}, f32[1,1,512,512]{3,2,1,0:T(8,128)}, u32[]{:S(2)}) %copy-start.1) | copy-done | bytes 1048600
  8.2 1.2 %copy-done.2 = f32[1,512,512]{2,1,0:T(8,128)S(1)} copy-done((f32[1,512,512]{2,1,0:T(8,128)S(1)}, f32[1,512,512]{2,1,0:T(8,128)}, u32[]{:S(2)}) %copy-start.2) | copy-done | bytes 1048600
  9.4 0.7 copy-done.4
  10.1 0.7 copy-done.5
  10.8 0.7 copy-done.6
  11.4 1.2 %shard_map.95 = (f32[136,512]{1,0:T(8,128)S(1)}, f32[136,512]{1,0:T(8,128)S(1)}, f32[136,512]{1,0:T(8,128)S(1)}, f32[136,512]{1,0:T(8,128)S(1)}, f32[128,512]{1,...) custom-call(f32[1]{0:T(128)S(6)} %copy.10.coeff, ...), custom_call_target="tpu_custom_call" | custom-call | tf_op jit(solution)/shard_map/pallas_call | solution.py:42
  12.7 0.0 copy-start.3
  12.7 0.8 collective-permute-start.3
  13.5 3.9 %collective-permute-start.4 = (f32[136,512]{1,0:T(8,128)S(1)}, f32[136,512]{1,0:T(8,128)S(1)}, u32[]{:S(2)}, u32[]{:S(2)}) collective-permute-start(f32[136,512]{1,0:T(8,128)S(1)} %get-tuple-element.42), channel_id=1, source_target_pairs={{0,32},{16,48},{32,0},{48,16},{64,96},{80,112},{96,64},{112,80},{1... | collective-permute-start | bytes 835592 | tf_op jit(solution)/shard_map/ppermute | solution.py:36
  17.4 0.2 collective-permute-start.5
  17.7 23.8 %collective-permute-done.3.e1 = f32[136,512]{1,0:T(8,128)S(1)} collective-permute-done((f32[136,512]{1,0:T(8,128)S(1)}, f32[136,512]{1,0:T(8,128)S(1)}, u32[]{:S(2)}, u32[]{:S(2)}) %collective-permute-start.3) | collective-permute-done | bytes 278560 | tf_op jit(solution)/shard_map/ppermute | solution.py:36
  41.5 0.1 shard_map.97
  41.5 0.1 collective-permute-start.6
  41.6 3.2 %collective-permute-start.7 = (f32[256,512]{1,0:T(8,128)S(1)}, f32[256,512]{1,0:T(8,128)S(1)}, u32[]{:S(2)}, u32[]{:S(2)}) collective-permute-start(f32[256,512]{1,0:T(8,128)S(1)} %get-tuple-element.47), channel_id=1, source_target_pairs={{0,48},{16,0},{32,16},{48,32},{64,112},{80,64},{96,80},{112,96},{1... | collective-permute-start | bytes 1572872 | tf_op jit(solution)/shard_map/ppermute | solution.py:36
  44.9 0.5 shard_map.96
  45.4 9.0 %collective-permute-done.6.far_top = f32[256,512]{1,0:T(8,128)S(1)} collective-permute-done((f32[256,512]{1,0:T(8,128)S(1)}, f32[256,512]{1,0:T(8,128)S(1)}, u32[]{:S(2)}, u32[]{:S(2)}) %collective-permute-start.6) | collective-permute-done | bytes 524320 | tf_op jit(solution)/shard_map/ppermute | solution.py:36
  54.4 2.1 %shard_map.98 = (bf16[512,512]{1,0:T(8,128)(2,1)S(1)}, bf16[512,512]{1,0:T(8,128)(2,1)S(1)}, f32[4,128,512]{2,1,0:T(8,128)S(1)}, f32[4,128,512]{2,1,0:T(8,128)S(...) custom-call(bf16[4,512,512]{2,1,0:T(8,128)(2,1)S(1)} %get-tuple-element.44.high.near_high, ...), custom_call_target="tpu_custom_call" | custom-call | tf_op jit(solution)/shard_map/pallas_call | solution.py:42
  56.5 1.1 %collective-permute-start.11 = (f32[128,512]{1,0:T(8,128)S(1)}, f32[128,512]{1,0:T(8,128)S(1)}, u32[]{:S(2)}, u32[]{:S(2)}) collective-permute-start(f32[128,512]{1,0:T(8,128)S(1)} %get-tuple-element.62), channel_id=1, source_target_pairs={{0,64},{16,80},{32,96},{48,112},{64,0},{80,16},{96,32},{112,48},{1... | collective-permute-start | bytes 786440 | tf_op jit(solution)/shard_map/ppermute | solution.py:375
  57.6 0.3 collective-permute-start.8
  57.9 4.1 %collective-permute-start.9 = (f32[128,512]{1,0:T(8,128)S(1)}, f32[128,512]{1,0:T(8,128)S(1)}, u32[]{:S(2)}, u32[]{:S(2)}) collective-permute-start(f32[128,512]{1,0:T(8,128)S(1)} %get-tuple-element.59), channel_id=1, source_target_pairs={{0,32},{16,48},{32,0},{48,16},{64,96},{80,112},{96,64},{112,80},{1... | collective-permute-start | bytes 786440 | tf_op jit(solution)/shard_map/ppermute | solution.py:36
  62.0 0.3 shard_map.99
  62.3 0.6 collective-permute-done.11.incoming.first_in
  62.9 0.6 collective-permute-start.12
  63.6 3.7 %collective-permute-done.8.s1 = f32[128,512]{1,0:T(8,128)S(1)} collective-permute-done((f32[128,512]{1,0:T(8,128)S(1)}, f32[128,512]{1,0:T(8,128)S(1)}, u32[]{:S(2)}, u32[]{:S(2)}) %collective-permute-start.8) | collective-permute-done | bytes 262176 | tf_op jit(solution)/shard_map/ppermute | solution.py:36
  67.3 2.8 %collective-permute-done.9.s2 = f32[128,512]{1,0:T(8,128)S(1)} collective-permute-done((f32[128,512]{1,0:T(8,128)S(1)}, f32[128,512]{1,0:T(8,128)S(1)}, u32[]{:S(2)}, u32[]{:S(2)}) %collective-permute-start.9) | collective-permute-done | bytes 262176 | tf_op jit(solution)/shard_map/ppermute | solution.py:36
  70.1 0.1 shard_map.100
  70.2 0.3 collective-permute-done.12.incoming.second_in
  70.5 2.4 %collective-permute-start.13 = (f32[128,512]{1,0:T(8,128)S(1)}, f32[128,512]{1,0:T(8,128)S(1)}, u32[]{:S(2)}, u32[]{:S(2)}) collective-permute-start(f32[128,512]{1,0:T(8,128)S(1)} %shard_map.102), channel_id=1, source_target_pairs={{0,64},{16,80},{32,96},{48,112},{64,0},{80,16},{96,32},{112,48},{1... | collective-permute-start | bytes 786440 | tf_op jit(solution)/shard_map/ppermute | solution.py:383
  72.9 4.3 %collective-permute-done.13.last_in = f32[128,512]{1,0:T(8,128)S(1)} collective-permute-done((f32[128,512]{1,0:T(8,128)S(1)}, f32[128,512]{1,0:T(8,128)S(1)}, u32[]{:S(2)}, u32[]{:S(2)}) %collective-permute-start.13) | collective-permute-done | bytes 262176 | tf_op jit(solution)/shard_map/ppermute | solution.py:383
  77.2 1.6 %shard_map.104 = (f32[4,128,512]{2,1,0:T(8,128)S(1)}, f32[128,512]{1,0:T(8,128)S(1)}, f32[128,512]{1,0:T(8,128)S(1)}, f32[128,512]{1,0:T(8,128)S(1)}, f32[128,512]{1,0:T(8,128)S(1)}) custom-call(bf16[4,512,512]{2,1,0:T(8,128)(2,1)S(1)} %get-tuple-element.55.high, bf16[4,512,512]{2,1,0:T(8,128)(2,1)S(1)} %get-tuple-element.56.low, ...), custom_call_target="tpu_custom_call" | custom-call | tf_op jit(solution)/shard_map/pallas_call | solution.py:42
  78.9 1.3 %collective-permute-start.14 = (f32[128,512]{1,0:T(8,128)S(1)}, f32[128,512]{1,0:T(8,128)S(1)}, u32[]{:S(2)}, u32[]{:S(2)}) collective-permute-start(f32[128,512]{1,0:T(8,128)S(1)} %get-tuple-element.70), channel_id=1, source_target_pairs={{0,16},{16,32},{32,48},{48,0},{64,80},{80,96},{96,112},{112,64},{1... | collective-permute-start | bytes 786440 | tf_op jit(solution)/shard_map/ppermute | solution.py:36
  80.1 2.8 %collective-permute-start.15 = (f32[128,512]{1,0:T(8,128)S(1)}, f32[128,512]{1,0:T(8,128)S(1)}, u32[]{:S(2)}, u32[]{:S(2)}) collective-permute-start(f32[128,512]{1,0:T(8,128)S(1)} %get-tuple-element.71), channel_id=1, source_target_pairs={{0,32},{16,48},{32,0},{48,16},{64,96},{80,112},{96,64},{112,80},{1... | collective-permute-start | bytes 786440 | tf_op jit(solution)/shard_map/ppermute | solution.py:36
  83.0 0.2 collective-permute-start.16
  83.2 0.8 shard_map.108
  83.9 10.2 %all-to-all-start = ((f32[32,1,512]{2,1,0:T(1,128)}), f32[32,1,512]{2,1,0:T(1,128)S(1)}, u32[]{:S(2)}, u32[]{:S(2)}) async-start(f32[32,1,512]{2,1,0:T(1,128)} %shard_map.108), calls=%async_computation | async-start | bytes 131072 | tf_op jit(solution)/shard_map/all_to_all | solution.py:393
  94.2 0.4 shard_map.106
  94.6 0.1 collective-permute-start.17
  94.7 0.3 shard_map.105.grid
  95.0 0.9 collective-permute-done.17.edge
  95.9 1.1 %shard_map.107 = (f32[512,512]{1,0:T(8,128)}, f32[8,128]{1,0:T(8,128)S(1)}) custom-call(f32[512,512]{1,0:T(8,128)S(1)} %shard_map.105.grid, f32[32,512]{1,0:T(8,128)S(1)} %collective-permute-done.17.edge), custom_call_target="tpu_custom_call" | custom-call | tf_op jit(solution)/shard_map/pallas_call | solution.py:42
  97.0 7.1 %all-to-all-done.lines = f32[32,1,512]{2,1,0:T(1,128)S(1)} async-done(((f32[32,1,512]{2,1,0:T(1,128)}), f32[32,1,512]{2,1,0:T(1,128)S(1)}, u32[]{:S(2)}, u32[]{:S(2)}) %all-to-all-start) | async-done | bytes 65568 | tf_op jit(solution)/shard_map/all_to_all | solution.py:393
  104.2 0.6 shard_map.109
  (21 shorter events, 0.1 us)
Async XLA Ops:
  0.6 40.8 %collective-permute-start.1 = (f32[512,512]{1,0:T(8,128)}, f32[512,512]{1,0:T(8,128)S(1)}, u32[]{:S(2)}, u32[]{:S(2)}) collective-permute-start(f32[512,512]{1,0:T(8,128)} %bitcast.10), channel_id=1, source_target_pairs={{0,48},{16,0},{32,16},{48,32},{64,112},{80,64},{96,80},{112,96},{1... | collective-permute-start | bytes 3145736 | tf_op jit(solution)/shard_map/ppermute | solution.py:36
  3.5 38.0 %collective-permute-start = (f32[512,512]{1,0:T(8,128)}, f32[512,512]{1,0:T(8,128)S(1)}, u32[]{:S(2)}, u32[]{:S(2)}) collective-permute-start(f32[512,512]{1,0:T(8,128)} %bitcast.11), channel_id=1, source_target_pairs={{0,16},{16,32},{32,48},{48,0},{64,80},{80,96},{96,112},{112,64},{1... | collective-permute-start | bytes 3145736 | tf_op jit(solution)/shard_map/ppermute | solution.py:36
  4.4 1.3 %collective-permute-start.2 = (f32[32,512]{1,0:T(8,128)S(1)}, f32[32,512]{1,0:T(8,128)S(1)}, u32[]{:S(2)}, u32[]{:S(2)}) collective-permute-start(f32[32,512]{1,0:T(8,128)S(1)} %select_bitcast_fusion), channel_id=1, source_target_pairs={{0,8},{8,0},{1,9},{9,1},{2,10},{10,2},{3,11},{11,3},{4,12},{12,4},... | collective-permute-start | bytes 196616 | tf_op jit(solution)/shard_map/ppermute | solution.py:349
  5.7 1.2 %copy-start = (f32[1,1,512,512]{3,2,1,0:T(8,128)S(1)}, f32[1,1,512,512]{3,2,1,0:T(8,128)}, u32[]{:S(2)}) copy-start(f32[1,1,512,512]{3,2,1,0:T(8,128)} %param.11) | copy-start | bytes 3145732
  6.9 1.2 %copy-start.1 = (f32[1,1,512,512]{3,2,1,0:T(8,128)S(1)}, f32[1,1,512,512]{3,2,1,0:T(8,128)}, u32[]{:S(2)}) copy-start(f32[1,1,512,512]{3,2,1,0:T(8,128)} %param.9) | copy-start | bytes 3145732
  8.2 1.2 %copy-start.2 = (f32[1,512,512]{2,1,0:T(8,128)S(1)}, f32[1,512,512]{2,1,0:T(8,128)}, u32[]{:S(2)}) copy-start(f32[1,512,512]{2,1,0:T(8,128)} %param.10) | copy-start | bytes 3145732
  9.4 0.7 copy-start.4
  10.1 0.7 copy-start.5
  10.8 0.7 copy-start.6
  12.7 32.2 %copy-start.3 = (f32[1,1,512,512]{3,2,1,0:T(8,128)S(1)}, f32[1,1,512,512]{3,2,1,0:T(8,128)}, u32[]{:S(2)}) copy-start(f32[1,1,512,512]{3,2,1,0:T(8,128)} %param.8) | copy-start | bytes 3145732
  12.7 28.8 %collective-permute-start.3 = (f32[136,512]{1,0:T(8,128)S(1)}, f32[136,512]{1,0:T(8,128)S(1)}, u32[]{:S(2)}, u32[]{:S(2)}) collective-permute-start(f32[136,512]{1,0:T(8,128)S(1)} %get-tuple-element.41), channel_id=1, source_target_pairs={{0,16},{16,32},{32,48},{48,0},{64,80},{80,96},{96,112},{112,64},{1... | collective-permute-start | bytes 835592 | tf_op jit(solution)/shard_map/ppermute | solution.py:36
  13.5 27.9 %collective-permute-start.4 = (f32[136,512]{1,0:T(8,128)S(1)}, f32[136,512]{1,0:T(8,128)S(1)}, u32[]{:S(2)}, u32[]{:S(2)}) collective-permute-start(f32[136,512]{1,0:T(8,128)S(1)} %get-tuple-element.42), channel_id=1, source_target_pairs={{0,32},{16,48},{32,0},{48,16},{64,96},{80,112},{96,64},{112,80},{1... | collective-permute-start | bytes 835592 | tf_op jit(solution)/shard_map/ppermute | solution.py:36
  17.4 24.0 %collective-permute-start.5 = (f32[136,512]{1,0:T(8,128)S(1)}, f32[136,512]{1,0:T(8,128)S(1)}, u32[]{:S(2)}, u32[]{:S(2)}) collective-permute-start(f32[136,512]{1,0:T(8,128)S(1)} %get-tuple-element.43), channel_id=1, source_target_pairs={{0,48},{16,0},{32,16},{48,32},{64,112},{80,64},{96,80},{112,96},{1... | collective-permute-start | bytes 835592 | tf_op jit(solution)/shard_map/ppermute | solution.py:36
  41.5 12.9 %collective-permute-start.6 = (f32[256,512]{1,0:T(8,128)S(1)}, f32[256,512]{1,0:T(8,128)S(1)}, u32[]{:S(2)}, u32[]{:S(2)}) collective-permute-start(f32[256,512]{1,0:T(8,128)S(1)} %get-tuple-element.46), channel_id=1, source_target_pairs={{0,16},{16,32},{32,48},{48,0},{64,80},{80,96},{96,112},{112,64},{1... | collective-permute-start | bytes 1572872 | tf_op jit(solution)/shard_map/ppermute | solution.py:36
  41.6 12.8 %collective-permute-start.7 = (f32[256,512]{1,0:T(8,128)S(1)}, f32[256,512]{1,0:T(8,128)S(1)}, u32[]{:S(2)}, u32[]{:S(2)}) collective-permute-start(f32[256,512]{1,0:T(8,128)S(1)} %get-tuple-element.47), channel_id=1, source_target_pairs={{0,48},{16,0},{32,16},{48,32},{64,112},{80,64},{96,80},{112,96},{1... | collective-permute-start | bytes 1572872 | tf_op jit(solution)/shard_map/ppermute | solution.py:36
  56.5 6.5 %collective-permute-start.11 = (f32[128,512]{1,0:T(8,128)S(1)}, f32[128,512]{1,0:T(8,128)S(1)}, u32[]{:S(2)}, u32[]{:S(2)}) collective-permute-start(f32[128,512]{1,0:T(8,128)S(1)} %get-tuple-element.62), channel_id=1, source_target_pairs={{0,64},{16,80},{32,96},{48,112},{64,0},{80,16},{96,32},{112,48},{1... | collective-permute-start | bytes 786440 | tf_op jit(solution)/shard_map/ppermute | solution.py:375
  57.6 9.7 %collective-permute-start.8 = (f32[128,512]{1,0:T(8,128)S(1)}, f32[128,512]{1,0:T(8,128)S(1)}, u32[]{:S(2)}, u32[]{:S(2)}) collective-permute-start(f32[128,512]{1,0:T(8,128)S(1)} %get-tuple-element.58), channel_id=1, source_target_pairs={{0,16},{16,32},{32,48},{48,0},{64,80},{80,96},{96,112},{112,64},{1... | collective-permute-start | bytes 786440 | tf_op jit(solution)/shard_map/ppermute | solution.py:36
  57.9 12.2 %collective-permute-start.9 = (f32[128,512]{1,0:T(8,128)S(1)}, f32[128,512]{1,0:T(8,128)S(1)}, u32[]{:S(2)}, u32[]{:S(2)}) collective-permute-start(f32[128,512]{1,0:T(8,128)S(1)} %get-tuple-element.59), channel_id=1, source_target_pairs={{0,32},{16,48},{32,0},{48,16},{64,96},{80,112},{96,64},{112,80},{1... | collective-permute-start | bytes 786440 | tf_op jit(solution)/shard_map/ppermute | solution.py:36
  62.0 8.1 %collective-permute-start.10 = (f32[128,512]{1,0:T(8,128)S(1)}, f32[128,512]{1,0:T(8,128)S(1)}, u32[]{:S(2)}, u32[]{:S(2)}) collective-permute-start(f32[128,512]{1,0:T(8,128)S(1)} %get-tuple-element.60), channel_id=1, source_target_pairs={{0,48},{16,0},{32,16},{48,32},{64,112},{80,64},{96,80},{112,96},{1... | collective-permute-start | bytes 786440 | tf_op jit(solution)/shard_map/ppermute | solution.py:36
  62.9 7.6 %collective-permute-start.12 = (f32[128,512]{1,0:T(8,128)S(1)}, f32[128,512]{1,0:T(8,128)S(1)}, u32[]{:S(2)}, u32[]{:S(2)}) collective-permute-start(f32[128,512]{1,0:T(8,128)S(1)} %shard_map.101), channel_id=1, source_target_pairs={{0,192},{16,208},{32,224},{48,240},{64,128},{80,144},{96,160},{112... | collective-permute-start | bytes 786440 | tf_op jit(solution)/shard_map/ppermute | solution.py:380
  70.5 6.7 %collective-permute-start.13 = (f32[128,512]{1,0:T(8,128)S(1)}, f32[128,512]{1,0:T(8,128)S(1)}, u32[]{:S(2)}, u32[]{:S(2)}) collective-permute-start(f32[128,512]{1,0:T(8,128)S(1)} %shard_map.102), channel_id=1, source_target_pairs={{0,64},{16,80},{32,96},{48,112},{64,0},{80,16},{96,32},{112,48},{1... | collective-permute-start | bytes 786440 | tf_op jit(solution)/shard_map/ppermute | solution.py:383
  78.9 15.3 %collective-permute-start.14 = (f32[128,512]{1,0:T(8,128)S(1)}, f32[128,512]{1,0:T(8,128)S(1)}, u32[]{:S(2)}, u32[]{:S(2)}) collective-permute-start(f32[128,512]{1,0:T(8,128)S(1)} %get-tuple-element.70), channel_id=1, source_target_pairs={{0,16},{16,32},{32,48},{48,0},{64,80},{80,96},{96,112},{112,64},{1... | collective-permute-start | bytes 786440 | tf_op jit(solution)/shard_map/ppermute | solution.py:36
  80.1 14.0 %collective-permute-start.15 = (f32[128,512]{1,0:T(8,128)S(1)}, f32[128,512]{1,0:T(8,128)S(1)}, u32[]{:S(2)}, u32[]{:S(2)}) collective-permute-start(f32[128,512]{1,0:T(8,128)S(1)} %get-tuple-element.71), channel_id=1, source_target_pairs={{0,32},{16,48},{32,0},{48,16},{64,96},{80,112},{96,64},{112,80},{1... | collective-permute-start | bytes 786440 | tf_op jit(solution)/shard_map/ppermute | solution.py:36
  83.0 11.2 %collective-permute-start.16 = (f32[128,512]{1,0:T(8,128)S(1)}, f32[128,512]{1,0:T(8,128)S(1)}, u32[]{:S(2)}, u32[]{:S(2)}) collective-permute-start(f32[128,512]{1,0:T(8,128)S(1)} %get-tuple-element.72), channel_id=1, source_target_pairs={{0,48},{16,0},{32,16},{48,32},{64,112},{80,64},{96,80},{112,96},{1... | collective-permute-start | bytes 786440 | tf_op jit(solution)/shard_map/ppermute | solution.py:36
  83.9 20.2 %all-to-all-start = ((f32[32,1,512]{2,1,0:T(1,128)}), f32[32,1,512]{2,1,0:T(1,128)S(1)}, u32[]{:S(2)}, u32[]{:S(2)}) async-start(f32[32,1,512]{2,1,0:T(1,128)} %shard_map.108), calls=%async_computation | async-start | bytes 131072 | tf_op jit(solution)/shard_map/all_to_all | solution.py:393
  94.6 1.3 %collective-permute-start.17 = (f32[32,512]{1,0:T(8,128)S(1)}, f32[32,512]{1,0:T(8,128)S(1)}, u32[]{:S(2)}, u32[]{:S(2)}) collective-permute-start(f32[32,512]{1,0:T(8,128)S(1)} %shard_map.106), channel_id=1, source_target_pairs={{0,8},{8,0},{1,9},{9,1},{2,10},{10,2},{3,11},{11,3},{4,12},{12,4},... | collective-permute-start | bytes 196616 | tf_op jit(solution)/shard_map/ppermute | solution.py:396

commit v5 on v4

--- a/solution.py
+++ b/solution.py
@@ -90,6 +90,10 @@
     sky_rays[...] = sky[:, pl.ds(pl.multiple_of(x * CH, CH), CH)].T
 
 
+def held_at(high, low):
+    return lambda rows, j, dims: times(rows, high[j], low[j], dims)
+
+
 def forward_chain(apply, thin, emitted, incoming, keep, first=0):
     def step(j, state):
         gained = apply(state, j, NT) * thin[j]
@@ -120,8 +124,10 @@
     far_bottom[...] = right[K // 2:]
 
 
-def near_body(own, left, right, e0, e1, e2, e3, high, low, thin, given, pair_high, pair_low):
-    x, y = place()
+def near_body(own, left, right, e0, e1, e2, e3, sky_rays,
+              high, low, thin, given, part_high, part_low, before_far, after_far):
+    x, y = place()
+    far = (x + 2) % ROW
     for dist, part in enumerate((e0, e1, e2, e3)):
         tile = (x - dist + ROW) % ROW
         given[tile] = part[:CH]
@@ -130,26 +136,95 @@
         tile = (x - dist + ROW) % ROW
         high[tile], low[tile] = split(part[...])
 
-    @pl.when((y == 1) | (y == 2))
-    def _():
-        base = jnp.where(x < 2, 0, 2)
-        rows = (high[base + 1].astype(F32) + low[base + 1].astype(F32)) * thin[base]
-        pair_high[...], pair_low[...] = split(times(rows, high[base], low[base], NN))
-
-
-def start_body(high, low, far_top, far_bottom, thin, given, pair_high, pair_low, sky_rays,
-               far_high, far_low, saved, radiance, whole_high, whole_low, out, far_pair):
+    apply = held_at(high, low)
+    inner = (y == 1) | (y == 2)
+    first = jnp.where(inner, jnp.where(x < 2, 0, 2), jnp.where(y == 0, far + 1, 0))
+    last = jnp.where(inner, first + 1, jnp.where(y == 0, ROW - 1, far - 1))
+
+    @pl.when(first <= last)
+    def _():
+        part_high[...] = high[first]
+        part_low[...] = low[first]
+
+        @pl.loop(first + 1, last + 1)
+        def _(j):
+            rows = (high[j].astype(F32) + low[j].astype(F32)) * thin[j - 1]
+            part_high[...], part_low[...] = split(times(rows, part_high[...], part_low[...], NN))
+
+    def forward(j, state):
+        return apply(state, j, NT) * thin[j] + given[j]
+
+    @pl.when(y == 0)
+    def _():
+        before_far[...] = lax.fori_loop(0, far, forward, sky_rays[...])
+
+        @pl.when(far < ROW - 1)
+        def _():
+            after_far[...] = lax.fori_loop(far + 2, ROW, forward, given[far + 1])
+
+    def backward_from(top):
+        def backward(i, state):
+            j = top - i
+            return apply((given[j] + state) * thin[j], j, NN)
+
+        return backward
+
+    @pl.when(y == ROWS - 1)
+    def _():
+        nothing = jnp.zeros((CH, K), F32)
+        before_far[...] = lax.fori_loop(0, ROW - 1 - far, backward_from(ROW - 1), nothing)
+        after_far[...] = lax.fori_loop(0, far, backward_from(far - 1), nothing)
+
+
+def start_body(far_top, far_bottom, thin, given, part_high, part_low, before_far, after_far, far_high, far_low, out):
     x, y = place()
     far = (x + 2) % ROW
     far_high[:K // 2], far_low[:K // 2] = split(far_top[...])
     far_high[K // 2:], far_low[K // 2:] = split(far_bottom[...])
 
-    def apply(rows, j, dims):
-        return lax.cond(
-            j == far,
-            lambda: times(rows, far_high[...], far_low[...], dims),
-            lambda: times(rows, high[j], low[j], dims),
-        )
+    @pl.when(y == 0)
+    def _():
+        state = times(before_far[...], far_high[...], far_low[...], NT) * thin[far] + given[far]
+        out[...] = state
+
+        @pl.when(far < ROW - 1)
+        def _():
+            out[...] = times(state, part_high[...], part_low[...], NT) * thin[ROW - 1] + after_far[...]
+
+    @pl.when(y == ROWS - 1)
+    def _():
+        state = times((given[far] + before_far[...]) * thin[far], far_high[...], far_low[...], NN)
+        out[...] = state
+
+        @pl.when(far > 0)
+        def _():
+            out[...] = times(state * thin[far - 1], part_high[...], part_low[...], NN) + after_far[...]
+
+
+def ends(high, low, thin, given, y, forward_row, out):
+    @pl.when(y == forward_row)
+    def _():
+        out[...] = forward_chain(held_at(high, low), thin, given, given[0], lambda j, g, s: None, 1)
+
+    @pl.when(y == ROWS - 1 - forward_row)
+    def _():
+        out[...] = backward_chain(held_at(high, low), thin, given, jnp.zeros((CH, K), F32), lambda j, a: None, True)
+
+
+def ends_body(near_high, near_low, far_high, far_low, thin, given, pair_high, pair_low, sky_rays,
+              high, low, whole_high, whole_low, added, saved, radiance):
+    x, y = place()
+    far = (x + 2) % ROW
+    for j in range(ROW):
+        @pl.when(j == far)
+        def _():
+            high[j] = far_high[...]
+            low[j] = far_low[...]
+
+        @pl.when(j != far)
+        def _():
+            high[j] = near_high[j]
+            low[j] = near_low[j]
 
     @pl.when(y == 0)
     def _():
@@ -157,67 +232,33 @@
             saved[j] = gained
             radiance[j] = state
 
-        out[...] = forward_chain(apply, thin, given, sky_rays[...], keep)
+        forward_chain(held_at(high, low), thin, given, sky_rays[...], keep)
 
     @pl.when(y == ROWS - 1)
     def _():
         def keep(j, adjoint):
             saved[j] = adjoint
 
-        out[...] = backward_chain(apply, thin, given, jnp.zeros((CH, K), F32), keep, True)
-
-    inner = (y == 1) | (y == 2)
-
-    @pl.when(inner & (x % 2 == 0))
-    def _():
-        rows = (high[far + 1].astype(F32) + low[far + 1].astype(F32)) * thin[far]
-        far_pair[...] = times(rows, far_high[...], far_low[...], NN)
-
-    @pl.when(inner & (x % 2 == 1))
-    def _():
-        rows = (far_high[...].astype(F32) + far_low[...].astype(F32)) * thin[far - 1]
-        far_pair[...] = times(rows, high[far - 1], low[far - 1], NN)
-
-    @pl.when(inner & (x < 2))
-    def _():
-        whole = times(far_pair[...] * thin[1], pair_high[...], pair_low[...], NN)
-        whole_high[...], whole_low[...] = split(whole)
-
-    @pl.when(inner & (x >= 2))
-    def _():
-        rows = (pair_high[...].astype(F32) + pair_low[...].astype(F32)) * thin[1]
-        first_high, first_low = split(far_pair[...])
-        whole_high[...], whole_low[...] = split(times(rows, first_high, first_low, NN))
-
-
-def held_at(high, low):
-    return lambda rows, j, dims: times(rows, high[j], low[j], dims)
-
-
-def ends(high, low, thin, given, y, forward_row, out):
-    @pl.when(y == forward_row)
-    def _():
-        out[...] = forward_chain(held_at(high, low), thin, given, given[0], lambda j, g, s: None, 1)
-
-    @pl.when(y == ROWS - 1 - forward_row)
-    def _():
-        out[...] = backward_chain(held_at(high, low), thin, given, jnp.zeros((CH, K), F32), lambda j, a: None, True)
-
-
-def ends_body(near_high, near_low, far_high, far_low, thin, given, high, low, added):
-    far = (place()[0] + 2) % ROW
-    for j in range(ROW):
-        @pl.when(j == far)
-        def _():
-            high[j] = far_high[...]
-            low[j] = far_low[...]
-
-        @pl.when(j != far)
-        def _():
-            high[j] = near_high[j]
-            low[j] = near_low[j]
-
-    ends(high, low, thin, given, place()[1], 1, added)
+        backward_chain(held_at(high, low), thin, given, jnp.zeros((CH, K), F32), keep, False)
+
+    @pl.when((y == 1) | (y == 2))
+    def _():
+        base = jnp.where(x < 2, 2, 0)
+        rows = (high[base + 1].astype(F32) + low[base + 1].astype(F32)) * thin[base]
+        far_pair = times(rows, high[base], low[base], NN)
+
+        @pl.when(x < 2)
+        def _():
+            whole = times(far_pair * thin[1], pair_high[...], pair_low[...], NN)
+            whole_high[...], whole_low[...] = split(whole)
+
+        @pl.when(x >= 2)
+        def _():
+            rows = (pair_high[...].astype(F32) + pair_low[...].astype(F32)) * thin[1]
+            first_high, first_low = split(far_pair)
+            whole_high[...], whole_low[...] = split(times(rows, first_high, first_low, NN))
+
+    ends(high, low, thin, given, y, 1, added)
 
 
 def later_body(high, low, thin, s0, s1, s2, s3, given, added):
@@ -366,16 +407,17 @@
     far_top, far_bottom = call(cut_body, [half, half], left, right, e1, e2, e3)
     far_bottom = shift_x(far_bottom, -1)
     far_top = shift_x(far_top, 1)
-    near_high, near_low, thin, given, pair_high, pair_low = call(
-        near_body, [operators, operators, line, chunk, whole, whole], local, left, right, e0, e1, e2, e3)
-    far_high, far_low, saved, early, whole_high, whole_low, out = call(
-        start_body, [whole, whole, chunk, chunk, whole, whole, part],
-        near_high, near_low, far_top, far_bottom, thin, given, pair_high, pair_low, sky_rays,
-        scratch=[pltpu.VMEM((K, K), F32)])
+    near_high, near_low, thin, given, part_high, part_low, before_far, after_far = call(
+        near_body, [operators, operators, line, chunk, whole, whole, part, part],
+        local, left, right, e0, e1, e2, e3, sky_rays)
+    far_high, far_low, out = call(
+        start_body, [whole, whole, part],
+        far_top, far_bottom, thin, given, part_high, part_low, before_far, after_far)
     first_in = lax.ppermute(out, "sweep", Y_SWAP)
     s1, s2, s3 = shift_x(s1, 1), shift_x(s2, 2), shift_x(s3, 3)
-    high, low, added = call(
-        ends_body, [operators, operators, part], near_high, near_low, far_high, far_low, thin, given)
+    high, low, whole_high, whole_low, added, saved, early = call(
+        ends_body, [operators, operators, whole, whole, part, chunk, chunk],
+        near_high, near_low, far_high, far_low, thin, given, part_high, part_low, sky_rays)
     (out,) = call(functools.partial(pass_body, 1), [part], first_in, whole_high, whole_low, thin, added)
     second_in = lax.ppermute(out, "sweep", Y_TURN)
     later, added = call(later_body, [chunk, part], high, low, thin, s0, s1, s2, s3)

time: 105 us -> 105 us (level)
  waiting for transfers between devices: 53.2 us -> 50.5 us
  Pallas kernels: 9.09 us -> 11.3 us
    ppermute x13, waiting for transfers between devices: 39.3 us -> 35.9 us  [shift_x(): return lax.ppermute(value, 'sweep', X_RING[by % ROW])]
    pallas_call x15, Pallas kernels: 9.09 us -> 11.3 us  [call(): pl.pallas_call(body, out_shape=[jax.ShapeDtypeStruct(shape, dtype) for sh...]
    ppermute x1, starting transfers between devices: 2.38 us -> 3.46 us  [per_device(): last_in = lax.ppermute(out, 'sweep', Y_SWAP)]
  transfers between devices with their start and end apart: 19 -> 19, of which waited for: 10 -> 10; matrix products, arithmetic and copies ran while one was open for 1% -> 1% of each run, Pallas kernels for 5% -> 8%
where the time goes in v5:
time: 105 us
  waiting for transfers between devices  50.5 us (48%)
  starting transfers between devices  35 us (33%)
  Pallas kernels  11.3 us (11%)
  local copies, waits for them, and re-layouts  5.69 us (5%)
  between operations  1.46 us (1%)
    ppermute x13, waiting for transfers between devices, shift_x(): return lax.ppermute(value, 'sweep', X_RING[by % ROW])  35.9 us
    ppermute x13, starting transfers between devices, shift_x(): return lax.ppermute(value, 'sweep', X_RING[by % ROW])  20.5 us
    pallas_call x15, Pallas kernels, call(): pl.pallas_call(body, out_shape=[jax.ShapeDtypeStruct(shape, dtype) for sh...  11.3 us
    all_to_all x1, starting transfers between devices, per_device(): lax.all_to_all(lines, ('sweep', 'band'), 0, 0, axis_index_groups=ROW_BANDS)  9.67 us
    all_to_all x1, waiting for transfers between devices, per_device(): lax.all_to_all(lines, ('sweep', 'band'), 0, 0, axis_index_groups=ROW_BANDS)  7.14 us
    unnamed x14, local copies, waits for them, and re-layouts  5.69 us
    ppermute x1, waiting for transfers between devices, per_device(): last_in = lax.ppermute(out, 'sweep', Y_SWAP)  4.35 us
    ppermute x1, starting transfers between devices, per_device(): last_in = lax.ppermute(out, 'sweep', Y_SWAP)  3.46 us
  transfers between devices with their start and end apart: 19, of which 10 were waited for; matrix products, arithmetic and copies ran while one was open for 1% of the time, Pallas kernels for 8%

profile of v5, /device:TPU:24, one launch (start us, length us, event | category | flops | bytes accessed | tf_op | source)
XLA Modules:
  0.0 104.8 jit_solution(1256455018327876250)
XLA Ops:
  0.6 2.8 %collective-permute-start.1 = (f32[512,512]{1,0:T(8,128)}, f32[512,512]{1,0:T(8,128)S(1)}, u32[]{:S(2)}, u32[]{:S(2)}) collective-permute-start(f32[512,512]{1,0:T(8,128)} %bitcast.10), channel_id=1, source_target_pairs={{0,48},{16,0},{32,16},{48,32},{64,112},{80,64},{96,80},{112,96},{1... | collective-permute-start | bytes 3145736 | tf_op jit(solution)/shard_map/ppermute | solution.py:36
  3.5 0.9 select_bitcast_fusion
  4.4 0.1 collective-permute-start.2
  5.1 0.6 collective-permute-done.2
  5.7 0.0 copy-start
  5.7 1.2 %copy-done = f32[1,1,512,512]{3,2,1,0:T(8,128)S(1)} copy-done((f32[1,1,512,512]{3,2,1,0:T(8,128)S(1)}, f32[1,1,512,512]{3,2,1,0:T(8,128)}, u32[]{:S(2)}) %copy-start) | copy-done | bytes 1048600
  6.9 1.2 %copy-done.1 = f32[1,1,512,512]{3,2,1,0:T(8,128)S(1)} copy-done((f32[1,1,512,512]{3,2,1,0:T(8,128)S(1)}, f32[1,1,512,512]{3,2,1,0:T(8,128)}, u32[]{:S(2)}) %copy-start.1) | copy-done | bytes 1048600
  8.2 1.2 %copy-done.2 = f32[1,512,512]{2,1,0:T(8,128)S(1)} copy-done((f32[1,512,512]{2,1,0:T(8,128)S(1)}, f32[1,512,512]{2,1,0:T(8,128)}, u32[]{:S(2)}) %copy-start.2) | copy-done | bytes 1048600
  9.4 0.7 copy-done.4
  10.1 0.7 copy-done.5
  10.8 0.7 copy-done.6
  11.4 1.2 %shard_map.95 = (f32[136,512]{1,0:T(8,128)S(1)}, f32[136,512]{1,0:T(8,128)S(1)}, f32[136,512]{1,0:T(8,128)S(1)}, f32[136,512]{1,0:T(8,128)S(1)}, f32[128,512]{1,...) custom-call(f32[1]{0:T(128)S(6)} %copy.10.coeff, ...), custom_call_target="tpu_custom_call" | custom-call | tf_op jit(solution)/shard_map/pallas_call | solution.py:42
  12.7 0.0 copy-start.3
  12.7 0.8 collective-permute-start.3
  13.5 3.9 %collective-permute-start.4 = (f32[136,512]{1,0:T(8,128)S(1)}, f32[136,512]{1,0:T(8,128)S(1)}, u32[]{:S(2)}, u32[]{:S(2)}) collective-permute-start(f32[136,512]{1,0:T(8,128)S(1)} %get-tuple-element.44), channel_id=1, source_target_pairs={{0,32},{16,48},{32,0},{48,16},{64,96},{80,112},{96,64},{112,80},{1... | collective-permute-start | bytes 835592 | tf_op jit(solution)/shard_map/ppermute | solution.py:36
  17.4 0.2 collective-permute-start.5
  17.7 23.8 %collective-permute-done.3.e1 = f32[136,512]{1,0:T(8,128)S(1)} collective-permute-done((f32[136,512]{1,0:T(8,128)S(1)}, f32[136,512]{1,0:T(8,128)S(1)}, u32[]{:S(2)}, u32[]{:S(2)}) %collective-permute-start.3) | collective-permute-done | bytes 278560 | tf_op jit(solution)/shard_map/ppermute | solution.py:36
  41.5 0.1 shard_map.97
  41.5 0.1 collective-permute-start.6
  41.6 3.2 %collective-permute-start.7 = (f32[256,512]{1,0:T(8,128)S(1)}, f32[256,512]{1,0:T(8,128)S(1)}, u32[]{:S(2)}, u32[]{:S(2)}) collective-permute-start(f32[256,512]{1,0:T(8,128)S(1)} %get-tuple-element.50), channel_id=1, source_target_pairs={{0,48},{16,0},{32,16},{48,32},{64,112},{80,64},{96,80},{112,96},{1... | collective-permute-start | bytes 1572872 | tf_op jit(solution)/shard_map/ppermute | solution.py:36
  44.9 2.8 %shard_map.96 = (bf16[4,512,512]{2,1,0:T(8,128)(2,1)S(1)}, bf16[4,512,512]{2,1,0:T(8,128)(2,1)S(1)}, f32[4,1,512]{2,1,0:T(1,128)S(1)}, f32[4,128,512]{2,1,0:T(8,...) custom-call(f32[512,512]{1,0:T(8,128)S(1)} %bitcast.12, ...), custom_call_target="tpu_custom_call" | custom-call | tf_op jit(solution)/shard_map/pallas_call | solution.py:42
  47.7 6.7 %collective-permute-done.6.far_top = f32[256,512]{1,0:T(8,128)S(1)} collective-permute-done((f32[256,512]{1,0:T(8,128)S(1)}, f32[256,512]{1,0:T(8,128)S(1)}, u32[]{:S(2)}, u32[]{:S(2)}) %collective-permute-start.6) | collective-permute-done | bytes 524320 | tf_op jit(solution)/shard_map/ppermute | solution.py:36
  54.4 1.0 shard_map.98
  55.4 0.1 collective-permute-start.11
  55.5 0.4 collective-permute-start.8
  55.8 4.1 %collective-permute-start.9 = (f32[128,512]{1,0:T(8,128)S(1)}, f32[128,512]{1,0:T(8,128)S(1)}, u32[]{:S(2)}, u32[]{:S(2)}) collective-permute-start(f32[128,512]{1,0:T(8,128)S(1)} %get-tuple-element.63), channel_id=1, source_target_pairs={{0,32},{16,48},{32,0},{48,16},{64,96},{80,112},{96,64},{112,80},{1... | collective-permute-start | bytes 786440 | tf_op jit(solution)/shard_map/ppermute | solution.py:36
  59.9 1.3 %shard_map.99 = (bf16[4,512,512]{2,1,0:T(8,128)(2,1)S(1)}, bf16[4,512,512]{2,1,0:T(8,128)(2,1)S(1)}, bf16[512,512]{1,0:T(8,128)(2,1)S(1)}, bf16[512,512]{1,0:T(8...) custom-call(bf16[4,512,512]{2,1,0:T(8,128)(2,1)S(1)} %get-tuple-element.47.near_high,, ...), custom_call_target="tpu_custom_call" | custom-call | tf_op jit(solution)/shard_map/pallas_call | solution.py:42
  61.3 0.6 collective-permute-done.11.incoming.first_in
  61.8 1.1 %collective-permute-start.12 = (f32[128,512]{1,0:T(8,128)S(1)}, f32[128,512]{1,0:T(8,128)S(1)}, u32[]{:S(2)}, u32[]{:S(2)}) collective-permute-start(f32[128,512]{1,0:T(8,128)S(1)} %shard_map.101), channel_id=1, source_target_pairs={{0,192},{16,208},{32,224},{48,240},{64,128},{80,144},{96,160},{112... | collective-permute-start | bytes 786440 | tf_op jit(solution)/shard_map/ppermute | solution.py:422
  62.9 2.6 %collective-permute-done.8.s1 = f32[128,512]{1,0:T(8,128)S(1)} collective-permute-done((f32[128,512]{1,0:T(8,128)S(1)}, f32[128,512]{1,0:T(8,128)S(1)}, u32[]{:S(2)}, u32[]{:S(2)}) %collective-permute-start.8) | collective-permute-done | bytes 262176 | tf_op jit(solution)/shard_map/ppermute | solution.py:36
  65.5 2.8 %collective-permute-done.9.s2 = f32[128,512]{1,0:T(8,128)S(1)} collective-permute-done((f32[128,512]{1,0:T(8,128)S(1)}, f32[128,512]{1,0:T(8,128)S(1)}, u32[]{:S(2)}, u32[]{:S(2)}) %collective-permute-start.9) | collective-permute-done | bytes 262176 | tf_op jit(solution)/shard_map/ppermute | solution.py:36
  68.3 0.1 shard_map.100
  68.4 1.0 collective-permute-done.12.incoming.second_in
  69.4 3.5 %collective-permute-start.13 = (f32[128,512]{1,0:T(8,128)S(1)}, f32[128,512]{1,0:T(8,128)S(1)}, u32[]{:S(2)}, u32[]{:S(2)}) collective-permute-start(f32[128,512]{1,0:T(8,128)S(1)} %shard_map.102), channel_id=1, source_target_pairs={{0,64},{16,80},{32,96},{48,112},{64,0},{80,16},{96,32},{112,48},{1... | collective-permute-start | bytes 786440 | tf_op jit(solution)/shard_map/ppermute | solution.py:425
  72.9 4.3 %collective-permute-done.13.last_in = f32[128,512]{1,0:T(8,128)S(1)} collective-permute-done((f32[128,512]{1,0:T(8,128)S(1)}, f32[128,512]{1,0:T(8,128)S(1)}, u32[]{:S(2)}, u32[]{:S(2)}) %collective-permute-start.13) | collective-permute-done | bytes 262176 | tf_op jit(solution)/shard_map/ppermute | solution.py:425
  77.2 1.6 %shard_map.104 = (f32[4,128,512]{2,1,0:T(8,128)S(1)}, f32[128,512]{1,0:T(8,128)S(1)}, f32[128,512]{1,0:T(8,128)S(1)}, f32[128,512]{1,0:T(8,128)S(1)}, f32[128,512]{1,0:T(8,128)S(1)}) custom-call(bf16[4,512,512]{2,1,0:T(8,128)(2,1)S(1)} %get-tuple-element.59.high, bf16[4,512,512]{2,1,0:T(8,128)(2,1)S(1)} %get-tuple-element.60.low, ...), custom_call_target="tpu_custom_call" | custom-call | tf_op jit(solution)/shard_map/pallas_call | solution.py:42
  78.8 2.1 %collective-permute-start.14 = (f32[128,512]{1,0:T(8,128)S(1)}, f32[128,512]{1,0:T(8,128)S(1)}, u32[]{:S(2)}, u32[]{:S(2)}) collective-permute-start(f32[128,512]{1,0:T(8,128)S(1)} %get-tuple-element.74), channel_id=1, source_target_pairs={{0,16},{16,32},{32,48},{48,0},{64,80},{80,96},{96,112},{112,64},{1... | collective-permute-start | bytes 786440 | tf_op jit(solution)/shard_map/ppermute | solution.py:36
  81.0 0.9 collective-permute-start.15
  81.9 1.8 %collective-permute-start.16 = (f32[128,512]{1,0:T(8,128)S(1)}, f32[128,512]{1,0:T(8,128)S(1)}, u32[]{:S(2)}, u32[]{:S(2)}) collective-permute-start(f32[128,512]{1,0:T(8,128)S(1)} %get-tuple-element.76), channel_id=1, source_target_pairs={{0,48},{16,0},{32,16},{48,32},{64,112},{80,64},{96,80},{112,96},{1... | collective-permute-start | bytes 786440 | tf_op jit(solution)/shard_map/ppermute | solution.py:36
  83.7 0.8 shard_map.108
  84.5 9.7 %all-to-all-start = ((f32[32,1,512]{2,1,0:T(1,128)}), f32[32,1,512]{2,1,0:T(1,128)S(1)}, u32[]{:S(2)}, u32[]{:S(2)}) async-start(f32[32,1,512]{2,1,0:T(1,128)} %shard_map.108), calls=%async_computation | async-start | bytes 131072 | tf_op jit(solution)/shard_map/all_to_all | solution.py:435
  94.2 0.4 shard_map.106
  94.6 0.1 collective-permute-start.17
  94.7 0.3 shard_map.105.grid
  95.0 0.9 collective-permute-done.17.edge
  95.9 1.1 %shard_map.107 = (f32[512,512]{1,0:T(8,128)}, f32[8,128]{1,0:T(8,128)S(1)}) custom-call(f32[512,512]{1,0:T(8,128)S(1)} %shard_map.105.grid, f32[32,512]{1,0:T(8,128)S(1)} %collective-permute-done.17.edge), custom_call_target="tpu_custom_call" | custom-call | tf_op jit(solution)/shard_map/pallas_call | solution.py:42
  97.0 7.1 %all-to-all-done.lines = f32[32,1,512]{2,1,0:T(1,128)S(1)} async-done(((f32[32,1,512]{2,1,0:T(1,128)}), f32[32,1,512]{2,1,0:T(1,128)S(1)}, u32[]{:S(2)}, u32[]{:S(2)}) %all-to-all-start) | async-done | bytes 65568 | tf_op jit(solution)/shard_map/all_to_all | solution.py:435
  104.2 0.6 shard_map.109
  (21 shorter events, 0.1 us)
Async XLA Ops:
  0.6 40.8 %collective-permute-start.1 = (f32[512,512]{1,0:T(8,128)}, f32[512,512]{1,0:T(8,128)S(1)}, u32[]{:S(2)}, u32[]{:S(2)}) collective-permute-start(f32[512,512]{1,0:T(8,128)} %bitcast.10), channel_id=1, source_target_pairs={{0,48},{16,0},{32,16},{48,32},{64,112},{80,64},{96,80},{112,96},{1... | collective-permute-start | bytes 3145736 | tf_op jit(solution)/shard_map/ppermute | solution.py:36
  3.5 38.0 %collective-permute-start = (f32[512,512]{1,0:T(8,128)}, f32[512,512]{1,0:T(8,128)S(1)}, u32[]{:S(2)}, u32[]{:S(2)}) collective-permute-start(f32[512,512]{1,0:T(8,128)} %bitcast.11), channel_id=1, source_target_pairs={{0,16},{16,32},{32,48},{48,0},{64,80},{80,96},{96,112},{112,64},{1... | collective-permute-start | bytes 3145736 | tf_op jit(solution)/shard_map/ppermute | solution.py:36
  4.4 1.3 %collective-permute-start.2 = (f32[32,512]{1,0:T(8,128)S(1)}, f32[32,512]{1,0:T(8,128)S(1)}, u32[]{:S(2)}, u32[]{:S(2)}) collective-permute-start(f32[32,512]{1,0:T(8,128)S(1)} %select_bitcast_fusion), channel_id=1, source_target_pairs={{0,8},{8,0},{1,9},{9,1},{2,10},{10,2},{3,11},{11,3},{4,12},{12,4},... | collective-permute-start | bytes 196616 | tf_op jit(solution)/shard_map/ppermute | solution.py:390
  5.7 1.2 %copy-start = (f32[1,1,512,512]{3,2,1,0:T(8,128)S(1)}, f32[1,1,512,512]{3,2,1,0:T(8,128)}, u32[]{:S(2)}) copy-start(f32[1,1,512,512]{3,2,1,0:T(8,128)} %param.11) | copy-start | bytes 3145732
  6.9 1.2 %copy-start.1 = (f32[1,1,512,512]{3,2,1,0:T(8,128)S(1)}, f32[1,1,512,512]{3,2,1,0:T(8,128)}, u32[]{:S(2)}) copy-start(f32[1,1,512,512]{3,2,1,0:T(8,128)} %param.9) | copy-start | bytes 3145732
  8.2 1.2 %copy-start.2 = (f32[1,512,512]{2,1,0:T(8,128)S(1)}, f32[1,512,512]{2,1,0:T(8,128)}, u32[]{:S(2)}) copy-start(f32[1,512,512]{2,1,0:T(8,128)} %param.10) | copy-start | bytes 3145732
  9.4 0.7 copy-start.4
  10.1 0.7 copy-start.5
  10.8 0.7 copy-start.6
  12.7 32.2 %copy-start.3 = (f32[1,1,512,512]{3,2,1,0:T(8,128)S(1)}, f32[1,1,512,512]{3,2,1,0:T(8,128)}, u32[]{:S(2)}) copy-start(f32[1,1,512,512]{3,2,1,0:T(8,128)} %param.8) | copy-start | bytes 3145732
  12.7 28.8 %collective-permute-start.3 = (f32[136,512]{1,0:T(8,128)S(1)}, f32[136,512]{1,0:T(8,128)S(1)}, u32[]{:S(2)}, u32[]{:S(2)}) collective-permute-start(f32[136,512]{1,0:T(8,128)S(1)} %get-tuple-element.43), channel_id=1, source_target_pairs={{0,16},{16,32},{32,48},{48,0},{64,80},{80,96},{96,112},{112,64},{1... | collective-permute-start | bytes 835592 | tf_op jit(solution)/shard_map/ppermute | solution.py:36
  13.5 27.9 %collective-permute-start.4 = (f32[136,512]{1,0:T(8,128)S(1)}, f32[136,512]{1,0:T(8,128)S(1)}, u32[]{:S(2)}, u32[]{:S(2)}) collective-permute-start(f32[136,512]{1,0:T(8,128)S(1)} %get-tuple-element.44), channel_id=1, source_target_pairs={{0,32},{16,48},{32,0},{48,16},{64,96},{80,112},{96,64},{112,80},{1... | collective-permute-start | bytes 835592 | tf_op jit(solution)/shard_map/ppermute | solution.py:36
  17.4 24.0 %collective-permute-start.5 = (f32[136,512]{1,0:T(8,128)S(1)}, f32[136,512]{1,0:T(8,128)S(1)}, u32[]{:S(2)}, u32[]{:S(2)}) collective-permute-start(f32[136,512]{1,0:T(8,128)S(1)} %get-tuple-element.45), channel_id=1, source_target_pairs={{0,48},{16,0},{32,16},{48,32},{64,112},{80,64},{96,80},{112,96},{1... | collective-permute-start | bytes 835592 | tf_op jit(solution)/shard_map/ppermute | solution.py:36
  41.5 12.9 %collective-permute-start.6 = (f32[256,512]{1,0:T(8,128)S(1)}, f32[256,512]{1,0:T(8,128)S(1)}, u32[]{:S(2)}, u32[]{:S(2)}) collective-permute-start(f32[256,512]{1,0:T(8,128)S(1)} %get-tuple-element.49), channel_id=1, source_target_pairs={{0,16},{16,32},{32,48},{48,0},{64,80},{80,96},{96,112},{112,64},{1... | collective-permute-start | bytes 1572872 | tf_op jit(solution)/shard_map/ppermute | solution.py:36
  41.6 12.8 %collective-permute-start.7 = (f32[256,512]{1,0:T(8,128)S(1)}, f32[256,512]{1,0:T(8,128)S(1)}, u32[]{:S(2)}, u32[]{:S(2)}) collective-permute-start(f32[256,512]{1,0:T(8,128)S(1)} %get-tuple-element.50), channel_id=1, source_target_pairs={{0,48},{16,0},{32,16},{48,32},{64,112},{80,64},{96,80},{112,96},{1... | collective-permute-start | bytes 1572872 | tf_op jit(solution)/shard_map/ppermute | solution.py:36
  55.4 6.5 %collective-permute-start.11 = (f32[128,512]{1,0:T(8,128)S(1)}, f32[128,512]{1,0:T(8,128)S(1)}, u32[]{:S(2)}, u32[]{:S(2)}) collective-permute-start(f32[128,512]{1,0:T(8,128)S(1)} %get-tuple-element.66), channel_id=1, source_target_pairs={{0,64},{16,80},{32,96},{48,112},{64,0},{80,16},{96,32},{112,48},{1... | collective-permute-start | bytes 786440 | tf_op jit(solution)/shard_map/ppermute | solution.py:416
  55.5 10.0 %collective-permute-start.8 = (f32[128,512]{1,0:T(8,128)S(1)}, f32[128,512]{1,0:T(8,128)S(1)}, u32[]{:S(2)}, u32[]{:S(2)}) collective-permute-start(f32[128,512]{1,0:T(8,128)S(1)} %get-tuple-element.62), channel_id=1, source_target_pairs={{0,16},{16,32},{32,48},{48,0},{64,80},{80,96},{96,112},{112,64},{1... | collective-permute-start | bytes 786440 | tf_op jit(solution)/shard_map/ppermute | solution.py:36
  55.8 12.5 %collective-permute-start.9 = (f32[128,512]{1,0:T(8,128)S(1)}, f32[128,512]{1,0:T(8,128)S(1)}, u32[]{:S(2)}, u32[]{:S(2)}) collective-permute-start(f32[128,512]{1,0:T(8,128)S(1)} %get-tuple-element.63), channel_id=1, source_target_pairs={{0,32},{16,48},{32,0},{48,16},{64,96},{80,112},{96,64},{112,80},{1... | collective-permute-start | bytes 786440 | tf_op jit(solution)/shard_map/ppermute | solution.py:36
  59.9 8.4 %collective-permute-start.10 = (f32[128,512]{1,0:T(8,128)S(1)}, f32[128,512]{1,0:T(8,128)S(1)}, u32[]{:S(2)}, u32[]{:S(2)}) collective-permute-start(f32[128,512]{1,0:T(8,128)S(1)} %get-tuple-element.64), channel_id=1, source_target_pairs={{0,48},{16,0},{32,16},{48,32},{64,112},{80,64},{96,80},{112,96},{1... | collective-permute-start | bytes 786440 | tf_op jit(solution)/shard_map/ppermute | solution.py:36
  61.8 7.6 %collective-permute-start.12 = (f32[128,512]{1,0:T(8,128)S(1)}, f32[128,512]{1,0:T(8,128)S(1)}, u32[]{:S(2)}, u32[]{:S(2)}) collective-permute-start(f32[128,512]{1,0:T(8,128)S(1)} %shard_map.101), channel_id=1, source_target_pairs={{0,192},{16,208},{32,224},{48,240},{64,128},{80,144},{96,160},{112... | collective-permute-start | bytes 786440 | tf_op jit(solution)/shard_map/ppermute | solution.py:422
  69.4 7.8 %collective-permute-start.13 = (f32[128,512]{1,0:T(8,128)S(1)}, f32[128,512]{1,0:T(8,128)S(1)}, u32[]{:S(2)}, u32[]{:S(2)}) collective-permute-start(f32[128,512]{1,0:T(8,128)S(1)} %shard_map.102), channel_id=1, source_target_pairs={{0,64},{16,80},{32,96},{48,112},{64,0},{80,16},{96,32},{112,48},{1... | collective-permute-start | bytes 786440 | tf_op jit(solution)/shard_map/ppermute | solution.py:425
  78.8 15.3 %collective-permute-start.14 = (f32[128,512]{1,0:T(8,128)S(1)}, f32[128,512]{1,0:T(8,128)S(1)}, u32[]{:S(2)}, u32[]{:S(2)}) collective-permute-start(f32[128,512]{1,0:T(8,128)S(1)} %get-tuple-element.74), channel_id=1, source_target_pairs={{0,16},{16,32},{32,48},{48,0},{64,80},{80,96},{96,112},{112,64},{1... | collective-permute-start | bytes 786440 | tf_op jit(solution)/shard_map/ppermute | solution.py:36
  81.0 13.2 %collective-permute-start.15 = (f32[128,512]{1,0:T(8,128)S(1)}, f32[128,512]{1,0:T(8,128)S(1)}, u32[]{:S(2)}, u32[]{:S(2)}) collective-permute-start(f32[128,512]{1,0:T(8,128)S(1)} %get-tuple-element.75), channel_id=1, source_target_pairs={{0,32},{16,48},{32,0},{48,16},{64,96},{80,112},{96,64},{112,80},{1... | collective-permute-start | bytes 786440 | tf_op jit(solution)/shard_map/ppermute | solution.py:36
  81.9 12.3 %collective-permute-start.16 = (f32[128,512]{1,0:T(8,128)S(1)}, f32[128,512]{1,0:T(8,128)S(1)}, u32[]{:S(2)}, u32[]{:S(2)}) collective-permute-start(f32[128,512]{1,0:T(8,128)S(1)} %get-tuple-element.76), channel_id=1, source_target_pairs={{0,48},{16,0},{32,16},{48,32},{64,112},{80,64},{96,80},{112,96},{1... | collective-permute-start | bytes 786440 | tf_op jit(solution)/shard_map/ppermute | solution.py:36
  84.5 19.7 %all-to-all-start = ((f32[32,1,512]{2,1,0:T(1,128)}), f32[32,1,512]{2,1,0:T(1,128)S(1)}, u32[]{:S(2)}, u32[]{:S(2)}) async-start(f32[32,1,512]{2,1,0:T(1,128)} %shard_map.108), calls=%async_computation | async-start | bytes 131072 | tf_op jit(solution)/shard_map/all_to_all | solution.py:435
  94.6 1.3 %collective-permute-start.17 = (f32[32,512]{1,0:T(8,128)S(1)}, f32[32,512]{1,0:T(8,128)S(1)}, u32[]{:S(2)}, u32[]{:S(2)}) collective-permute-start(f32[32,512]{1,0:T(8,128)S(1)} %shard_map.106), channel_id=1, source_target_pairs={{0,8},{8,0},{1,9},{9,1},{2,10},{10,2},{3,11},{11,3},{4,12},{12,4},... | collective-permute-start | bytes 196616 | tf_op jit(solution)/shard_map/ppermute | solution.py:438
